TPU v7x, 32 devices: a whole 2x2x4 slice. The times are simulated.
32 devices in a mesh: az: 8 (over z, y), rad: 4 (over x, core).
Axes of the slice: x: 2, y: 2, z: 4, core: 2. Of those that a mesh axis runs over, the one named last changes fastest.
Arguments:
- material_id: int32 [8, 2048], P('rad', 'az'), may hold values from 0 to 7
- thickness: float32 [8, 2048], P('rad', 'az'), may hold values from 0.7 to 1.4
- sigma_table: float32 [8], replicated, may hold values from 0.01 to 0.03
- nu_table: float32 [8], replicated, may hold values from 0.5 to 2
- angular_frequency: float32 [1], replicated, may hold values from 0.5 to 2
Outputs:
- merged_map: float32 [2, 1040, 4160], P(None, 'rad', 'az')
All inputs are finite; a program needn't handle non-finite values.
Results may differ from a plain program's by a relative error of at most 0.0003.
Values sent between devices are 32-bit elements; how exact they have to be, the bound alone decides.
No kernel may reach another device: no remote copies, remote signals or barrier semaphores. Data moves between devices by JAX's collectives and lax.ppermute only.
A program may use at most 128 MiB of HBM per device.

v0:
```python
import jax
import jax.numpy as jnp
import numpy as np
from jax import lax
from jax.sharding import PartitionSpec as P

SHEET_NODES = 16


def padded(cells, sides, width, closed):
    for axis, dim in sides:
        count = lax.axis_size(axis)
        ends = count if closed else count - 1
        head = lax.slice_in_dim(cells, 0, width, axis=dim)
        tail = lax.slice_in_dim(cells, cells.shape[dim] - width, cells.shape[dim], axis=dim)
        cells = jnp.concatenate(
            [
                lax.ppermute(tail, axis, [(i, (i + 1) % count) for i in range(ends)]),
                cells,
                lax.ppermute(head, axis, [((i + 1) % count, i) for i in range(ends)]),
            ],
            axis=dim,
        )
    return cells


def swapped(block, axis, apart):
    count = lax.axis_size(axis)
    route = []
    for low in range(count):
        high = low | 1 << apart
        if high != low and high < count:
            route += [(low, high), (high, low)]
    return lax.ppermute(block, axis, route)


def matmul(left_factor, right_factor):
    return jnp.dot(left_factor, right_factor, precision=lax.Precision.HIGHEST)


def complex_times(left_value, right_value):
    return jnp.stack(
        [
            left_value[0] * right_value[0] - left_value[1] * right_value[1],
            left_value[0] * right_value[1] + left_value[1] * right_value[0],
        ]
    )


def complex_divide(numerator, denominator):
    magnitude = denominator[0] * denominator[0] + denominator[1] * denominator[1]
    return jnp.stack(
        [
            (numerator[0] * denominator[0] + numerator[1] * denominator[1]) / magnitude,
            (numerator[1] * denominator[0] - numerator[0] * denominator[1]) / magnitude,
        ]
    )


def harmonic(left_value, right_value):
    return complex_divide(2.0 * complex_times(left_value, right_value), left_value + right_value)


def cell_inputs(material_id, thickness, sigma_table, nu_table, angular_frequency):
    levels = jnp.arange(sigma_table.shape[0], dtype=jnp.int32)
    onehot = (material_id[None] == levels[:, None, None]).astype(jnp.float32)
    sigma_cell = jnp.sum(onehot * sigma_table[:, None, None], axis=0)
    base_value = jnp.sum(onehot * nu_table[:, None, None], axis=0)
    angular = angular_frequency[0]
    skin_ratio = angular * sigma_cell * thickness * thickness
    return (skin_ratio, base_value)


def lamination(skin_ratio, base_value):
    zero_field = jnp.zeros_like(skin_ratio)
    unit_value = jnp.stack([zero_field + 1.0, zero_field])
    factors = []
    carries = []
    for sheet_node in range(SHEET_NODES):
        if sheet_node < SHEET_NODES - 1:
            pivot_value = jnp.stack([zero_field + 2.0, skin_ratio])
        else:
            pivot_value = jnp.stack([zero_field + 1.0, 0.5 * skin_ratio])
        if sheet_node == 0:
            source = unit_value
        else:
            pivot_value = pivot_value + factors[-1]
            source = carries[-1]
        inverse = complex_divide(unit_value, pivot_value)
        factors.append(-inverse)
        carries.append(complex_times(source, inverse))
    sheet_field = carries[-1]
    total_field = sheet_field
    for sheet_node in range(SHEET_NODES - 2, -1, -1):
        sheet_field = carries[sheet_node] - complex_times(factors[sheet_node], sheet_field)
        total_field = total_field + sheet_field
    average = total_field / SHEET_NODES
    return complex_divide(jnp.stack([base_value, zero_field]), average)


def tile_faces(own_cells, left_rim, right_rim, below_rim, above_rim, center_radius, face_radius):
    depth_count = own_cells.shape[1]
    arc_inner = harmonic(own_cells[:, :, :-1], own_cells[:, :, 1:]) / center_radius[:, None]
    left_edge = harmonic(left_rim, own_cells[:, :, 0]) / center_radius
    right_edge = harmonic(own_cells[:, :, -1], right_rim) / center_radius
    west_faces = jnp.concatenate([2.0 * left_edge[:, :, None], arc_inner], axis=2)
    east_faces = jnp.concatenate([arc_inner, 2.0 * right_edge[:, :, None]], axis=2)
    column = jnp.concatenate([below_rim[:, None, :], own_cells, above_rim[:, None, :]], axis=1)
    radial = harmonic(column[:, :-1], column[:, 1:]) * face_radius[:, None]
    south_faces = jnp.concatenate([2.0 * radial[:, :1], radial[:, 1:depth_count]], axis=1)
    north_faces = jnp.concatenate([radial[:, 1:depth_count], 2.0 * radial[:, depth_count:]], axis=1)
    return (west_faces, east_faces, south_faces, north_faces)


def complex_inverse(matrix):
    lower_factor = jnp.linalg.cholesky(matrix[0])
    coupling = jax.scipy.linalg.cho_solve((lower_factor, True), matrix[1])
    coupled = matrix[0] + matmul(matrix[1], coupling)
    second_factor = jnp.linalg.cholesky(coupled)
    identity = jnp.eye(matrix.shape[1], dtype=matrix.dtype)
    inverse_re = jax.scipy.linalg.cho_solve((second_factor, True), identity)
    inverse_im = -matmul(coupling, inverse_re)
    return jnp.stack([inverse_re, inverse_im])


def complex_solve(matrix, right_side):
    lower_factor = jnp.linalg.cholesky(matrix[0])
    coupling = jax.scipy.linalg.cho_solve((lower_factor, True), matrix[1])
    shifted = jax.scipy.linalg.cho_solve((lower_factor, True), right_side[1])
    coupled = matrix[0] + matmul(matrix[1], coupling)
    second_factor = jnp.linalg.cholesky(coupled)
    solved_re = jax.scipy.linalg.cho_solve(
        (second_factor, True), right_side[0] + matmul(matrix[1], shifted)
    )
    solved_im = shifted - matmul(coupling, solved_re)
    return jnp.stack([solved_re, solved_im])


def boundary_cells(depth_count, arc_count):
    return np.concatenate(
        [
            np.arange(arc_count),
            (depth_count - 1) * arc_count + np.arange(arc_count),
            np.arange(depth_count) * arc_count,
            np.arange(depth_count) * arc_count + arc_count - 1,
        ]
    ).astype(np.int32)


def node_orders(depth_count, arc_count):
    sides = 2 * arc_count + np.arange(2 * depth_count)
    order_alpha = np.concatenate(
        [np.arange(arc_count), sides, arc_count + np.arange(arc_count)]
    ).astype(np.int32)
    order_beta = np.concatenate(
        [arc_count + np.arange(arc_count), sides, np.arange(arc_count)]
    ).astype(np.int32)
    return (order_alpha, order_beta)


def permute(local_map, node_order):
    return jnp.take(jnp.take(local_map, node_order, axis=1), node_order, axis=2)


def tile_map(west_faces, east_faces, south_faces, north_faces):
    depth_count = west_faces.shape[1]
    arc_count = west_faces.shape[2]
    cell_count = depth_count * arc_count
    diagonal = (west_faces + east_faces + south_faces + north_faces).reshape(2, cell_count)
    along_arc = jnp.concatenate(
        [east_faces[:, :, :-1], jnp.zeros_like(east_faces[:, :, :1])], axis=2
    )
    along_arc = along_arc.reshape(2, cell_count)[:, :-1]
    along_radius = north_faces[:, :-1, :].reshape(2, cell_count - arc_count)
    matrices = []
    for component in range(2):
        matrices.append(
            jnp.diag(diagonal[component])
            - jnp.diag(along_arc[component], 1)
            - jnp.diag(along_arc[component], -1)
            - jnp.diag(along_radius[component], arc_count)
            - jnp.diag(along_radius[component], -arc_count)
        )
    inverse = complex_inverse(jnp.stack(matrices))
    cell_index = boundary_cells(depth_count, arc_count)
    picked = inverse[:, cell_index][:, :, cell_index]
    edge_gains = jnp.concatenate(
        [south_faces[:, 0, :], north_faces[:, -1, :], west_faces[:, :, 0], east_faces[:, :, -1]],
        axis=1,
    )
    scaled = complex_times(complex_times(edge_gains[:, :, None], picked), edge_gains[:, None, :])
    return jnp.stack([jnp.diag(edge_gains[0]), jnp.diag(edge_gains[1])]) - scaled


def merge_half(own_perm, partner_se, partner_ss, is_alpha):
    arc_count = partner_ss.shape[1]
    outer_count = own_perm.shape[1] - arc_count
    own_ee = own_perm[:, :outer_count, :outer_count]
    own_es = own_perm[:, :outer_count, outer_count:]
    own_se = own_perm[:, outer_count:, :outer_count]
    own_ss = own_perm[:, outer_count:, outer_count:]
    total_ss = own_ss + partner_ss
    first_block = jnp.where(is_alpha, own_se, partner_se)
    second_block = jnp.where(is_alpha, partner_se, own_se)
    right_side = jnp.concatenate([first_block, second_block], axis=2)
    solved = complex_solve(total_ss, right_side)
    product_re = matmul(own_es[0], solved[0]) - matmul(own_es[1], solved[1])
    product_im = matmul(own_es[0], solved[1]) + matmul(own_es[1], solved[0])
    empty_block = jnp.zeros_like(own_ee)
    placed = jnp.where(
        is_alpha,
        jnp.concatenate([own_ee, empty_block], axis=2),
        jnp.concatenate([empty_block, own_ee], axis=2),
    )
    return placed - jnp.stack([product_re, product_im])


def per_device(material_id, thickness, sigma_table, nu_table, angular_frequency):
    depth_count, arc_count = thickness.shape
    skin_ratio, base_value = cell_inputs(
        material_id, thickness, sigma_table, nu_table, angular_frequency
    )
    cycle_index = lax.axis_index("rad")
    cycle_count = lax.axis_size("rad")
    own_cells = lamination(skin_ratio, base_value)
    side_rims = padded(own_cells, (("az", 2),), 1, True)
    end_rims = padded(own_cells, (("rad", 1),), 1, False)
    rim_cells = jnp.concatenate(
        [side_rims[:, :, 0], side_rims[:, :, -1], end_rims[:, 0, :], end_rims[:, -1, :]], axis=1
    )
    left_rim = rim_cells[:, :depth_count]
    right_rim = rim_cells[:, depth_count : 2 * depth_count]
    below_rim = rim_cells[:, 2 * depth_count : 2 * depth_count + arc_count]
    above_rim = rim_cells[:, 2 * depth_count + arc_count :]
    below_rim = jnp.where(cycle_index == 0, own_cells[:, 0, :], below_rim)
    above_rim = jnp.where(cycle_index == cycle_count - 1, own_cells[:, -1, :], above_rim)
    radial_count = depth_count * cycle_count
    positions = (cycle_index * depth_count).astype(jnp.float32) + jnp.arange(
        depth_count + 1, dtype=jnp.float32
    )
    face_radius = 1.0 + positions / radial_count
    center_radius = 1.0 + (positions[:depth_count] + 0.5) / radial_count
    face_set = tile_faces(
        own_cells, left_rim, right_rim, below_rim, above_rim, center_radius, face_radius
    )
    local_map = tile_map(face_set[0], face_set[1], face_set[2], face_set[3])
    order_alpha, order_beta = node_orders(depth_count, arc_count)
    is_alpha = cycle_index % 2 == 0
    own_perm = permute(local_map, jnp.where(is_alpha, order_alpha, order_beta))
    outer_count = own_perm.shape[1] - arc_count
    partner_local = swapped(local_map, "rad", 0)
    partner_perm = permute(partner_local, jnp.where(is_alpha, order_beta, order_alpha))
    partner_rows = partner_perm[:, outer_count:, :]
    return merge_half(
        own_perm, partner_rows[:, :, :outer_count], partner_rows[:, :, outer_count:], is_alpha
    )


def solution(mesh):
    placed = (P("rad", "az"), P("rad", "az"), P(), P(), P())
    return jax.shard_map(
        per_device, mesh=mesh, in_specs=placed, out_specs=P(None, "rad", "az"), check_vma=False
    )
```

profile of v0, /device:TPU:0, one launch (start us, length us, event | category | flops | bytes accessed | tf_op | source)
XLA Modules:
  0.0 608.0 jit_solution(9144274520434391460)
XLA Ops:
  22.3 11.7 %cholesky.373 = f32[128,128]{1,0:T(8,128)S(1)} custom-call(f32[128,128]{1,0:T(8,128)S(1)} %cholesky.559), custom_call_target="Cholesky" | custom-call | tf_op jit(solution)/shard_map/jit(cholesky)/cholesky | solution.py:116
  34.1 9.8 %custom-call.52 = f32[1,128,128]{1,2,0:T(8,128)S(1)} custom-call(f32[1,128,128]{2,1,0:T(8,128)S(1)} %get-tuple-element.181), custom_call_target="InvertDiagBlocksLowerTriangular" | custom-call | tf_op jit(solution)/shard_map/jit(cholesky)/cholesky | solution.py:116
  44.6 12.1 %cholesky.392 = f32[128,128]{1,0:T(8,128)S(1)} custom-call(f32[128,128]{1,0:T(8,128)S(1)} %cholesky.563), custom_call_target="Cholesky" | custom-call | tf_op jit(solution)/shard_map/jit(cholesky)/cholesky | solution.py:116
  67.8 11.7 %cholesky.413 = f32[128,128]{1,0:T(8,128)S(1)} custom-call(f32[128,128]{1,0:T(8,128)S(1)} %cholesky.568), custom_call_target="Cholesky" | custom-call | tf_op jit(solution)/shard_map/jit(cholesky)/cholesky | solution.py:116
  79.5 9.8 %custom-call.54 = f32[1,128,128]{1,2,0:T(8,128)S(1)} custom-call(f32[1,128,128]{2,1,0:T(8,128)S(1)} %get-tuple-element.175), custom_call_target="InvertDiagBlocksLowerTriangular" | custom-call | tf_op jit(solution)/shard_map/jit(cholesky)/cholesky/custom-call.14 | solution.py:116
  90.0 11.9 %cholesky.426 = f32[128,128]{1,0:T(8,128)S(1)} custom-call(f32[128,128]{1,0:T(8,128)S(1)} %convolution_subtract_fusion.27), custom_call_target="Cholesky" | custom-call | tf_op jit(solution)/shard_map/jit(cholesky)/cholesky | solution.py:116
  116.6 39.3 %custom-call.55 = f32[4,128,128]{1,2,0:T(8,128)S(1)} custom-call(f32[4,128,128]{2,1,0:T(8,128)S(1)} %get-tuple-element.48), custom_call_target="InvertDiagBlocksLowerTriangular" | custom-call | tf_op jit(solution)/shard_map/jit(_cho_solve)/triangular_solve | solution.py:117
  167.4 12.1 %cholesky.441 = f32[128,128]{1,0:T(8,128)S(1)} custom-call(f32[128,128]{1,0:T(8,128)S(1)} %cholesky.572), custom_call_target="Cholesky" | custom-call | tf_op jit(solution)/shard_map/jit(cholesky)/cholesky | solution.py:119
  179.6 9.8 %custom-call.56 = f32[1,128,128]{1,2,0:T(8,128)S(1)} custom-call(f32[1,128,128]{2,1,0:T(8,128)S(1)} %get-tuple-element.171), custom_call_target="InvertDiagBlocksLowerTriangular" | custom-call | tf_op jit(solution)/shard_map/jit(cholesky)/cholesky | solution.py:119
  190.1 11.7 %cholesky.460 = f32[128,128]{1,0:T(8,128)S(1)} custom-call(f32[128,128]{1,0:T(8,128)S(1)} %cholesky.576), custom_call_target="Cholesky" | custom-call | tf_op jit(solution)/shard_map/jit(cholesky)/cholesky | solution.py:119
  213.3 11.9 %cholesky.481 = f32[128,128]{1,0:T(8,128)S(1)} custom-call(f32[128,128]{1,0:T(8,128)S(1)} %cholesky.581), custom_call_target="Cholesky" | custom-call | tf_op jit(solution)/shard_map/jit(cholesky)/cholesky | solution.py:119
  225.2 9.8 %custom-call.58 = f32[1,128,128]{1,2,0:T(8,128)S(1)} custom-call(f32[1,128,128]{2,1,0:T(8,128)S(1)} %get-tuple-element.165), custom_call_target="InvertDiagBlocksLowerTriangular" | custom-call | tf_op jit(solution)/shard_map/jit(cholesky)/cholesky/custom-call.14 | solution.py:119
  236.4 11.7 %cholesky.494 = f32[128,128]{1,0:T(8,128)S(1)} custom-call(f32[128,128]{1,0:T(8,128)S(1)} %convolution_subtract_fusion.26), custom_call_target="Cholesky" | custom-call | tf_op jit(solution)/shard_map/jit(cholesky)/cholesky | solution.py:119
  261.9 39.5 %custom-call.59 = f32[4,128,128]{1,2,0:T(8,128)S(1)} custom-call(f32[4,128,128]{2,1,0:T(8,128)S(1)} %get-tuple-element.49), custom_call_target="InvertDiagBlocksLowerTriangular" | custom-call | tf_op jit(solution)/shard_map/jit(_cho_solve)/triangular_solve | solution.py:121
  392.4 10.5 %gather_fusion.4 = f32[516,2,516]{2,1,0:T(2,128)} fusion(f32[2,516,516]{2,0,1:T(2,128)} %copy.389, s32[1024]{0:T(1024)S(1)} %pad_clamp_fusion), kind=kCustom, calls=%fused_computation.2.clone | custom fusion | bytes 4262160 | tf_op jit(solution)/shard_map/jit(_take)/gather | solution.py:162
  415.6 10.7 %gather_fusion.5 = f32[516,2,516]{2,1,0:T(2,128)} fusion(f32[2,516,516]{1,0,2:T(2,128)} %copy.390, s32[1024]{0:T(1024)S(1)} %pad_clamp_fusion), kind=kCustom, calls=%fused_computation.3.clone | custom fusion | bytes 4262160 | tf_op jit(solution)/shard_map/jit(_take)/gather | solution.py:162
  432.6 11.7 %cholesky.509 = f32[128,128]{1,0:T(8,128)S(1)} custom-call(f32[128,128]{1,0:T(8,128)S(1)} %cholesky.585), custom_call_target="Cholesky" | custom-call | tf_op jit(solution)/shard_map/jit(cholesky)/cholesky | solution.py:127
  445.0 10.6 %custom-call.60 = f32[1,128,128]{1,2,0:T(8,128)S(1)} custom-call(f32[1,128,128]{2,1,0:T(8,128)} %get-tuple-element.161), custom_call_target="InvertDiagBlocksLowerTriangular" | custom-call | tf_op jit(solution)/shard_map/jit(cholesky)/cholesky/custom-call.14 | solution.py:127
  458.4 12.5 %cholesky.519 = f32[128,128]{1,0:T(8,128)S(1)} custom-call(f32[128,128]{1,0:T(8,128)} %convolution_subtract_fusion.25), custom_call_target="Cholesky" | custom-call | tf_op jit(solution)/shard_map/jit(cholesky)/cholesky | solution.py:127
  480.6 21.6 %custom-call.40 = f32[2,128,128]{1,2,0:T(8,128)} custom-call(f32[2,128,128]{2,1,0:T(8,128)} %get-tuple-element.35), custom_call_target="InvertDiagBlocksLowerTriangular" | custom-call | tf_op jit(solution)/shard_map/jit(_cho_solve)/triangular_solve | solution.py:128
  517.0 11.7 %cholesky.536 = f32[128,128]{1,0:T(8,128)S(1)} custom-call(f32[128,128]{1,0:T(8,128)S(1)} %cholesky.588), custom_call_target="Cholesky" | custom-call | tf_op jit(solution)/shard_map/jit(cholesky)/cholesky | solution.py:131
  529.4 10.8 %custom-call.61 = f32[1,128,128]{1,2,0:T(8,128)S(1)} custom-call(f32[1,128,128]{2,1,0:T(8,128)} %get-tuple-element.157), custom_call_target="InvertDiagBlocksLowerTriangular" | custom-call | tf_op jit(solution)/shard_map/jit(cholesky)/cholesky/custom-call.14 | solution.py:131
  540.6 11.7 %cholesky.546 = f32[128,128]{1,0:T(8,128)S(1)} custom-call(f32[128,128]{1,0:T(8,128)S(1)} %convolution_subtract_fusion.24), custom_call_target="Cholesky" | custom-call | tf_op jit(solution)/shard_map/jit(cholesky)/cholesky | solution.py:131
  559.0 20.3 %custom-call.63 = f32[2,128,128]{1,2,0:T(8,128)} custom-call(f32[2,128,128]{2,1,0:T(8,128)S(1)} %get-tuple-element.51), custom_call_target="InvertDiagBlocksLowerTriangular" | custom-call | tf_op jit(solution)/shard_map/jit(_cho_solve)/triangular_solve | solution.py:132
  (435 shorter events, 277.3 us)
Async XLA Ops:
  0.0 10.7 %copy-start.21 = (s32[516]{0:T(1024)S(1)}, s32[516]{0:T(1024)}, u32[]{:S(2)}) copy-start(s32[516]{0:T(1024)} %constant.386) | copy-start | bytes 6196
  4.3 7.6 %collective-permute-start.2 = (f32[2,2,1]{2,0,1:T(2,128)S(1)}, f32[2,2,1]{2,0,1:T(2,128)S(1)}, u32[]{:S(2)}, u32[]{:S(2)}) collective-permute-start(f32[2,2,1]{2,0,1:T(2,128)S(1)} %fusion.147), channel_id=1, source_target_pairs={{0,4},{4,8},{8,12},{12,16},{16,20},{20,24},{24,28},{28,0},{1,5},{5... | collective-permute-start | bytes 56 | tf_op jit(solution)/shard_map/ppermute | solution.py:18
  7.3 9.2 %collective-permute-start = (f32[2,1,256]{2,0,1:T(2,128)S(1)}, f32[2,1,256]{2,0,1:T(2,128)S(1)}, u32[]{:S(2)}, u32[]{:S(2)}) collective-permute-start(f32[2,1,256]{2,0,1:T(2,128)S(1)} %fusion.146), channel_id=1, source_target_pairs={{0,1},{1,2},{2,3},{4,5},{5,6},{6,7},{8,9},{9,10},{10,11},{12,13},{... | collective-permute-start | bytes 6152 | tf_op jit(solution)/shard_map/ppermute | solution.py:18
  12.0 3.7 collective-permute-start.3
  16.5 3.6 collective-permute-start.1
  161.9 4.8 copy-start.7
  162.8 4.0 copy-start.13
  163.8 2.9 copy-start.17
  167.3 34.5 %copy-start.3 = (f32[512,512]{1,0:T(8,128)}, f32[512,512]{1,0:T(8,128)S(1)}, u32[]{:S(2)}) copy-start(f32[512,512]{1,0:T(8,128)S(1)} %fusion.7) | copy-start | bytes 3145732
  201.9 99.6 %copy-start.2 = (f32[512,512]{0,1:T(8,128)S(1)}, f32[512,512]{0,1:T(8,128)}, u32[]{:S(2)}) copy-start(f32[512,512]{0,1:T(8,128)} %fusion.9) | copy-start | bytes 3145732
  306.6 2.7 copy-start.8
  306.6 2.7 copy-start.14
  306.7 2.7 copy-start.18
  341.1 8.0 %copy-start.19 = (s32[516]{0:T(1024)S(1)}, s32[516]{0:T(1024)}, u32[]{:S(2)}) copy-start(s32[516]{0:T(1024)} %constant.301.clone) | copy-start | bytes 6196
  341.1 8.0 %copy-start.20 = (s32[516]{0:T(1024)S(1)}, s32[516]{0:T(1024)}, u32[]{:S(2)}) copy-start(s32[516]{0:T(1024)} %constant.302.clone) | copy-start | bytes 6196
  346.7 38.0 %collective-permute-start.4 = (f32[2,516,516]{1,0,2:T(2,128)}, f32[2,516,516]{1,0,2:T(2,128)}, u32[]{:S(2)}, u32[]{:S(2)}) collective-permute-start(f32[2,516,516]{1,0,2:T(2,128)} %maximum_subtract_fusion), channel_id=1, source_target_pairs={{0,1},{1,0},{2,3},{3,2},{4,5},{5,4},{6,7},{7,6},{8,9},{9,8},{10,11... | collective-permute-start | bytes 6390152 | tf_op jit(solution)/shard_map/ppermute | solution.py:34
  471.7 1.9 copy-start.12
  480.6 26.0 %copy-start.4 = (f32[256,256]{1,0:T(8,128)}, f32[256,256]{1,0:T(8,128)S(1)}, u32[]{:S(2)}) copy-start(f32[256,256]{1,0:T(8,128)S(1)} %get-tuple-element.522) | copy-start | bytes 786436
  502.2 4.4 copy-start.10
  503.4 6.4 %copy-start = (f32[2,256,260]{1,2,0:T(8,128)S(1)}, f32[2,256,260]{1,2,0:T(8,128)}, u32[]{:S(2)}) copy-start(f32[2,256,260]{1,2,0:T(8,128)} %get-tuple-element.152) | copy-start | bytes 1597444
  503.4 6.4 %copy-start.1 = (f32[2,256,260]{1,2,0:T(8,128)S(1)}, f32[2,256,260]{1,2,0:T(8,128)}, u32[]{:S(2)}) copy-start(f32[2,256,260]{1,2,0:T(8,128)} %get-tuple-element.153) | copy-start | bytes 1597444
  507.2 4.1 copy-start.5
  509.9 2.7 copy-start.6
  579.3 6.6 %copy-start.16 = (f32[2,128,128]{1,2,0:T(8,128)S(1)}, f32[2,128,128]{1,2,0:T(8,128)}, u32[]{:S(2)}) copy-start(f32[2,128,128]{1,2,0:T(8,128)} %custom-call.63) | copy-start | bytes 393220
  (3 other events, 2.0 us)
where the time goes:
time: 613 us; the launch traced here: 608 us
  other arithmetic  397 us (65%)
  local copies, waits for them, and re-layouts  124 us (20%)
  matrix products  60.2 us (10%)
  between operations  10.8 us (2%)
  starting transfers between devices  10.6 us (2%)
    another operation x15, other arithmetic, complex_inverse(): lower_factor = jnp.linalg.cholesky(matrix[0])  80.9 us
    another operation x15, other arithmetic, complex_inverse(): second_factor = jnp.linalg.cholesky(coupled)  79.7 us
    another operation x3, other arithmetic, complex_inverse(): coupling = jax.scipy.linalg.cho_solve((lower_factor, True), matrix[1])  40 us
    another operation x2, other arithmetic, complex_inverse(): inverse_re = jax.scipy.linalg.cho_solve((second_factor, True), identity)  39.7 us
    another operation x7, other arithmetic, complex_solve(): lower_factor = jnp.linalg.cholesky(matrix[0])  36.9 us
    gather x4, local copies, waits for them, and re-layouts, permute(): return jnp.take(jnp.take(local_map, node_order, axis=1), node_order, axis=2)  36.3 us
    another operation x7, other arithmetic, complex_solve(): second_factor = jnp.linalg.cholesky(coupled)  36.2 us
    another operation x3, other arithmetic, complex_solve(): coupling = jax.scipy.linalg.cho_solve((lower_factor, True), matrix[1])  22.6 us
  transfers between devices with their start and end apart: 5, of which 3 were waited for; matrix products, arithmetic and copies ran while one was open for 6% of the time, Pallas kernels for 0%

commit v1 on v0

v1 whole, which is shorter than its diff:
```python
import jax
import jax.numpy as jnp
from jax import lax
from jax.experimental import pallas as pl
from jax.experimental.pallas import tpu as pltpu
from jax.sharding import PartitionSpec as P

SHEET_NODES = 16
LANES = 128
GROUPS = 4


def lane_roll(value, shift):
    return pltpu.roll(value, shift % value.shape[1], 1)


def sub_roll(value, shift):
    return pltpu.roll(value, shift % value.shape[0], 0)


def lane_take(value, index):
    return jnp.take_along_axis(value, index, axis=1, mode="promise_in_bounds")


def iota(dim):
    return lax.broadcasted_iota(jnp.int32, (8, LANES), dim)


class Cx:
    def __init__(self, re, im):
        self.re, self.im = re, im

    def __add__(self, other):
        return Cx(self.re + other.re, self.im + other.im)

    def __sub__(self, other):
        return Cx(self.re - other.re, self.im - other.im)

    def __neg__(self):
        return Cx(-self.re, -self.im)

    def __mul__(self, other):
        if not isinstance(other, Cx):
            return Cx(self.re * other, self.im * other)
        return Cx(
            self.re * other.re - self.im * other.im, self.re * other.im + self.im * other.re
        )

    def inverse(self):
        scale = 1.0 / (self.re * self.re + self.im * self.im)
        return Cx(self.re * scale, -self.im * scale)

    def root(self):
        size = jnp.sqrt(self.re * self.re + self.im * self.im)
        re = jnp.sqrt(0.5 * (size + self.re))
        return Cx(re, 0.5 * self.im / re)

    def map(self, function):
        return Cx(function(self.re), function(self.im))

    def row(self, index):
        return self.map(lambda part: jnp.broadcast_to(part[index : index + 1], (8, LANES)))

    def lanes(self, shift):
        return self.map(lambda part: lane_roll(part, shift))

    def subs(self, shift):
        return self.map(lambda part: sub_roll(part, shift))


def pick(mask, first, second):
    if not isinstance(second, Cx):
        return first.map(lambda part: jnp.where(mask, part, second))
    return Cx(jnp.where(mask, first.re, second.re), jnp.where(mask, first.im, second.im))


def total(terms):
    terms = list(terms)
    while len(terms) > 1:
        terms = [
            terms[i] + terms[i + 1] if i + 1 < len(terms) else terms[i]
            for i in range(0, len(terms), 2)
        ]
    return terms[0]


def harmonic(left, right):
    return (left * right) * (left + right).inverse() * 2.0


def lamination(skin, base):
    above = Cx(jnp.ones_like(skin), jnp.zeros_like(skin))
    field = Cx(jnp.ones_like(skin), 0.5 * skin)
    summed = above
    for _ in range(SHEET_NODES - 1):
        summed = summed + field
        below = Cx(
            2.0 * field.re - skin * field.im - above.re,
            2.0 * field.im + skin * field.re - above.im,
        )
        above, field = field, below
    return field * summed.inverse() * (base * SHEET_NODES)


def factor(entry):
    work = {(r, c): entry(r, c) for r in range(4) for c in range(r + 1)}
    lower, pivots = {}, []
    for k in range(4):
        inverse = work[k, k].inverse()
        pivots.append(inverse)
        for r in range(k + 1, 4):
            lower[r, k] = work[r, k] * inverse
        for r in range(k + 1, 4):
            for c in range(k + 1, r + 1):
                work[r, c] = work[r, c] - lower[r, k] * work[c, k]
    return lower, pivots


def solve(lower, pivots, right):
    half = []
    for r in range(4):
        value = right[r]
        for c in range(r):
            value = value - lower[r, c] * half[c]
        half.append(value)
    out = [None] * 4
    for r in range(3, -1, -1):
        value = half[r] * pivots[r]
        for c in range(r + 1, 4):
            value = value - lower[c, r] * out[c]
        out[r] = value
    return out


def seeds(lower, pivots):
    column = iota(0) & 3
    unit = {}
    for r in range(4):
        for c in range(r - 1, -1, -1):
            value = -lower[r, c]
            for k in range(c + 1, r):
                value = value - lower[r, k] * unit[k, c]
            unit[r, c] = value
    roots = [pivot.root() for pivot in pivots]
    out = []
    for r in range(4):
        value = pick(column == r, roots[r], 0.0)
        for k in range(r + 1, 4):
            value = pick(column == k, roots[k] * unit[k, r], value)
        out.append(value)
    return out


def evens(tiles):
    lane = iota(1)
    index = (2 * lane) & (LANES - 1)

    def one(offset):
        return Cx(
            *(
                jnp.where(
                    lane < LANES // 2,
                    lane_take(first, index + offset),
                    lane_take(second, index + offset),
                )
                for first, second in ((tiles[0].re, tiles[1].re), (tiles[0].im, tiles[1].im))
            )
        )

    return one(0), one(1)


def natural(even, odd):
    lane = iota(1)
    out = []
    for half in range(2):
        index = half * (LANES // 2) + (lane >> 1)
        out.append(
            Cx(
                *(
                    jnp.where((lane & 1) == 0, lane_take(first, index), lane_take(second, index))
                    for first, second in ((even.re, odd.re), (even.im, odd.im))
                )
            )
        )
    return out


def split(value):
    high = value.map(lambda part: part.astype(jnp.bfloat16).astype(jnp.float32))
    return high, value - high


def contract(left, right):
    return lax.dot_general(
        left.astype(jnp.bfloat16),
        right.astype(jnp.bfloat16),
        (((0,), (0,)), ((), ())),
        preferred_element_type=jnp.float32,
    )


def strip(main, side, is_alpha, first_cycle, radial_count):
    lane, sub = iota(1), iota(0)
    lower4 = sub < 4
    column = sub & 3

    cells = lamination(main[0], main[1])
    rims = lamination(side[0], side[1])
    tiles = [cells.map(lambda part: part[:, :LANES]), cells.map(lambda part: part[:, LANES:])]
    cycle = (first_cycle + sub - 1).astype(jnp.float32)
    center = 1.0 + (cycle + 0.5) / radial_count
    face = 1.0 + cycle / radial_count
    per_center = 1.0 / center
    first_lane, last_lane = lane == 0, lane == LANES - 1

    ahead = [tile.lanes(1) for tile in tiles]
    west = [
        harmonic(pick(first_lane, rims.lanes(1), ahead[0]), tiles[0]) * per_center,
        harmonic(pick(first_lane, ahead[0], ahead[1]), tiles[1]) * per_center,
    ]
    wall = harmonic(tiles[1], rims.lanes(-1)) * per_center * 2.0
    back = [tile.lanes(-1) for tile in west]
    east = [pick(last_lane, back[1], back[0]), pick(last_lane, wall, back[1])]
    west[0] = pick(first_lane, west[0] * 2.0, west[0])
    south, north = [], []
    for tile in tiles:
        radial = harmonic(tile.subs(1), tile) * face
        radial = pick((sub == 1) | (sub == 5), radial * 2.0, radial)
        south.append(radial)
        north.append(radial.subs(-1))
    diagonal = [west[h] + east[h] + south[h] + north[h] for h in range(2)]
    gain_in = [south[h].row(1) for h in range(2)]
    gain_out = [north[h].row(4) for h in range(2)]

    diag_e, diag_o = evens(diagonal)
    east_e, east_o = evens(east)
    up_e, up_o = evens(north)
    left_e = pick(last_lane, east_o, 0.0)
    left_e = (east_o - left_e).lanes(1)

    def entry_e(r, c):
        if r == c:
            return diag_e.row(r + 1)
        return -up_e.row(r)

    lower_e, pivots_e = {}, []
    work = diag_e.row(1)
    for r in range(4):
        pivots_e.append(work.inverse())
        if r < 3:
            coupling = up_e.row(r + 1)
            lower_e[r + 1, r] = -(coupling * pivots_e[r])
            work = diag_e.row(r + 2) + lower_e[r + 1, r] * coupling
    zero = jnp.zeros((8, LANES), jnp.float32)
    nothing = Cx(zero, zero)
    half = []
    for r in range(4):
        value = Cx(jnp.where(column == r, 1.0, zero), zero)
        if r:
            value = value - lower_e[r, r - 1] * half[r - 1]
        half.append(value)
    inverse_e = [None] * 4
    for r in range(3, -1, -1):
        value = half[r] * pivots_e[r]
        if r < 3:
            value = value - lower_e[r + 1, r] * inverse_e[r + 1]
        inverse_e[r] = value
    for r in range(4):
        for c in range(r - 1):
            lower_e[r, c] = nothing
    seeds_e = seeds(lower_e, pivots_e)
    sides_e = pick(lower4, left_e.subs(-1), east_e.subs(3))
    reach_e = [inverse_e[r] * sides_e for r in range(4)]
    matrix, pair = [], []
    for r in range(4):
        to_left = (left_e.row(r + 1) * reach_e[r]).lanes(-1)
        to_right = east_e.row(r + 1) * reach_e[r]
        pair.append(pick(lower4, to_right, to_left))
        change = pick(lower4, to_left, to_right)
        base = pick(column == r, diag_o.row(r + 1), 0.0)
        if r < 3:
            base = pick(column == r + 1, -up_o.row(r + 1), base)
        if r > 0:
            base = pick(column == r - 1, -up_o.row(r), base)
        matrix.append(base - change - change.subs(4))

    for level in range(1, 8):
        step = 1 << (level - 1)
        stay = ((lane + 1) & (2 * step - 1)) == 0
        reach = solve(*factor(lambda r, c: matrix[r].row(c)), pair)
        next_matrix, next_pair = [], []
        for r in range(4):
            to_left = total(pair[k].row(r) * reach[k] for k in range(4)).lanes(-step)
            to_right = total(pair[k].row(4 + r) * reach[k] for k in range(4)).lanes(step)
            change = pick(lower4, to_left, to_right)
            change = change + change.subs(4)
            next_matrix.append(pick(stay, matrix[r] - change, matrix[r]))
            next_pair.append(pick(stay, pick(lower4, to_right, to_left), pair[r]))
        matrix, pair = next_matrix, next_pair

    lower, pivots = factor(lambda r, c: matrix[r].row(c))
    reach = solve(lower, pivots, pair)
    reach_rows = [[reach[r].row(k) for k in range(8)] for r in range(4)]
    seed = seeds(lower, pivots)

    def level_of(group):
        return jnp.where(lower4, 2 * group - 1, 2 * group)

    own_level = jnp.ones((8, LANES), jnp.int32)
    for level in range(2, 9):
        own_level = own_level + (((lane + 1) & ((1 << (level - 1)) - 1)) == 0).astype(jnp.int32)

    odd = {}
    for group in range(1, GROUPS + 1):
        rows = [pick(own_level == level_of(group), seed[r], 0.0) for r in range(4)]
        for level in range(min(2 * group - 1, 7), 0, -1):
            step = 1 << (level - 1)
            here = own_level == level
            before = [row.lanes(step) for row in rows]
            after = [row.lanes(-step) for row in rows]
            fresh = []
            for r in range(4):
                terms = [reach_rows[r][k] * before[k] for k in range(4)]
                terms += [reach_rows[r][4 + k] * after[k] for k in range(4)]
                fresh.append(rows[r] + pick(here, total(terms), 0.0))
            rows = fresh
        odd[group] = rows

    reach_e_rows = [[reach_e[r].row(k) for k in range(8)] for r in range(4)]
    even = {0: [pick(first_lane & lower4, seeds_e[r], 0.0) for r in range(4)]}
    odd[0] = [nothing] * 4
    for group in range(1, GROUPS + 1):
        before = [row.lanes(1) for row in odd[group]]
        even[group] = []
        for r in range(4):
            terms = [reach_e_rows[r][k] * before[k] for k in range(4)]
            terms += [reach_e_rows[r][4 + k] * odd[group][k] for k in range(4)]
            even[group].append(total(terms))

    def corners(lefts, rights):
        return pick(
            lane == 0,
            lefts[0],
            pick(
                lane == 1,
                lefts[1].lanes(1),
                pick(lane == 2, rights[0].lanes(3), pick(lane == 3, rights[1].lanes(4), 0.0)),
            ),
        )

    gains_left = [west[0].row(r + 1) for r in range(4)]
    gains_right = [east[1].row(r + 1) for r in range(4)]
    gain_corner = [
        corners(gains_left[2 * t : 2 * t + 2], gains_right[2 * t : 2 * t + 2]) for t in range(2)
    ]
    inner, outer, corner = {}, {}, {}
    for group in range(GROUPS + 1):
        if group:
            low = natural(even[group][0], odd[group][0])
            high = natural(even[group][3], odd[group][3])
        else:
            low, high = [even[0][0], nothing], [even[0][3], nothing]
        inner[group] = [low[h] * gain_in[h] for h in range(2)]
        outer[group] = [high[h] * gain_out[h] for h in range(2)]
        corner[group] = [
            corners(even[group][2 * t : 2 * t + 2], odd[group][2 * t : 2 * t + 2]) * gain_corner[t]
            for t in range(2)
        ]

    left_parts, right_parts = [], []
    for group in range(GROUPS + 1):
        if group in (0, GROUPS):
            low, high = inner[group], outer[group]
        else:
            near = lane < (2 << level_of(group))
            low = [pick(near, inner[group][0], 0.0), nothing]
            high = [pick(near, outer[group][0], 0.0), nothing]
        side_a, side_b = corner[group]
        own = [pick(is_alpha, low[h], high[h]) for h in range(2)]
        own.append(pick(is_alpha, side_a, side_b))
        moved = [high[0].lanes(4), high[1].lanes(4)]
        every = [
            low[0],
            low[1],
            pick(lower_lanes(lane, 4), side_a, moved[0]),
            pick(lower_lanes(lane, 4), moved[0], moved[1]),
            pick(lower_lanes(lane, 4), moved[1], pick(lane < 8, side_b.lanes(4), 0.0)),
        ]
        left_parts.append([split(value) for value in own])
        right_parts.append([split(value) for value in every])

    def wide(parts, which, name, sign=1.0):
        rows = []
        for group in parts:
            pieces = [getattr(value[which], name) for value in group]
            rows.append(jnp.concatenate(pieces, axis=1) * sign)
        return rows

    fill = [jnp.zeros((8, 3 * LANES), jnp.float32)] * 2
    left = (
        wide(left_parts, 0, "re")
        + wide(left_parts, 0, "re")
        + wide(left_parts, 1, "re")
        + wide(left_parts, 0, "im")
        + wide(left_parts, 0, "im")
        + wide(left_parts, 1, "im")
        + fill
    )
    fill = [jnp.zeros((8, 5 * LANES), jnp.float32)] * 2
    right_re = (
        wide(right_parts, 0, "re")
        + wide(right_parts, 1, "re")
        + wide(right_parts, 0, "re")
        + wide(right_parts, 0, "im", -1.0)
        + wide(right_parts, 1, "im", -1.0)
        + wide(right_parts, 0, "im", -1.0)
        + fill
    )
    right_im = (
        wide(right_parts, 0, "im")
        + wide(right_parts, 1, "im")
        + wide(right_parts, 0, "im")
        + wide(right_parts, 0, "re")
        + wide(right_parts, 1, "re")
        + wide(right_parts, 0, "re")
        + fill
    )
    left = jnp.concatenate(left, axis=0)
    top = Cx(
        contract(left, jnp.concatenate(right_re, axis=0)),
        contract(left, jnp.concatenate(right_im, axis=0)),
    )

    masks = []
    for level in range(1, 7):
        for tile in range(max((1 << (6 - level)) // 2, 1)):
            masks.append((level, (lane >> (level + 1)) == 2 * tile + (sub >> 2)))

    def spread(value):
        out = []
        for level, mask in masks:
            out.append(jnp.where(mask, value[level], 0.0))
        return jnp.concatenate(out, axis=0)

    def both(values, half):
        levels = {}
        for group in range(1, GROUPS):
            value = values[group][half]
            if half == 0:
                value = pick(lane < (2 << level_of(group)), nothing, value)
            turned = value.subs(4)
            levels[2 * group - 1] = split(pick(lower4, value, turned))
            levels[2 * group] = split(pick(lower4, turned, value))
        return {
            (which, name): spread(
                {level: getattr(pair[which], name) for level, pair in levels.items()}
            )
            for which in range(2)
            for name in ("re", "im")
        }

    even_d = [inverse_e[0].row(0), inverse_e[0].row(3), inverse_e[3].row(3)]
    even_d = [natural(value, nothing) for value in even_d]
    local = []
    for half in range(2):
        low, high = both(inner, half), both(outer, half)
        own = {key: jnp.where(is_alpha, low[key], high[key]) for key in low}
        every = {key: jnp.concatenate([low[key], high[key]], axis=1) for key in low}
        hr, hi, lr, li = (0, "re"), (0, "im"), (1, "re"), (1, "im")
        left = jnp.concatenate([own[key] for key in (hr, hi, hr, hi, lr, li)], axis=0)
        right_re = jnp.concatenate(
            [every[hr], -every[hi], every[lr], -every[li], every[hr], -every[hi]], axis=0
        )
        right_im = jnp.concatenate([every[key] for key in (hi, hr, li, lr, hi, hr)], axis=0)
        product = Cx(contract(left, right_re), contract(left, right_im))
        g_in, g_out = gain_in[half], gain_out[half]
        solo = (lane & 1) == 0
        if half == 0:
            solo = solo & (lane > 0)
        cross = even_d[1][half] * g_in * g_out
        on_in = pick(is_alpha, even_d[0][half] * g_in * g_in, cross)
        on_out = pick(is_alpha, cross, even_d[2][half] * g_out * g_out)
        on_in = pick(solo, on_in, 0.0) - pick(is_alpha, g_in, nothing)
        on_out = pick(solo, on_out, 0.0) - pick(is_alpha, nothing, g_out)
        local.append((product, on_in, on_out))
    edge = pick((lane == sub) & lower4, pick(is_alpha, gain_corner[0], gain_corner[1]), 0.0)
    return top, local, edge


def lower_lanes(lane, count):
    return lane < count


def finish(top, local, edge, is_alpha, store):
    lane, sub = iota(1), iota(0)
    for part, name in enumerate(("re", "im")):
        full = getattr(top, name)
        edge_part = getattr(edge, name)
        for half in range(2):
            product = getattr(local[half][0], name)
            on_in = getattr(local[half][1], name)
            on_out = getattr(local[half][2], name)
            for row in range(0, LANES, 8):
                here = lane == sub + row
                low = product[row : row + 8, :LANES] + jnp.where(here, on_in, 0.0)
                high = product[row : row + 8, LANES:] + jnp.where(here, on_out, 0.0)
                high = lane_roll(high, 4)
                at = half * LANES + row
                out = [full[at : at + 8, t * LANES : (t + 1) * LANES] for t in range(5)]
                out[half] = out[half] + low
                out[2 + half] = out[2 + half] + jnp.where(lane < 4, 0.0, high)
                out[3 + half] = out[3 + half] + jnp.where(lane < 4, high, 0.0)
                store(part, at, 8, [-value for value in out])
        at = 2 * LANES
        out = [full[at : at + 8, t * LANES : (t + 1) * LANES] for t in range(5)]
        out[2] = out[2] - jnp.where(is_alpha, edge_part, 0.0)
        out[4] = out[4] - jnp.where(is_alpha, 0.0, lane_roll(edge_part, 4))
        store(part, at, 4, [-value for value in out])


def gather_rows(own, sides, partner, near, far, is_alpha, is_first, is_last, main, side):
    lane = lax.broadcasted_iota(jnp.int32, (2, LANES), 1)
    for field in range(2):
        at = 2 * field
        mine, other = own[at : at + 2, :], partner[at : at + 2, :]
        alpha = jnp.where(is_alpha, mine, other)
        beta = jnp.where(is_alpha, other, mine)
        below = jnp.where(is_alpha, near[at + 1 : at + 2, :], far[at + 1 : at + 2, :])
        above = jnp.where(is_alpha, far[at : at + 1, :], near[at : at + 1, :])
        main[field, 0:1, :] = jnp.where(is_first, alpha[0:1], below)
        main[field, 1:3, :] = alpha
        main[field, 3:5, :] = beta
        main[field, 5:6, :] = jnp.where(is_last, beta[1:2], above)
        main[field, 6:8, :] = beta
        left_own, right_own = sides[at : at + 2, LANES:], sides[4 + at : 6 + at, :LANES]
        left_other = partner[4 + at : 6 + at, LANES:]
        right_other = partner[8 + at : 10 + at, :LANES]
        ends_own = jnp.where(lane == LANES - 1, left_own, jnp.where(lane == 0, right_own, 1.0))
        ends_other = jnp.where(
            lane == LANES - 1, left_other, jnp.where(lane == 0, right_other, 1.0)
        )
        ends_alpha = jnp.where(is_alpha, ends_own, ends_other)
        ends_beta = jnp.where(is_alpha, ends_other, ends_own)
        side[field, 0:1, :] = ends_alpha[0:1]
        side[field, 1:3, :] = ends_alpha
        side[field, 3:5, :] = ends_beta
        side[field, 5:7, :] = ends_beta
        side[field, 7:8, :] = ends_beta[0:1]


def merge_kernel(cycles, depth, own, sides, partner, near, far, out, main, side):
    index = lax.axis_index("rad")
    is_alpha = index % 2 == 0
    is_first = index // 2 == 0
    is_last = index // 2 == cycles // 2 - 1
    gather_rows(own, sides, partner, near, far, is_alpha, is_first, is_last, main, side)
    top, local, edge = strip(
        (main[0], main[1]),
        (side[0], side[1]),
        is_alpha,
        (index // 2) * (2 * depth),
        cycles * depth,
    )

    def store(part, row, count, tiles):
        for number, tile in enumerate(tiles):
            width = min(LANES, out.shape[2] - number * LANES)
            out[part, row : row + count, number * LANES : number * LANES + width] = tile[
                :count, :width
            ]

    finish(top, local, edge, is_alpha, store)


def cell_inputs(material_id, thickness, sigma_table, nu_table, angular_frequency):
    levels = jnp.arange(sigma_table.shape[0], dtype=jnp.int32)
    onehot = (material_id[None] == levels[:, None, None]).astype(jnp.float32)
    sigma_cell = jnp.sum(onehot * sigma_table[:, None, None], axis=0)
    base_value = jnp.sum(onehot * nu_table[:, None, None], axis=0)
    angular = angular_frequency[0]
    skin_ratio = angular * sigma_cell * thickness * thickness
    return (skin_ratio, base_value)


def per_device(material_id, thickness, sigma_table, nu_table, angular_frequency):
    depth, arc = thickness.shape
    cells = jnp.concatenate(
        cell_inputs(material_id, thickness, sigma_table, nu_table, angular_frequency), axis=0
    )
    cycles, blocks = lax.axis_size("rad"), lax.axis_size("az")
    left = lax.ppermute(cells, "az", [(i, (i + 1) % blocks) for i in range(blocks)])
    right = lax.ppermute(cells, "az", [((i + 1) % blocks, i) for i in range(blocks)])
    near, far = [], []
    for low in range(1, cycles - 1, 2):
        near += [(low, low + 1), (low + 1, low)]
    for low in range(0, cycles - 2, 2):
        far += [(low + 2, low), (low + 1, low + 3)]
    near = lax.ppermute(cells, "rad", near)
    far = lax.ppermute(cells, "rad", far)
    swap = [(i, i ^ 1) for i in range(cycles)]
    partner = lax.ppermute(jnp.concatenate([cells, left, right], axis=0), "rad", swap)
    outer_nodes = arc + 2 * depth
    return pl.pallas_call(
        lambda *refs: merge_kernel(cycles, depth, *refs),
        out_shape=jax.ShapeDtypeStruct((2, outer_nodes, 2 * outer_nodes), jnp.float32),
        in_specs=[pl.BlockSpec(memory_space=pltpu.VMEM)] * 5,
        out_specs=pl.BlockSpec(memory_space=pltpu.VMEM),
        scratch_shapes=[
            pltpu.VMEM((2, 8, arc), jnp.float32),
            pltpu.VMEM((2, 8, LANES), jnp.float32),
        ],
        compiler_params=pltpu.CompilerParams(vmem_limit_bytes=48 * 1024 * 1024),
        name="pair_map",
    )(cells, jnp.concatenate([left, right], axis=0), partner, near, far)


def solution(mesh):
    placed = (P("rad", "az"), P("rad", "az"), P(), P(), P())
    return jax.shard_map(
        per_device, mesh=mesh, in_specs=placed, out_specs=P(None, "rad", "az"), check_vma=False
    )
```

time: 613 us -> 21.5 us (0.04)
  other arithmetic: 397 us -> 1.49 us
  local copies, waits for them, and re-layouts: 124 us -> 1.75 us
  matrix products: 60.2 us -> 0 us
  between operations: 10.8 us -> 0.72 us
    another operation x84 -> x0, other arithmetic: 357 us -> none  [the longest x15 80.9 us: complex_inverse(): lower_factor = jnp.linalg.cholesky(matrix[0])]
    gather x7 -> x0, local copies, waits for them, and re-layouts: 53.3 us -> none  [the longest x4 36.3 us: permute(): return jnp.take(jnp.take(local_map, node_order, axis=1), node_order, axis=2)]
    another operation x62 -> x0, matrix products: 39.2 us -> none  [the longest x14 7.72 us: complex_inverse(): inverse_re = jax.scipy.linalg.cho_solve((second_factor, True), identity)]
    another operation x60 -> x0, local copies, waits for them, and re-layouts: 28.2 us -> none  [the longest x15 8.59 us: complex_inverse(): coupling = jax.scipy.linalg.cho_solve((lower_factor, True), matrix[1])]
    dot_general x9 -> x0, matrix products: 21 us -> none  [matmul(): return jnp.dot(left_factor, right_factor, precision=lax.Precision.HIGHEST)]
    sub x35 -> x0, other arithmetic: 15.6 us -> none  [the longest x18 7.2 us: complex_times(): left_value[0] * right_value[0] - left_value[1] * right_value[1]]
    select_n x2 -> x0, local copies, waits for them, and re-layouts: 14.2 us -> none  [permute(): return jnp.take(jnp.take(local_map, node_order, axis=1), node_order, axis=2)]
    select_n x8 -> x0, other arithmetic: 13.8 us -> none  [the longest x5 12.4 us: permute(): return jnp.take(jnp.take(local_map, node_order, axis=1), node_order, axis=2)]
  transfers between devices with their start and end apart: 5 -> 5, of which waited for: 3 -> 2; matrix products, arithmetic and copies ran while one was open for 6% -> 0% of each run, Pallas kernels for 0% -> 0%
where the time goes in v1:
time: 21.5 us; the launch traced here: 21.3 us
  starting transfers between devices  8.07 us (38%)
  waiting for transfers between devices  5.47 us (25%)
  Pallas kernels  3.8 us (18%)
  local copies, waits for them, and re-layouts  1.75 us (8%)
  other arithmetic  1.49 us (7%)
  between operations  0.72 us (3%)
    ppermute x1, starting transfers between devices, per_device(): lax.ppermute(cells, 'az', [((i + 1) % blocks, i) for i in range(blocks)])  6.05 us
    ppermute x1, waiting for transfers between devices, per_device(): lax.ppermute(cells, 'az', [(i, (i + 1) % blocks) for i in range(blocks)])  4.33 us
    pallas_call x1, Pallas kernels, per_device(): pl.pallas_call(lambda *refs: merge_kernel(cycles, depth, *refs), out_shap...  3.8 us
    pallas_call x1, local copies, waits for them, and re-layouts, per_device(): pl.pallas_call(lambda *refs: merge_kernel(cycles, depth, *refs), out_shap...  1.75 us
    ppermute x1, starting transfers between devices, per_device(): far = lax.ppermute(cells, 'rad', far)  1.28 us
    ppermute x1, waiting for transfers between devices, per_device(): lax.ppermute(jnp.concatenate([cells, left, right], axis=0), 'rad', swap)  1.13 us
    reduce_sum x1, other arithmetic, cell_inputs(): sigma_cell = jnp.sum(onehot * sigma_table[:, None, None], axis=0)  0.77 us
    mul x1, other arithmetic, cell_inputs(): skin_ratio = angular * sigma_cell * thickness * thickness  0.69 us
  transfers between devices with their start and end apart: 5, of which 2 were waited for; matrix products, arithmetic and copies ran while one was open for 0% of the time, Pallas kernels for 0%

profile of v1, /device:TPU:0, one launch (start us, length us, event | category | flops | bytes accessed | tf_op | source)
XLA Modules:
  0.0 21.3 jit_solution(15331088057514900768)
XLA Ops:
  0.7 0.8 %select_reduce_fusion.1 = (f32[2,256]{1,0:T(2,128)S(1)}, f32[2,256]{1,0:T(2,128)S(1)}) fusion(f32[8]{0:T(128)} %param.7, s32[2,256]{1,0:T(2,128)} %param.5, f32[8]{0:T(128)} %param.8), kind=kLoop, calls=%fused_computation.2 | loop fusion | flops 19456 | bytes 6208 | tf_op jit(solution)/shard_map/reduce_sum | solution.py:579
  1.4 0.7 %multiply_multiply_fusion = f32[2,256]{1,0:T(2,128)S(1)} fusion(f32[2,256]{1,0:T(2,128)} %param.6, f32[2,256]{1,0:T(2,128)S(1)} %get-tuple-element.5, f32[]{:T(128)} %bitcast.1), kind=kLoop, calls=%fused_computation.6 | loop fusion | flops 1536 | bytes 6148 | tf_op jit(solution)/shard_map/mul | solution.py:582
  2.1 6.1 %collective-permute-start.1 = (f32[4,256]{1,0:T(4,128)S(1)}, f32[4,256]{1,0:T(4,128)S(1)}, u32[]{:S(2)}, u32[]{:S(2)}) collective-permute-start(f32[4,256]{1,0:T(4,128)S(1)} %pad_maximum_fusion.2.refs_0_), channel_id=1, source_target_pairs={{4,0},{8,4},{12,8},{16,12},{20,16},{24,20},{28,24},{0,28},{5,1},{9... | collective-permute-start | bytes 12296 | tf_op jit(solution)/shard_map/ppermute | solution.py:593
  8.2 0.0 collective-permute-start
  8.2 1.3 %collective-permute-start.4 = (f32[4,256]{1,0:T(4,128)S(1)}, f32[4,256]{1,0:T(4,128)S(1)}, u32[]{:S(2)}, u32[]{:S(2)}) collective-permute-start(f32[4,256]{1,0:T(4,128)S(1)} %pad_maximum_fusion.2.refs_0_), channel_id=1, source_target_pairs={{2,0},{1,3},{6,4},{5,7},{10,8},{9,11},{14,12},{13,15},{18,16},{17,... | collective-permute-start | bytes 12296 | tf_op jit(solution)/shard_map/ppermute | solution.py:600
  9.5 0.7 %collective-permute-start.3 = (f32[4,256]{1,0:T(4,128)S(1)}, f32[4,256]{1,0:T(4,128)S(1)}, u32[]{:S(2)}, u32[]{:S(2)}) collective-permute-start(f32[4,256]{1,0:T(4,128)S(1)} %pad_maximum_fusion.2.refs_0_), channel_id=1, source_target_pairs={{1,2},{2,1},{5,6},{6,5},{9,10},{10,9},{13,14},{14,13},{17,18},{18,... | collective-permute-start | bytes 12296 | tf_op jit(solution)/shard_map/ppermute | solution.py:599
  10.1 0.0 collective-permute-done.1
  10.2 4.3 %collective-permute-done = f32[4,256]{1,0:T(4,128)S(1)} collective-permute-done((f32[4,256]{1,0:T(4,128)S(1)}, f32[4,256]{1,0:T(4,128)S(1)}, u32[]{:S(2)}, u32[]{:S(2)}) %collective-permute-start) | collective-permute-done | bytes 4128 | tf_op jit(solution)/shard_map/ppermute | solution.py:592
  14.5 0.1 collective-permute-start.2
  14.6 0.0 collective-permute-done.4.refs_4_
  14.6 0.0 collective-permute-done.3.refs_3_
  14.6 1.1 %collective-permute-done.2.refs_2_ = f32[12,256]{1,0:T(8,128)S(1)} collective-permute-done((f32[12,256]{1,0:T(8,128)S(1)}, f32[12,256]{1,0:T(8,128)S(1)}, u32[]{:S(2)}, u32[]{:S(2)}) %collective-permute-start.2) | collective-permute-done | bytes 12320 | tf_op jit(solution)/shard_map/ppermute | solution.py:602
  15.8 3.8 %pair_map.1 = f32[2,260,520]{2,1,0:T(8,128)S(1)} custom-call(f32[4,256]{1,0:T(4,128)S(1)} %pad_maximum_fusion.2.refs_0_, f32[8,256]{1,0:T(8,128)S(1)} %pad_maximum_fusion.1.refs_1_, f32[12,256]{1,0:T(8,128)S(1)} %collective-permute-done.2.refs_2_, f32[4,256]{1,0:T(4,128)S(1)} %collective-permute-done.3.refs_3_, f32[4,256]{1,0:T(4,128)S(1)} %collective-permute-done.4.refs_4_), custom_call_target="tpu_custom_call" | custom-call | tf_op jit(solution)/shard_map/pair_map/pallas_call | solution.py:604
  19.6 1.7 %copy.7 = f32[2,260,520]{2,0,1:T(2,128)} copy(f32[2,260,520]{2,1,0:T(8,128)S(1)} %pair_map.1) | data formatting | bytes 2163200 | tf_op jit(solution)/shard_map/pair_map/pallas_call | solution.py:604
  (3 shorter events, 0.0 us)
Async XLA Ops:
  2.1 8.0 %collective-permute-start.1 = (f32[4,256]{1,0:T(4,128)S(1)}, f32[4,256]{1,0:T(4,128)S(1)}, u32[]{:S(2)}, u32[]{:S(2)}) collective-permute-start(f32[4,256]{1,0:T(4,128)S(1)} %pad_maximum_fusion.2.refs_0_), channel_id=1, source_target_pairs={{4,0},{8,4},{12,8},{16,12},{20,16},{24,20},{28,24},{0,28},{5,1},{9... | collective-permute-start | bytes 12296 | tf_op jit(solution)/shard_map/ppermute | solution.py:593
  8.2 6.3 %collective-permute-start = (f32[4,256]{1,0:T(4,128)S(1)}, f32[4,256]{1,0:T(4,128)S(1)}, u32[]{:S(2)}, u32[]{:S(2)}) collective-permute-start(f32[4,256]{1,0:T(4,128)S(1)} %pad_maximum_fusion.2.refs_0_), channel_id=1, source_target_pairs={{0,4},{4,8},{8,12},{12,16},{16,20},{20,24},{24,28},{28,0},{1,5},{5... | collective-permute-start | bytes 12296 | tf_op jit(solution)/shard_map/ppermute | solution.py:592
  8.2 6.4 %collective-permute-start.4 = (f32[4,256]{1,0:T(4,128)S(1)}, f32[4,256]{1,0:T(4,128)S(1)}, u32[]{:S(2)}, u32[]{:S(2)}) collective-permute-start(f32[4,256]{1,0:T(4,128)S(1)} %pad_maximum_fusion.2.refs_0_), channel_id=1, source_target_pairs={{2,0},{1,3},{6,4},{5,7},{10,8},{9,11},{14,12},{13,15},{18,16},{17,... | collective-permute-start | bytes 12296 | tf_op jit(solution)/shard_map/ppermute | solution.py:600
  9.5 5.1 %collective-permute-start.3 = (f32[4,256]{1,0:T(4,128)S(1)}, f32[4,256]{1,0:T(4,128)S(1)}, u32[]{:S(2)}, u32[]{:S(2)}) collective-permute-start(f32[4,256]{1,0:T(4,128)S(1)} %pad_maximum_fusion.2.refs_0_), channel_id=1, source_target_pairs={{1,2},{2,1},{5,6},{6,5},{9,10},{10,9},{13,14},{14,13},{17,18},{18,... | collective-permute-start | bytes 12296 | tf_op jit(solution)/shard_map/ppermute | solution.py:599
  14.5 1.2 %collective-permute-start.2 = (f32[12,256]{1,0:T(8,128)S(1)}, f32[12,256]{1,0:T(8,128)S(1)}, u32[]{:S(2)}, u32[]{:S(2)}) collective-permute-start(f32[12,256]{1,0:T(8,128)S(1)} %pad_maximum_fusion), channel_id=1, source_target_pairs={{0,1},{1,0},{2,3},{3,2},{4,5},{5,4},{6,7},{7,6},{8,9},{9,8},{10,11... | collective-permute-start | bytes 36872 | tf_op jit(solution)/shard_map/ppermute | solution.py:602

commit v2 on v1

--- a/solution.py
+++ b/solution.py
@@ -519,29 +519,27 @@
         store(part, at, 4, [-value for value in out])
 
 
-def gather_rows(own, sides, partner, near, far, is_alpha, is_first, is_last, main, side):
+def gather_rows(own, partner, is_alpha, is_even, is_first, is_last, main, side):
     lane = lax.broadcasted_iota(jnp.int32, (2, LANES), 1)
     for field in range(2):
         at = 2 * field
         mine, other = own[at : at + 2, :], partner[at : at + 2, :]
         alpha = jnp.where(is_alpha, mine, other)
         beta = jnp.where(is_alpha, other, mine)
-        below = jnp.where(is_alpha, near[at + 1 : at + 2, :], far[at + 1 : at + 2, :])
-        above = jnp.where(is_alpha, far[at : at + 1, :], near[at : at + 1, :])
-        main[field, 0:1, :] = jnp.where(is_first, alpha[0:1], below)
+        near, far = own[12 + at : 14 + at, :], partner[12 + at : 14 + at, :]
+        main[field, 0:1, :] = jnp.where(is_first, alpha[0:1], jnp.where(is_alpha, near, far)[1:2])
         main[field, 1:3, :] = alpha
         main[field, 3:5, :] = beta
-        main[field, 5:6, :] = jnp.where(is_last, beta[1:2], above)
+        main[field, 5:6, :] = jnp.where(is_last, beta[1:2], jnp.where(is_alpha, far, near)[0:1])
         main[field, 6:8, :] = beta
-        left_own, right_own = sides[at : at + 2, LANES:], sides[4 + at : 6 + at, :LANES]
-        left_other = partner[4 + at : 6 + at, LANES:]
-        right_other = partner[8 + at : 10 + at, :LANES]
-        ends_own = jnp.where(lane == LANES - 1, left_own, jnp.where(lane == 0, right_own, 1.0))
-        ends_other = jnp.where(
-            lane == LANES - 1, left_other, jnp.where(lane == 0, right_other, 1.0)
-        )
-        ends_alpha = jnp.where(is_alpha, ends_own, ends_other)
-        ends_beta = jnp.where(is_alpha, ends_other, ends_own)
+        ends = []
+        for tiles in (own, partner):
+            long, short = tiles[4 + at : 6 + at, :], tiles[8 + at : 10 + at, :]
+            left = jnp.where(is_even, long, short)[:, LANES:]
+            right = jnp.where(is_even, short, long)[:, :LANES]
+            ends.append(jnp.where(lane == LANES - 1, left, jnp.where(lane == 0, right, 1.0)))
+        ends_alpha = jnp.where(is_alpha, ends[0], ends[1])
+        ends_beta = jnp.where(is_alpha, ends[1], ends[0])
         side[field, 0:1, :] = ends_alpha[0:1]
         side[field, 1:3, :] = ends_alpha
         side[field, 3:5, :] = ends_beta
@@ -549,12 +547,13 @@
         side[field, 7:8, :] = ends_beta[0:1]
 
 
-def merge_kernel(cycles, depth, own, sides, partner, near, far, out, main, side):
+def merge_kernel(cycles, depth, own, partner, out, main, side):
     index = lax.axis_index("rad")
+    is_even = lax.axis_index("az") % 2 == 0
     is_alpha = index % 2 == 0
     is_first = index // 2 == 0
     is_last = index // 2 == cycles // 2 - 1
-    gather_rows(own, sides, partner, near, far, is_alpha, is_first, is_last, main, side)
+    gather_rows(own, partner, is_alpha, is_even, is_first, is_last, main, side)
     top, local, edge = strip(
         (main[0], main[1]),
         (side[0], side[1]),
@@ -573,38 +572,65 @@
     finish(top, local, edge, is_alpha, store)
 
 
-def cell_inputs(material_id, thickness, sigma_table, nu_table, angular_frequency):
-    levels = jnp.arange(sigma_table.shape[0], dtype=jnp.int32)
-    onehot = (material_id[None] == levels[:, None, None]).astype(jnp.float32)
-    sigma_cell = jnp.sum(onehot * sigma_table[:, None, None], axis=0)
-    base_value = jnp.sum(onehot * nu_table[:, None, None], axis=0)
-    angular = angular_frequency[0]
-    skin_ratio = angular * sigma_cell * thickness * thickness
-    return (skin_ratio, base_value)
+def cell_kernel(*refs):
+    sources, (out_ref,), targets, sems = refs[:5], refs[5:6], refs[6:11], refs[11]
+    copies = [
+        pltpu.make_async_copy(source, target, sems.at[number])
+        for number, (source, target) in enumerate(zip(sources, targets))
+    ]
+    for copy in copies:
+        copy.start()
+    for copy in copies:
+        copy.wait()
+    material_ref, sheet_ref, sigma_ref, nu_ref, angular_ref = targets
+    material, sheet = material_ref[...], sheet_ref[...]
+    sigma, base = jnp.zeros_like(sheet), jnp.zeros_like(sheet)
+    for level in range(sigma_ref.shape[0]):
+        sigma = jnp.where(material == level, sigma_ref[level], sigma)
+        base = jnp.where(material == level, nu_ref[level], base)
+    out_ref[:2, :] = angular_ref[0] * sigma * sheet * sheet
+    out_ref[2:, :] = base
+
+
+def cell_inputs(*arguments):
+    spaces = (pltpu.VMEM, pltpu.VMEM, pltpu.SMEM, pltpu.SMEM, pltpu.SMEM)
+    return pl.pallas_call(
+        cell_kernel,
+        out_shape=jax.ShapeDtypeStruct((4, arguments[1].shape[1]), jnp.float32),
+        in_specs=[pl.BlockSpec(memory_space=pltpu.HBM)] * 5,
+        out_specs=pl.BlockSpec(memory_space=pltpu.VMEM),
+        scratch_shapes=[
+            space(value.shape, value.dtype) for space, value in zip(spaces, arguments)
+        ]
+        + [pltpu.SemaphoreType.DMA((5,))],
+        compiler_params=pltpu.CompilerParams(vmem_limit_bytes=63 * 1024 * 1024),
+        name="cells",
+    )(*arguments)
+
+
+def swapped(cells, axis, first):
+    count = lax.axis_size(axis)
+    route = []
+    for low in range(first, count, 2):
+        high = (low + 1) % count
+        if high or axis == "az":
+            route += [(low, high), (high, low)]
+    return lax.ppermute(cells, axis, route)
 
 
 def per_device(material_id, thickness, sigma_table, nu_table, angular_frequency):
     depth, arc = thickness.shape
-    cells = jnp.concatenate(
-        cell_inputs(material_id, thickness, sigma_table, nu_table, angular_frequency), axis=0
-    )
-    cycles, blocks = lax.axis_size("rad"), lax.axis_size("az")
-    left = lax.ppermute(cells, "az", [(i, (i + 1) % blocks) for i in range(blocks)])
-    right = lax.ppermute(cells, "az", [((i + 1) % blocks, i) for i in range(blocks)])
-    near, far = [], []
-    for low in range(1, cycles - 1, 2):
-        near += [(low, low + 1), (low + 1, low)]
-    for low in range(0, cycles - 2, 2):
-        far += [(low + 2, low), (low + 1, low + 3)]
-    near = lax.ppermute(cells, "rad", near)
-    far = lax.ppermute(cells, "rad", far)
-    swap = [(i, i ^ 1) for i in range(cycles)]
-    partner = lax.ppermute(jnp.concatenate([cells, left, right], axis=0), "rad", swap)
+    cells = cell_inputs(material_id, thickness, sigma_table, nu_table, angular_frequency)
+    cycles = lax.axis_size("rad")
+    near = swapped(cells, "rad", 1)
+    short = swapped(cells, "az", 0)
+    long = swapped(cells, "az", 1)
+    known = jnp.concatenate([cells, long, short, near], axis=0)
     outer_nodes = arc + 2 * depth
     return pl.pallas_call(
         lambda *refs: merge_kernel(cycles, depth, *refs),
         out_shape=jax.ShapeDtypeStruct((2, outer_nodes, 2 * outer_nodes), jnp.float32),
-        in_specs=[pl.BlockSpec(memory_space=pltpu.VMEM)] * 5,
+        in_specs=[pl.BlockSpec(memory_space=pltpu.VMEM)] * 2,
         out_specs=pl.BlockSpec(memory_space=pltpu.VMEM),
         scratch_shapes=[
             pltpu.VMEM((2, 8, arc), jnp.float32),
@@ -612,7 +638,7 @@
         ],
         compiler_params=pltpu.CompilerParams(vmem_limit_bytes=48 * 1024 * 1024),
         name="pair_map",
-    )(cells, jnp.concatenate([left, right], axis=0), partner, near, far)
+    )(known, swapped(known, "rad", 0))
 
 
 def solution(mesh):

time: 21.5 us -> 21.1 us (0.981)
  waiting for transfers between devices: 5.47 us -> 3.81 us
  Pallas kernels: 3.8 us -> 5.27 us
  other arithmetic: 1.49 us -> 0.7 us
  starting transfers between devices: 8.07 us -> 8.73 us
    ppermute x5 -> x4, waiting for transfers between devices: 5.47 us -> 3.81 us  [swapped(): return lax.ppermute(cells, axis, route)]
    pallas_call x0 -> x1, Pallas kernels: none -> 1.46 us  [cell_inputs(): pl.pallas_call(cell_kernel, out_shape=jax.ShapeDtypeStruct((4, arguments[...]
    reduce_sum x1 -> x0, other arithmetic: 0.77 us -> none  [cell_inputs(): sigma_cell = jnp.sum(onehot * sigma_table[:, None, None], axis=0)]
    mul x1 -> x0, other arithmetic: 0.69 us -> none  [cell_inputs(): skin_ratio = angular * sigma_cell * thickness * thickness]
    concatenate x3 -> x1, other arithmetic: 0.03 us -> 0.7 us  [per_device(): known = jnp.concatenate([cells, long, short, near], axis=0)]
    ppermute x5 -> x4, starting transfers between devices: 8.07 us -> 8.73 us  [swapped(): return lax.ppermute(cells, axis, route)]
  transfers between devices with their start and end apart: 5 -> 4, of which waited for: 2 -> 2; matrix products, arithmetic and copies ran while one was open for 0% -> 0% of each run, Pallas kernels for 0% -> 0%
where the time goes in v2:
time: 21.1 us; the launch traced here: 20.9 us
  starting transfers between devices  8.73 us (41%)
  Pallas kernels  5.27 us (25%)
  waiting for transfers between devices  3.81 us (18%)
  local copies, waits for them, and re-layouts  1.75 us (8%)
  other arithmetic  0.7 us (3%)
  between operations  0.68 us (3%)
    ppermute x4, starting transfers between devices, swapped(): return lax.ppermute(cells, axis, route)  8.73 us
    ppermute x4, waiting for transfers between devices, swapped(): return lax.ppermute(cells, axis, route)  3.81 us
    pallas_call x1, Pallas kernels, per_device(): pl.pallas_call(lambda *refs: merge_kernel(cycles, depth, *refs), out_shap...  3.8 us
    pallas_call x1, local copies, waits for them, and re-layouts, per_device(): pl.pallas_call(lambda *refs: merge_kernel(cycles, depth, *refs), out_shap...  1.75 us
    pallas_call x1, Pallas kernels, cell_inputs(): pl.pallas_call(cell_kernel, out_shape=jax.ShapeDtypeStruct((4, arguments[...  1.46 us
    concatenate x1, other arithmetic, per_device(): known = jnp.concatenate([cells, long, short, near], axis=0)  0.7 us
  transfers between devices with their start and end apart: 4, of which 2 were waited for; matrix products, arithmetic and copies ran while one was open for 0% of the time, Pallas kernels for 0%

profile of v2, /device:TPU:0, one launch (start us, length us, event | category | flops | bytes accessed | tf_op | source)
XLA Modules:
  0.0 20.9 jit_solution(15820369630570178392)
XLA Ops:
  0.7 1.5 %cells.1 = f32[4,256]{1,0:T(4,128)} custom-call(s32[2,256]{1,0:T(2,128)} %refs_0_.1, f32[2,256]{1,0:T(2,128)} %refs_1_.1, f32[8]{0:T(128)} %refs_2_.1, f32[8]{0:T(128)} %refs_3_.1, f32[1]{0:T(128)S(6)} %copy.7.refs_4_), custom_call_target="tpu_custom_call" | custom-call | tf_op jit(solution)/shard_map/cells/pallas_call | solution.py:597
  2.1 0.7 %collective-permute-start.2 = (f32[4,256]{1,0:T(4,128)}, f32[4,256]{1,0:T(4,128)S(1)}, u32[]{:S(2)}, u32[]{:S(2)}) collective-permute-start(f32[4,256]{1,0:T(4,128)} %cells.1), channel_id=1, source_target_pairs={{1,2},{2,1},{5,6},{6,5},{9,10},{10,9},{13,14},{14,13},{17,18},{18,... | collective-permute-start | bytes 12296 | tf_op jit(solution)/shard_map/ppermute | solution.py:618
  2.8 3.0 %collective-permute-start.1 = (f32[4,256]{1,0:T(4,128)}, f32[4,256]{1,0:T(4,128)S(1)}, u32[]{:S(2)}, u32[]{:S(2)}) collective-permute-start(f32[4,256]{1,0:T(4,128)} %cells.1), channel_id=1, source_target_pairs={{0,4},{4,0},{8,12},{12,8},{16,20},{20,16},{24,28},{28,24},{1,5},{5... | collective-permute-start | bytes 12296 | tf_op jit(solution)/shard_map/ppermute | solution.py:618
  5.8 3.5 %collective-permute-start = (f32[4,256]{1,0:T(4,128)}, f32[4,256]{1,0:T(4,128)S(1)}, u32[]{:S(2)}, u32[]{:S(2)}) collective-permute-start(f32[4,256]{1,0:T(4,128)} %cells.1), channel_id=1, source_target_pairs={{4,8},{8,4},{12,16},{16,12},{20,24},{24,20},{28,0},{0,28},{5,9},{9... | collective-permute-start | bytes 12296 | tf_op jit(solution)/shard_map/ppermute | solution.py:618
  9.4 0.0 collective-permute-done.2
  9.4 0.0 collective-permute-done.1
  9.4 3.0 %collective-permute-done = f32[4,256]{1,0:T(4,128)S(1)} collective-permute-done((f32[4,256]{1,0:T(4,128)}, f32[4,256]{1,0:T(4,128)S(1)}, u32[]{:S(2)}, u32[]{:S(2)}) %collective-permute-start) | collective-permute-done | bytes 4128 | tf_op jit(solution)/shard_map/ppermute | solution.py:618
  12.3 0.7 %pad_maximum_fusion.refs_0_ = f32[16,256]{1,0:T(8,128)S(1)} fusion(f32[4,256]{1,0:T(4,128)S(1)} %collective-permute-done.2, f32[4,256]{1,0:T(4,128)S(1)} %collective-permute-done.1, f32[4,256]{1,0:T(4,128)S(1)} %collective-permute-done, f32[4,256]{1,0:T(4,128)} %cells.1), kind=kLoop, calls=%fused_computation | loop fusion | flops 12288 | bytes 32768 | tf_op jit(solution)/shard_map/concatenate | solution.py:628
  13.0 1.5 %collective-permute-start.3 = (f32[16,256]{1,0:T(8,128)S(1)}, f32[16,256]{1,0:T(8,128)S(1)}, u32[]{:S(2)}, u32[]{:S(2)}) collective-permute-start(f32[16,256]{1,0:T(8,128)S(1)} %pad_maximum_fusion.refs_0_), channel_id=1, source_target_pairs={{0,1},{1,0},{2,3},{3,2},{4,5},{5,4},{6,7},{7,6},{8,9},{9,8},{10,11... | collective-permute-start | bytes 49160 | tf_op jit(solution)/shard_map/ppermute | solution.py:618
  14.5 0.8 %collective-permute-done.3.refs_1_ = f32[16,256]{1,0:T(8,128)S(1)} collective-permute-done((f32[16,256]{1,0:T(8,128)S(1)}, f32[16,256]{1,0:T(8,128)S(1)}, u32[]{:S(2)}, u32[]{:S(2)}) %collective-permute-start.3) | collective-permute-done | bytes 16416 | tf_op jit(solution)/shard_map/ppermute | solution.py:618
  15.4 3.8 %pair_map.1 = f32[2,260,520]{2,1,0:T(8,128)S(1)} custom-call(f32[16,256]{1,0:T(8,128)S(1)} %pad_maximum_fusion.refs_0_, f32[16,256]{1,0:T(8,128)S(1)} %collective-permute-done.3.refs_1_), custom_call_target="tpu_custom_call" | custom-call | tf_op jit(solution)/shard_map/pair_map/pallas_call | solution.py:630
  19.2 1.7 %copy.6 = f32[2,260,520]{2,0,1:T(2,128)} copy(f32[2,260,520]{2,1,0:T(8,128)S(1)} %pair_map.1) | data formatting | bytes 2163200 | tf_op jit(solution)/shard_map/pair_map/pallas_call | solution.py:630
Async XLA Ops:
  2.1 7.2 %collective-permute-start.2 = (f32[4,256]{1,0:T(4,128)}, f32[4,256]{1,0:T(4,128)S(1)}, u32[]{:S(2)}, u32[]{:S(2)}) collective-permute-start(f32[4,256]{1,0:T(4,128)} %cells.1), channel_id=1, source_target_pairs={{1,2},{2,1},{5,6},{6,5},{9,10},{10,9},{13,14},{14,13},{17,18},{18,... | collective-permute-start | bytes 12296 | tf_op jit(solution)/shard_map/ppermute | solution.py:618
  2.8 6.6 %collective-permute-start.1 = (f32[4,256]{1,0:T(4,128)}, f32[4,256]{1,0:T(4,128)S(1)}, u32[]{:S(2)}, u32[]{:S(2)}) collective-permute-start(f32[4,256]{1,0:T(4,128)} %cells.1), channel_id=1, source_target_pairs={{0,4},{4,0},{8,12},{12,8},{16,20},{20,16},{24,28},{28,24},{1,5},{5... | collective-permute-start | bytes 12296 | tf_op jit(solution)/shard_map/ppermute | solution.py:618
  5.8 6.5 %collective-permute-start = (f32[4,256]{1,0:T(4,128)}, f32[4,256]{1,0:T(4,128)S(1)}, u32[]{:S(2)}, u32[]{:S(2)}) collective-permute-start(f32[4,256]{1,0:T(4,128)} %cells.1), channel_id=1, source_target_pairs={{4,8},{8,4},{12,16},{16,12},{20,24},{24,20},{28,0},{0,28},{5,9},{9... | collective-permute-start | bytes 12296 | tf_op jit(solution)/shard_map/ppermute | solution.py:618
  13.0 2.3 %collective-permute-start.3 = (f32[16,256]{1,0:T(8,128)S(1)}, f32[16,256]{1,0:T(8,128)S(1)}, u32[]{:S(2)}, u32[]{:S(2)}) collective-permute-start(f32[16,256]{1,0:T(8,128)S(1)} %pad_maximum_fusion.refs_0_), channel_id=1, source_target_pairs={{0,1},{1,0},{2,3},{3,2},{4,5},{5,4},{6,7},{7,6},{8,9},{9,8},{10,11... | collective-permute-start | bytes 49160 | tf_op jit(solution)/shard_map/ppermute | solution.py:618

commit v3 on v2

--- a/solution.py
+++ b/solution.py
@@ -519,41 +519,39 @@
         store(part, at, 4, [-value for value in out])
 
 
-def gather_rows(own, partner, is_alpha, is_even, is_first, is_last, main, side):
+def gather_rows(known, block, pair, is_first, is_last, main, side):
+    blocks, cycles = known.shape[:2]
     lane = lax.broadcasted_iota(jnp.int32, (2, LANES), 1)
+    low, high = 2 * pair, 2 * pair + 1
+    under, over = jnp.maximum(low - 1, 0), jnp.minimum(high + 1, cycles - 1)
+    before, after = (block + blocks - 1) % blocks, (block + 1) % blocks
     for field in range(2):
-        at = 2 * field
-        mine, other = own[at : at + 2, :], partner[at : at + 2, :]
-        alpha = jnp.where(is_alpha, mine, other)
-        beta = jnp.where(is_alpha, other, mine)
-        near, far = own[12 + at : 14 + at, :], partner[12 + at : 14 + at, :]
-        main[field, 0:1, :] = jnp.where(is_first, alpha[0:1], jnp.where(is_alpha, near, far)[1:2])
+        rows = slice(2 * field, 2 * field + 2)
+        alpha, beta = known[block, low, rows, :], known[block, high, rows, :]
+        below, above = known[block, under, rows, :], known[block, over, rows, :]
+        main[field, 0:1, :] = jnp.where(is_first, alpha[0:1], below[1:2])
         main[field, 1:3, :] = alpha
         main[field, 3:5, :] = beta
-        main[field, 5:6, :] = jnp.where(is_last, beta[1:2], jnp.where(is_alpha, far, near)[0:1])
+        main[field, 5:6, :] = jnp.where(is_last, beta[1:2], above[0:1])
         main[field, 6:8, :] = beta
         ends = []
-        for tiles in (own, partner):
-            long, short = tiles[4 + at : 6 + at, :], tiles[8 + at : 10 + at, :]
-            left = jnp.where(is_even, long, short)[:, LANES:]
-            right = jnp.where(is_even, short, long)[:, :LANES]
+        for cycle in (low, high):
+            left = known[before, cycle, rows, LANES:]
+            right = known[after, cycle, rows, :LANES]
             ends.append(jnp.where(lane == LANES - 1, left, jnp.where(lane == 0, right, 1.0)))
-        ends_alpha = jnp.where(is_alpha, ends[0], ends[1])
-        ends_beta = jnp.where(is_alpha, ends[1], ends[0])
-        side[field, 0:1, :] = ends_alpha[0:1]
-        side[field, 1:3, :] = ends_alpha
-        side[field, 3:5, :] = ends_beta
-        side[field, 5:7, :] = ends_beta
-        side[field, 7:8, :] = ends_beta[0:1]
-
-
-def merge_kernel(cycles, depth, own, partner, out, main, side):
+        side[field, 0:1, :] = ends[0][0:1]
+        side[field, 1:3, :] = ends[0]
+        side[field, 3:5, :] = ends[1]
+        side[field, 5:7, :] = ends[1]
+        side[field, 7:8, :] = ends[1][0:1]
+
+
+def merge_kernel(cycles, depth, known, out, main, side):
     index = lax.axis_index("rad")
-    is_even = lax.axis_index("az") % 2 == 0
     is_alpha = index % 2 == 0
     is_first = index // 2 == 0
     is_last = index // 2 == cycles // 2 - 1
-    gather_rows(own, partner, is_alpha, is_even, is_first, is_last, main, side)
+    gather_rows(known, lax.axis_index("az"), index // 2, is_first, is_last, main, side)
     top, local, edge = strip(
         (main[0], main[1]),
         (side[0], side[1]),
@@ -608,29 +606,17 @@
     )(*arguments)
 
 
-def swapped(cells, axis, first):
-    count = lax.axis_size(axis)
-    route = []
-    for low in range(first, count, 2):
-        high = (low + 1) % count
-        if high or axis == "az":
-            route += [(low, high), (high, low)]
-    return lax.ppermute(cells, axis, route)
-
-
 def per_device(material_id, thickness, sigma_table, nu_table, angular_frequency):
     depth, arc = thickness.shape
     cells = cell_inputs(material_id, thickness, sigma_table, nu_table, angular_frequency)
     cycles = lax.axis_size("rad")
-    near = swapped(cells, "rad", 1)
-    short = swapped(cells, "az", 0)
-    long = swapped(cells, "az", 1)
-    known = jnp.concatenate([cells, long, short, near], axis=0)
+    known = lax.all_gather(cells, ("az", "rad"))
+    known = known.reshape((lax.axis_size("az"), cycles) + cells.shape)
     outer_nodes = arc + 2 * depth
     return pl.pallas_call(
         lambda *refs: merge_kernel(cycles, depth, *refs),
         out_shape=jax.ShapeDtypeStruct((2, outer_nodes, 2 * outer_nodes), jnp.float32),
-        in_specs=[pl.BlockSpec(memory_space=pltpu.VMEM)] * 2,
+        in_specs=[pl.BlockSpec(memory_space=pltpu.VMEM)],
         out_specs=pl.BlockSpec(memory_space=pltpu.VMEM),
         scratch_shapes=[
             pltpu.VMEM((2, 8, arc), jnp.float32),
@@ -638,7 +624,7 @@
         ],
         compiler_params=pltpu.CompilerParams(vmem_limit_bytes=48 * 1024 * 1024),
         name="pair_map",
-    )(known, swapped(known, "rad", 0))
+    )(known)
 
 
 def solution(mesh):

time: 21.1 us -> 51.7 us (2.45)
  blocking collectives: 0 us -> 43.8 us
  starting transfers between devices: 8.73 us -> 0 us
  waiting for transfers between devices: 3.81 us -> 0 us
  other arithmetic: 0.7 us -> 0 us
    all_gather x0 -> x1, blocking collectives: none -> 43.8 us  [per_device(): known = lax.all_gather(cells, ('az', 'rad'))]
    ppermute x4 -> x0, starting transfers between devices: 8.73 us -> none  [swapped(): return lax.ppermute(cells, axis, route)]
    ppermute x4 -> x0, waiting for transfers between devices: 3.81 us -> none  [swapped(): return lax.ppermute(cells, axis, route)]
    concatenate x1 -> x0, other arithmetic: 0.7 us -> none  [per_device(): known = jnp.concatenate([cells, long, short, near], axis=0)]
  transfers between devices with their start and end apart: 4 -> 0, of which waited for: 2 -> 0; matrix products, arithmetic and copies ran while one was open for 0% -> 0% of each run, Pallas kernels for 0% -> 0%
where the time goes in v3:
time: 51.7 us; the launch traced here: 51.5 us
  blocking collectives  43.8 us (85%)
  Pallas kernels  5.25 us (10%)
  local copies, waits for them, and re-layouts  1.75 us (3%)
  between operations  0.67 us (1%)
    all_gather x1, blocking collectives, per_device(): known = lax.all_gather(cells, ('az', 'rad'))  43.8 us
    pallas_call x1, Pallas kernels, per_device(): pl.pallas_call(lambda *refs: merge_kernel(cycles, depth, *refs), out_shap...  3.79 us
    pallas_call x1, local copies, waits for them, and re-layouts, per_device(): pl.pallas_call(lambda *refs: merge_kernel(cycles, depth, *refs), out_shap...  1.75 us
    pallas_call x1, Pallas kernels, cell_inputs(): pl.pallas_call(cell_kernel, out_shape=jax.ShapeDtypeStruct((4, arguments[...  1.46 us

profile of v3, /device:TPU:0, one launch (start us, length us, event | category | flops | bytes accessed | tf_op | source)
XLA Modules:
  0.0 51.5 jit_solution(11783546005500767463)
XLA Ops:
  0.7 1.5 %cells.1 = f32[4,256]{1,0:T(4,128)} custom-call(s32[2,256]{1,0:T(2,128)} %refs_0_.1, f32[2,256]{1,0:T(2,128)} %refs_1_.1, f32[8]{0:T(128)} %refs_2_.1, f32[8]{0:T(128)} %refs_3_.1, f32[1]{0:T(128)S(6)} %copy.8.refs_4_), custom_call_target="tpu_custom_call" | custom-call | tf_op jit(solution)/shard_map/cells/pallas_call | solution.py:595
  2.1 43.8 %all-gather.1 = f32[32,4,256]{2,1,0:T(4,128)S(1)} all-gather(f32[1,4,256]{2,1,0:T(4,128)} %bitcast.3), channel_id=2, replica_groups=mesh['az'=8,'rad'=4] {'az','rad'}, dimensions={0}, use_global_device_ids=true | all-gather | bytes 135168 | tf_op jit(solution)/shard_map/all_gather | solution.py:613
  45.9 3.8 %pair_map.1 = f32[2,260,520]{2,1,0:T(8,128)S(1)} custom-call(f32[8,4,4,256]{3,2,1,0:T(4,128)S(1)} %bitcast.2), custom_call_target="tpu_custom_call" | custom-call | tf_op jit(solution)/shard_map/pair_map/pallas_call | solution.py:616
  49.7 1.7 %copy.7 = f32[2,260,520]{2,0,1:T(2,128)} copy(f32[2,260,520]{2,1,0:T(8,128)S(1)} %pair_map.1) | data formatting | bytes 2163200 | tf_op jit(solution)/shard_map/pair_map/pallas_call | solution.py:616

commit v4 on v2

--- a/solution.py
+++ b/solution.py
@@ -519,24 +519,24 @@
         store(part, at, 4, [-value for value in out])
 
 
-def gather_rows(own, partner, is_alpha, is_even, is_first, is_last, main, side):
+def gather_rows(angular, own, other, is_alpha, is_even, is_first, is_last, main, side):
     lane = lax.broadcasted_iota(jnp.int32, (2, LANES), 1)
     for field in range(2):
-        at = 2 * field
-        mine, other = own[at : at + 2, :], partner[at : at + 2, :]
-        alpha = jnp.where(is_alpha, mine, other)
-        beta = jnp.where(is_alpha, other, mine)
-        near, far = own[12 + at : 14 + at, :], partner[12 + at : 14 + at, :]
+        scale = angular if field == 0 else 1.0
+        rows = slice(2 * field, 2 * field + 2)
+        (mine, near, short, long), (theirs, far, short_x, long_x) = (
+            [ref[rows, :] * scale for ref in refs] for refs in (own, other)
+        )
+        alpha, beta = jnp.where(is_alpha, mine, theirs), jnp.where(is_alpha, theirs, mine)
         main[field, 0:1, :] = jnp.where(is_first, alpha[0:1], jnp.where(is_alpha, near, far)[1:2])
         main[field, 1:3, :] = alpha
         main[field, 3:5, :] = beta
         main[field, 5:6, :] = jnp.where(is_last, beta[1:2], jnp.where(is_alpha, far, near)[0:1])
         main[field, 6:8, :] = beta
         ends = []
-        for tiles in (own, partner):
-            long, short = tiles[4 + at : 6 + at, :], tiles[8 + at : 10 + at, :]
-            left = jnp.where(is_even, long, short)[:, LANES:]
-            right = jnp.where(is_even, short, long)[:, :LANES]
+        for longs, shorts in ((long, short), (long_x, short_x)):
+            left = jnp.where(is_even, longs, shorts)[:, LANES:]
+            right = jnp.where(is_even, shorts, longs)[:, :LANES]
             ends.append(jnp.where(lane == LANES - 1, left, jnp.where(lane == 0, right, 1.0)))
         ends_alpha = jnp.where(is_alpha, ends[0], ends[1])
         ends_beta = jnp.where(is_alpha, ends[1], ends[0])
@@ -547,13 +547,14 @@
         side[field, 7:8, :] = ends_beta[0:1]
 
 
-def merge_kernel(cycles, depth, own, partner, out, main, side):
+def merge_kernel(cycles, depth, angular, *refs):
+    own, other, (out, main, side) = refs[:4], refs[4:8], refs[8:]
     index = lax.axis_index("rad")
     is_even = lax.axis_index("az") % 2 == 0
     is_alpha = index % 2 == 0
     is_first = index // 2 == 0
     is_last = index // 2 == cycles // 2 - 1
-    gather_rows(own, partner, is_alpha, is_even, is_first, is_last, main, side)
+    gather_rows(angular[0], own, other, is_alpha, is_even, is_first, is_last, main, side)
     top, local, edge = strip(
         (main[0], main[1]),
         (side[0], side[1]),
@@ -573,7 +574,7 @@
 
 
 def cell_kernel(*refs):
-    sources, (out_ref,), targets, sems = refs[:5], refs[5:6], refs[6:11], refs[11]
+    sources, (out_ref,), targets, sems = refs[:4], refs[4:5], refs[5:9], refs[9]
     copies = [
         pltpu.make_async_copy(source, target, sems.at[number])
         for number, (source, target) in enumerate(zip(sources, targets))
@@ -582,28 +583,28 @@
         copy.start()
     for copy in copies:
         copy.wait()
-    material_ref, sheet_ref, sigma_ref, nu_ref, angular_ref = targets
+    material_ref, sheet_ref, sigma_ref, nu_ref = targets
     material, sheet = material_ref[...], sheet_ref[...]
     sigma, base = jnp.zeros_like(sheet), jnp.zeros_like(sheet)
     for level in range(sigma_ref.shape[0]):
         sigma = jnp.where(material == level, sigma_ref[level], sigma)
         base = jnp.where(material == level, nu_ref[level], base)
-    out_ref[:2, :] = angular_ref[0] * sigma * sheet * sheet
+    out_ref[:2, :] = sigma * sheet * sheet
     out_ref[2:, :] = base
 
 
 def cell_inputs(*arguments):
-    spaces = (pltpu.VMEM, pltpu.VMEM, pltpu.SMEM, pltpu.SMEM, pltpu.SMEM)
+    spaces = (pltpu.VMEM, pltpu.VMEM, pltpu.SMEM, pltpu.SMEM)
     return pl.pallas_call(
         cell_kernel,
         out_shape=jax.ShapeDtypeStruct((4, arguments[1].shape[1]), jnp.float32),
-        in_specs=[pl.BlockSpec(memory_space=pltpu.HBM)] * 5,
+        in_specs=[pl.BlockSpec(memory_space=pl.ANY)] * 4,
         out_specs=pl.BlockSpec(memory_space=pltpu.VMEM),
         scratch_shapes=[
             space(value.shape, value.dtype) for space, value in zip(spaces, arguments)
         ]
-        + [pltpu.SemaphoreType.DMA((5,))],
-        compiler_params=pltpu.CompilerParams(vmem_limit_bytes=63 * 1024 * 1024),
+        + [pltpu.SemaphoreType.DMA((4,))],
+        compiler_params=pltpu.CompilerParams(vmem_limit_bytes=40 * 1024 * 1024),
         name="cells",
     )(*arguments)
 
@@ -613,24 +614,23 @@
     route = []
     for low in range(first, count, 2):
         high = (low + 1) % count
-        if high or axis == "az":
-            route += [(low, high), (high, low)]
+        route += [(low, high), (high, low)]
     return lax.ppermute(cells, axis, route)
 
 
 def per_device(material_id, thickness, sigma_table, nu_table, angular_frequency):
     depth, arc = thickness.shape
-    cells = cell_inputs(material_id, thickness, sigma_table, nu_table, angular_frequency)
+    cells = cell_inputs(material_id, thickness, sigma_table, nu_table)
     cycles = lax.axis_size("rad")
-    near = swapped(cells, "rad", 1)
-    short = swapped(cells, "az", 0)
-    long = swapped(cells, "az", 1)
-    known = jnp.concatenate([cells, long, short, near], axis=0)
+    long, short = swapped(cells, "az", 1), swapped(cells, "az", 0)
+    own = [cells, swapped(cells, "rad", 1), short, long]
+    other = [swapped(part, "rad", 0) for part in own]
     outer_nodes = arc + 2 * depth
     return pl.pallas_call(
         lambda *refs: merge_kernel(cycles, depth, *refs),
         out_shape=jax.ShapeDtypeStruct((2, outer_nodes, 2 * outer_nodes), jnp.float32),
-        in_specs=[pl.BlockSpec(memory_space=pltpu.VMEM)] * 2,
+        in_specs=[pl.BlockSpec(memory_space=pltpu.SMEM)]
+        + [pl.BlockSpec(memory_space=pltpu.VMEM)] * 8,
         out_specs=pl.BlockSpec(memory_space=pltpu.VMEM),
         scratch_shapes=[
             pltpu.VMEM((2, 8, arc), jnp.float32),
@@ -638,7 +638,7 @@
         ],
         compiler_params=pltpu.CompilerParams(vmem_limit_bytes=48 * 1024 * 1024),
         name="pair_map",
-    )(known, swapped(known, "rad", 0))
+    )(angular_frequency, *own, *other)
 
 
 def solution(mesh):

time: 21.1 us -> 20 us (0.948)
  local copies, waits for them, and re-layouts: 1.75 us -> 4.42 us
  waiting for transfers between devices: 3.81 us -> 2.14 us
  Pallas kernels: 5.27 us -> 4.4 us
  other arithmetic: 0.7 us -> 0 us
  starting transfers between devices: 8.73 us -> 8.19 us
    unnamed x0 -> x8, local copies, waits for them, and re-layouts: none -> 2.67 us
    ppermute x4 -> x7, waiting for transfers between devices: 3.81 us -> 2.14 us  [swapped(): return lax.ppermute(cells, axis, route)]
    pallas_call x1, Pallas kernels: 1.46 us -> 0.6 us  [cell_inputs(): pl.pallas_call(cell_kernel, out_shape=jax.ShapeDtypeStruct((4, arguments[...]
    concatenate x1 -> x0, other arithmetic: 0.7 us -> none  [per_device(): known = jnp.concatenate([cells, long, short, near], axis=0)]
    ppermute x4 -> x7, starting transfers between devices: 8.73 us -> 8.19 us  [swapped(): return lax.ppermute(cells, axis, route)]
  transfers between devices with their start and end apart: 4 -> 7, of which waited for: 2 -> 2; matrix products, arithmetic and copies ran while one was open for 0% -> 0% of each run, Pallas kernels for 0% -> 0%
where the time goes in v4:
time: 20 us; the launch traced here: 19.9 us
  starting transfers between devices  8.19 us (41%)
  local copies, waits for them, and re-layouts  4.42 us (22%)
  Pallas kernels  4.4 us (22%)
  waiting for transfers between devices  2.14 us (11%)
  between operations  0.7 us (4%)
    ppermute x7, starting transfers between devices, swapped(): return lax.ppermute(cells, axis, route)  8.19 us
    pallas_call x1, Pallas kernels, per_device(): pl.pallas_call(lambda *refs: merge_kernel(cycles, depth, *refs), out_shap...  3.8 us
    unnamed x8, local copies, waits for them, and re-layouts  2.67 us
    ppermute x7, waiting for transfers between devices, swapped(): return lax.ppermute(cells, axis, route)  2.14 us
    pallas_call x1, local copies, waits for them, and re-layouts, per_device(): pl.pallas_call(lambda *refs: merge_kernel(cycles, depth, *refs), out_shap...  1.75 us
    pallas_call x1, Pallas kernels, cell_inputs(): pl.pallas_call(cell_kernel, out_shape=jax.ShapeDtypeStruct((4, arguments[...  0.6 us
  transfers between devices with their start and end apart: 7, of which 2 were waited for; matrix products, arithmetic and copies ran while one was open for 0% of the time, Pallas kernels for 0%

profile of v4, /device:TPU:0, one launch (start us, length us, event | category | flops | bytes accessed | tf_op | source)
XLA Modules:
  0.0 19.9 jit_solution(7212411782537454095)
XLA Ops:
  0.0 0.0 copy-start
  0.0 0.7 %copy-done = s32[2,256]{1,0:T(2,128)S(1)} copy-done((s32[2,256]{1,0:T(2,128)S(1)}, s32[2,256]{1,0:T(2,128)}, u32[]{:S(2)}) %copy-start) | copy-done | bytes 2072
  0.7 0.0 copy-start.1
  0.7 0.7 %copy-done.1 = f32[2,256]{1,0:T(2,128)S(1)} copy-done((f32[2,256]{1,0:T(2,128)S(1)}, f32[2,256]{1,0:T(2,128)}, u32[]{:S(2)}) %copy-start.1) | copy-done | bytes 2072
  1.4 0.0 copy-start.2
  1.4 0.7 %copy-done.2 = f32[8]{0:T(128)S(1)} copy-done((f32[8]{0:T(128)S(1)}, f32[8]{0:T(128)}, u32[]{:S(2)}) %copy-start.2) | copy-done | bytes 56
  2.0 0.7 %copy-done.3 = f32[8]{0:T(128)S(1)} copy-done((f32[8]{0:T(128)S(1)}, f32[8]{0:T(128)}, u32[]{:S(2)}) %copy-start.3) | copy-done | bytes 56
  2.7 0.6 %cells.1.refs_1_ = f32[4,256]{1,0:T(4,128)S(1)} custom-call(s32[2,256]{1,0:T(2,128)S(1)} %copy-done, f32[2,256]{1,0:T(2,128)S(1)} %copy-done.1, f32[8]{0:T(128)S(1)} %copy-done.2, f32[8]{0:T(128)S(1)} %copy-done.3), custom_call_target="tpu_custom_call" | custom-call | tf_op jit(solution)/shard_map/cells/pallas_call | solution.py:598
  3.3 6.1 %collective-permute-start.2 = (f32[4,256]{1,0:T(4,128)S(1)}, f32[4,256]{1,0:T(4,128)S(1)}, u32[]{:S(2)}, u32[]{:S(2)}) collective-permute-start(f32[4,256]{1,0:T(4,128)S(1)} %cells.1.refs_1_), channel_id=1, source_target_pairs={{4,8},{8,4},{12,16},{16,12},{20,24},{24,20},{28,0},{0,28},{5,9},{9... | collective-permute-start | bytes 12296 | tf_op jit(solution)/shard_map/ppermute | solution.py:618
  9.4 0.0 collective-permute-start.1
  9.4 0.7 %collective-permute-start = (f32[4,256]{1,0:T(4,128)S(1)}, f32[4,256]{1,0:T(4,128)S(1)}, u32[]{:S(2)}, u32[]{:S(2)}) collective-permute-start(f32[4,256]{1,0:T(4,128)S(1)} %cells.1.refs_1_), channel_id=1, source_target_pairs={{1,2},{2,1},{3,0},{0,3},{5,6},{6,5},{7,4},{4,7},{9,10},{10,9},{11,... | collective-permute-start | bytes 12296 | tf_op jit(solution)/shard_map/ppermute | solution.py:618
  10.0 1.0 %collective-permute-start.3 = (f32[4,256]{1,0:T(4,128)S(1)}, f32[4,256]{1,0:T(4,128)S(1)}, u32[]{:S(2)}, u32[]{:S(2)}) collective-permute-start(f32[4,256]{1,0:T(4,128)S(1)} %cells.1.refs_1_), channel_id=1, source_target_pairs={{0,1},{1,0},{2,3},{3,2},{4,5},{5,4},{6,7},{7,6},{8,9},{9,8},{10,11... | collective-permute-start | bytes 12296 | tf_op jit(solution)/shard_map/ppermute | solution.py:618
  11.0 0.0 collective-permute-done.2.refs_4_
  11.0 0.0 collective-permute-start.6
  11.0 2.0 %collective-permute-done.1.refs_3_ = f32[4,256]{1,0:T(4,128)S(1)} collective-permute-done((f32[4,256]{1,0:T(4,128)S(1)}, f32[4,256]{1,0:T(4,128)S(1)}, u32[]{:S(2)}, u32[]{:S(2)}) %collective-permute-start.1) | collective-permute-done | bytes 4128 | tf_op jit(solution)/shard_map/ppermute | solution.py:618
  13.0 0.0 collective-permute-start.5
  13.0 0.0 collective-permute-done.refs_2_
  13.0 0.5 %collective-permute-start.4 = (f32[4,256]{1,0:T(4,128)S(1)}, f32[4,256]{1,0:T(4,128)S(1)}, u32[]{:S(2)}, u32[]{:S(2)}) collective-permute-start(f32[4,256]{1,0:T(4,128)S(1)} %collective-permute-done.refs_2_), channel_id=1, source_target_pairs={{0,1},{1,0},{2,3},{3,2},{4,5},{5,4},{6,7},{7,6},{8,9},{9,8},{10,11... | collective-permute-start | bytes 12296 | tf_op jit(solution)/shard_map/ppermute | solution.py:618
  14.1 0.0 collective-permute-done.3.refs_5_
  14.1 0.0 collective-permute-done.6.refs_8_
  14.1 0.0 collective-permute-done.5.refs_7_
  14.2 0.1 collective-permute-done.4.refs_6_
  14.3 3.8 %pair_map.1 = f32[2,260,520]{2,1,0:T(8,128)S(1)} custom-call(f32[1]{0:T(128)S(6)} %copy.7.refs_0_, f32[4,256]{1,0:T(4,128)S(1)} %cells.1.refs_1_, f32[4,256]{1,0:T(4,128)S(1)} %collective-permute-done.refs_2_, f32[4,256]{1,0:T(4,128)S(1)} %collective-permute-done.1.refs_3_, f32[4,256]{1,0:T(4,128)S(1)} %collective-permute-done.2.refs_4_, ...), custom_call_target="tpu_custom_call" | custom-call | tf_op jit(solution)/shard_map/pair_map/pallas_call | solution.py:629
  18.1 1.7 %copy.6 = f32[2,260,520]{2,0,1:T(2,128)} copy(f32[2,260,520]{2,1,0:T(8,128)S(1)} %pair_map.1) | data formatting | bytes 2163200 | tf_op jit(solution)/shard_map/pair_map/pallas_call | solution.py:629
  (1 shorter events, 0.0 us)
Async XLA Ops:
  0.0 0.7 %copy-start = (s32[2,256]{1,0:T(2,128)S(1)}, s32[2,256]{1,0:T(2,128)}, u32[]{:S(2)}) copy-start(s32[2,256]{1,0:T(2,128)} %refs_0_.2) | copy-start | bytes 6148
  0.7 0.7 %copy-start.1 = (f32[2,256]{1,0:T(2,128)S(1)}, f32[2,256]{1,0:T(2,128)}, u32[]{:S(2)}) copy-start(f32[2,256]{1,0:T(2,128)} %refs_1_.1) | copy-start | bytes 6148
  1.4 0.7 %copy-start.2 = (f32[8]{0:T(128)S(1)}, f32[8]{0:T(128)}, u32[]{:S(2)}) copy-start(f32[8]{0:T(128)} %refs_2_.1) | copy-start | bytes 100
  2.0 0.7 %copy-start.3 = (f32[8]{0:T(128)S(1)}, f32[8]{0:T(128)}, u32[]{:S(2)}) copy-start(f32[8]{0:T(128)} %refs_3_.1) | copy-start | bytes 100
  3.3 7.7 %collective-permute-start.2 = (f32[4,256]{1,0:T(4,128)S(1)}, f32[4,256]{1,0:T(4,128)S(1)}, u32[]{:S(2)}, u32[]{:S(2)}) collective-permute-start(f32[4,256]{1,0:T(4,128)S(1)} %cells.1.refs_1_), channel_id=1, source_target_pairs={{4,8},{8,4},{12,16},{16,12},{20,24},{24,20},{28,0},{0,28},{5,9},{9... | collective-permute-start | bytes 12296 | tf_op jit(solution)/shard_map/ppermute | solution.py:618
  9.4 3.6 %collective-permute-start.1 = (f32[4,256]{1,0:T(4,128)S(1)}, f32[4,256]{1,0:T(4,128)S(1)}, u32[]{:S(2)}, u32[]{:S(2)}) collective-permute-start(f32[4,256]{1,0:T(4,128)S(1)} %cells.1.refs_1_), channel_id=1, source_target_pairs={{0,4},{4,0},{8,12},{12,8},{16,20},{20,16},{24,28},{28,24},{1,5},{5... | collective-permute-start | bytes 12296 | tf_op jit(solution)/shard_map/ppermute | solution.py:618
  9.4 3.6 %collective-permute-start = (f32[4,256]{1,0:T(4,128)S(1)}, f32[4,256]{1,0:T(4,128)S(1)}, u32[]{:S(2)}, u32[]{:S(2)}) collective-permute-start(f32[4,256]{1,0:T(4,128)S(1)} %cells.1.refs_1_), channel_id=1, source_target_pairs={{1,2},{2,1},{3,0},{0,3},{5,6},{6,5},{7,4},{4,7},{9,10},{10,9},{11,... | collective-permute-start | bytes 12296 | tf_op jit(solution)/shard_map/ppermute | solution.py:618
  10.0 4.1 %collective-permute-start.3 = (f32[4,256]{1,0:T(4,128)S(1)}, f32[4,256]{1,0:T(4,128)S(1)}, u32[]{:S(2)}, u32[]{:S(2)}) collective-permute-start(f32[4,256]{1,0:T(4,128)S(1)} %cells.1.refs_1_), channel_id=1, source_target_pairs={{0,1},{1,0},{2,3},{3,2},{4,5},{5,4},{6,7},{7,6},{8,9},{9,8},{10,11... | collective-permute-start | bytes 12296 | tf_op jit(solution)/shard_map/ppermute | solution.py:618
  11.0 3.2 %collective-permute-start.6 = (f32[4,256]{1,0:T(4,128)S(1)}, f32[4,256]{1,0:T(4,128)S(1)}, u32[]{:S(2)}, u32[]{:S(2)}) collective-permute-start(f32[4,256]{1,0:T(4,128)S(1)} %collective-permute-done.2.refs_4_), channel_id=1, source_target_pairs={{0,1},{1,0},{2,3},{3,2},{4,5},{5,4},{6,7},{7,6},{8,9},{9,8},{10,11... | collective-permute-start | bytes 12296 | tf_op jit(solution)/shard_map/ppermute | solution.py:618
  13.0 1.2 %collective-permute-start.5 = (f32[4,256]{1,0:T(4,128)S(1)}, f32[4,256]{1,0:T(4,128)S(1)}, u32[]{:S(2)}, u32[]{:S(2)}) collective-permute-start(f32[4,256]{1,0:T(4,128)S(1)} %collective-permute-done.1.refs_3_), channel_id=1, source_target_pairs={{0,1},{1,0},{2,3},{3,2},{4,5},{5,4},{6,7},{7,6},{8,9},{9,8},{10,11... | collective-permute-start | bytes 12296 | tf_op jit(solution)/shard_map/ppermute | solution.py:618
  13.0 1.3 %collective-permute-start.4 = (f32[4,256]{1,0:T(4,128)S(1)}, f32[4,256]{1,0:T(4,128)S(1)}, u32[]{:S(2)}, u32[]{:S(2)}) collective-permute-start(f32[4,256]{1,0:T(4,128)S(1)} %collective-permute-done.refs_2_), channel_id=1, source_target_pairs={{0,1},{1,0},{2,3},{3,2},{4,5},{5,4},{6,7},{7,6},{8,9},{9,8},{10,11... | collective-permute-start | bytes 12296 | tf_op jit(solution)/shard_map/ppermute | solution.py:618

commit v5 on v4

--- a/solution.py
+++ b/solution.py
@@ -519,13 +519,28 @@
         store(part, at, 4, [-value for value in out])
 
 
+def cell_data(ref, angular):
+    value = ref[...]
+    levels = value[:2].astype(jnp.int32)
+    lookups = []
+    for row in (4, 5):
+        table = jnp.broadcast_to(value[row : row + 1, :LANES], (8, LANES))
+        halves = []
+        for half in range(2):
+            index = levels[:, half * LANES : (half + 1) * LANES]
+            index = jnp.concatenate([index] * 4, axis=0)
+            halves.append(lane_take(table, index)[:2])
+        lookups.append(jnp.concatenate(halves, axis=1))
+    sheet = value[2:4]
+    return angular * lookups[0] * sheet * sheet, lookups[1]
+
+
 def gather_rows(angular, own, other, is_alpha, is_even, is_first, is_last, main, side):
     lane = lax.broadcasted_iota(jnp.int32, (2, LANES), 1)
+    own, other = [[cell_data(ref, angular) for ref in refs] for refs in (own, other)]
     for field in range(2):
-        scale = angular if field == 0 else 1.0
-        rows = slice(2 * field, 2 * field + 2)
-        (mine, near, short, long), (theirs, far, short_x, long_x) = (
-            [ref[rows, :] * scale for ref in refs] for refs in (own, other)
+        (mine, near, long, short), (theirs, far, long_x, short_x) = (
+            [data[field] for data in part] for part in (own, other)
         )
         alpha, beta = jnp.where(is_alpha, mine, theirs), jnp.where(is_alpha, theirs, mine)
         main[field, 0:1, :] = jnp.where(is_first, alpha[0:1], jnp.where(is_alpha, near, far)[1:2])
@@ -573,7 +588,7 @@
     finish(top, local, edge, is_alpha, store)
 
 
-def cell_kernel(*refs):
+def pack_kernel(*refs):
     sources, (out_ref,), targets, sems = refs[:4], refs[4:5], refs[5:9], refs[9]
     copies = [
         pltpu.make_async_copy(source, target, sems.at[number])
@@ -584,29 +599,23 @@
     for copy in copies:
         copy.wait()
     material_ref, sheet_ref, sigma_ref, nu_ref = targets
-    material, sheet = material_ref[...], sheet_ref[...]
-    sigma, base = jnp.zeros_like(sheet), jnp.zeros_like(sheet)
-    for level in range(sigma_ref.shape[0]):
-        sigma = jnp.where(material == level, sigma_ref[level], sigma)
-        base = jnp.where(material == level, nu_ref[level], base)
-    out_ref[:2, :] = sigma * sheet * sheet
-    out_ref[2:, :] = base
-
-
-def cell_inputs(*arguments):
-    spaces = (pltpu.VMEM, pltpu.VMEM, pltpu.SMEM, pltpu.SMEM)
+    out_ref[:2, :] = material_ref[...].astype(jnp.float32)
+    out_ref[2:4, :] = sheet_ref[...]
+    for row, ref in ((4, sigma_ref), (5, nu_ref)):
+        out_ref[row : row + 1, : ref.shape[0]] = ref[...].reshape(1, ref.shape[0])
+
+
+def packed(*arguments):
+    held = [pltpu.with_memory_space_constraint(value, pltpu.HBM) for value in arguments]
     return pl.pallas_call(
-        cell_kernel,
-        out_shape=jax.ShapeDtypeStruct((4, arguments[1].shape[1]), jnp.float32),
-        in_specs=[pl.BlockSpec(memory_space=pl.ANY)] * 4,
+        pack_kernel,
+        out_shape=jax.ShapeDtypeStruct((8, arguments[1].shape[1]), jnp.float32),
+        in_specs=[pl.BlockSpec(memory_space=pltpu.HBM)] * 4,
         out_specs=pl.BlockSpec(memory_space=pltpu.VMEM),
-        scratch_shapes=[
-            space(value.shape, value.dtype) for space, value in zip(spaces, arguments)
-        ]
+        scratch_shapes=[pltpu.VMEM(value.shape, value.dtype) for value in arguments]
         + [pltpu.SemaphoreType.DMA((4,))],
-        compiler_params=pltpu.CompilerParams(vmem_limit_bytes=40 * 1024 * 1024),
         name="cells",
-    )(*arguments)
+    )(*held)
 
 
 def swapped(cells, axis, first):
@@ -620,10 +629,9 @@
 
 def per_device(material_id, thickness, sigma_table, nu_table, angular_frequency):
     depth, arc = thickness.shape
-    cells = cell_inputs(material_id, thickness, sigma_table, nu_table)
+    cells = packed(material_id, thickness, sigma_table, nu_table)
     cycles = lax.axis_size("rad")
-    long, short = swapped(cells, "az", 1), swapped(cells, "az", 0)
-    own = [cells, swapped(cells, "rad", 1), short, long]
+    own = [cells, swapped(cells, "rad", 1), swapped(cells, "az", 1), swapped(cells, "az", 0)]
     other = [swapped(part, "rad", 0) for part in own]
     outer_nodes = arc + 2 * depth
     return pl.pallas_call(

time: 20 us -> 19 us (0.950)
  local copies, waits for them, and re-layouts: 4.42 us -> 2.45 us
  Pallas kernels: 4.4 us -> 5.26 us
  starting transfers between devices: 8.19 us -> 8.42 us
    unnamed x8 -> x2, local copies, waits for them, and re-layouts: 2.67 us -> 0.7 us
    pallas_call x1, Pallas kernels: 0.6 us -> 1.34 us  [packed(): pl.pallas_call(pack_kernel, out_shape=jax.ShapeDtypeStruct((8, arguments[...]
    ppermute x7, starting transfers between devices: 8.19 us -> 8.42 us  [swapped(): return lax.ppermute(cells, axis, route)]
  transfers between devices with their start and end apart: 7 -> 7, of which waited for: 2 -> 3; matrix products, arithmetic and copies ran while one was open for 0% -> 0% of each run, Pallas kernels for 0% -> 0%
where the time goes in v5:
time: 19 us; the launch traced here: 18.8 us
  starting transfers between devices  8.42 us (44%)
  Pallas kernels  5.26 us (28%)
  local copies, waits for them, and re-layouts  2.45 us (13%)
  waiting for transfers between devices  1.95 us (10%)
  between operations  0.7 us (4%)
    ppermute x7, starting transfers between devices, swapped(): return lax.ppermute(cells, axis, route)  8.42 us
    pallas_call x1, Pallas kernels, per_device(): pl.pallas_call(lambda *refs: merge_kernel(cycles, depth, *refs), out_shap...  3.92 us
    ppermute x7, waiting for transfers between devices, swapped(): return lax.ppermute(cells, axis, route)  1.95 us
    pallas_call x1, local copies, waits for them, and re-layouts, per_device(): pl.pallas_call(lambda *refs: merge_kernel(cycles, depth, *refs), out_shap...  1.75 us
    pallas_call x1, Pallas kernels, packed(): pl.pallas_call(pack_kernel, out_shape=jax.ShapeDtypeStruct((8, arguments[...  1.34 us
    unnamed x2, local copies, waits for them, and re-layouts  0.7 us
  transfers between devices with their start and end apart: 7, of which 3 were waited for; matrix products, arithmetic and copies ran while one was open for 0% of the time, Pallas kernels for 0%

profile of v5, /device:TPU:0, one launch (start us, length us, event | category | flops | bytes accessed | tf_op | source)
XLA Modules:
  0.0 18.8 jit_solution(7227466481299383285)
XLA Ops:
  0.0 1.3 %cells.1.refs_1_ = f32[8,256]{1,0:T(8,128)} custom-call(s32[2,256]{1,0:T(2,128)} %refs_0_.2, f32[2,256]{1,0:T(2,128)} %refs_1_.1, f32[8]{0:T(128)} %refs_2_.1, f32[8]{0:T(128)} %refs_3_.1), custom_call_target="tpu_custom_call" | custom-call | tf_op jit(solution)/shard_map/cells/pallas_call | solution.py:610
  1.3 3.0 %collective-permute-start.2 = (f32[8,256]{1,0:T(8,128)}, f32[8,256]{1,0:T(8,128)S(1)}, u32[]{:S(2)}, u32[]{:S(2)}) collective-permute-start(f32[8,256]{1,0:T(8,128)} %cells.1.refs_1_), channel_id=1, source_target_pairs={{0,4},{4,0},{8,12},{12,8},{16,20},{20,16},{24,28},{28,24},{1,5},{5... | collective-permute-start | bytes 24584 | tf_op jit(solution)/shard_map/ppermute | solution.py:627
  4.4 3.5 %collective-permute-start.1 = (f32[8,256]{1,0:T(8,128)}, f32[8,256]{1,0:T(8,128)S(1)}, u32[]{:S(2)}, u32[]{:S(2)}) collective-permute-start(f32[8,256]{1,0:T(8,128)} %cells.1.refs_1_), channel_id=1, source_target_pairs={{4,8},{8,4},{12,16},{16,12},{20,24},{24,20},{28,0},{0,28},{5,9},{9... | collective-permute-start | bytes 24584 | tf_op jit(solution)/shard_map/ppermute | solution.py:627
  7.9 0.4 %collective-permute-start = (f32[8,256]{1,0:T(8,128)}, f32[8,256]{1,0:T(8,128)S(1)}, u32[]{:S(2)}, u32[]{:S(2)}) collective-permute-start(f32[8,256]{1,0:T(8,128)} %cells.1.refs_1_), channel_id=1, source_target_pairs={{1,2},{2,1},{3,0},{0,3},{5,6},{6,5},{7,4},{4,7},{9,10},{10,9},{11,... | collective-permute-start | bytes 24584 | tf_op jit(solution)/shard_map/ppermute | solution.py:627
  8.3 1.2 %collective-permute-start.3 = (f32[8,256]{1,0:T(8,128)}, f32[8,256]{1,0:T(8,128)S(1)}, u32[]{:S(2)}, u32[]{:S(2)}) collective-permute-start(f32[8,256]{1,0:T(8,128)} %cells.1.refs_1_), channel_id=1, source_target_pairs={{0,1},{1,0},{2,3},{3,2},{4,5},{5,4},{6,7},{7,6},{8,9},{9,8},{10,11... | collective-permute-start | bytes 24584 | tf_op jit(solution)/shard_map/ppermute | solution.py:627
  9.5 0.0 collective-permute-done.2.refs_4_
  9.5 0.0 collective-permute-start.6
  9.5 1.4 %collective-permute-done.1.refs_3_ = f32[8,256]{1,0:T(8,128)S(1)} collective-permute-done((f32[8,256]{1,0:T(8,128)}, f32[8,256]{1,0:T(8,128)S(1)}, u32[]{:S(2)}, u32[]{:S(2)}) %collective-permute-start.1) | collective-permute-done | bytes 8224 | tf_op jit(solution)/shard_map/ppermute | solution.py:627
  10.9 0.0 collective-permute-start.5
  10.9 0.3 %collective-permute-done.refs_2_ = f32[8,256]{1,0:T(8,128)S(1)} collective-permute-done((f32[8,256]{1,0:T(8,128)}, f32[8,256]{1,0:T(8,128)S(1)}, u32[]{:S(2)}, u32[]{:S(2)}) %collective-permute-start) | collective-permute-done | bytes 8224 | tf_op jit(solution)/shard_map/ppermute | solution.py:627
  11.2 0.2 %collective-permute-start.4 = (f32[8,256]{1,0:T(8,128)S(1)}, f32[8,256]{1,0:T(8,128)S(1)}, u32[]{:S(2)}, u32[]{:S(2)}) collective-permute-start(f32[8,256]{1,0:T(8,128)S(1)} %collective-permute-done.refs_2_), channel_id=1, source_target_pairs={{0,1},{1,0},{2,3},{3,2},{4,5},{5,4},{6,7},{7,6},{8,9},{9,8},{10,11... | collective-permute-start | bytes 24584 | tf_op jit(solution)/shard_map/ppermute | solution.py:627
  12.1 0.0 collective-permute-done.3.refs_5_
  12.1 0.0 collective-permute-done.6.refs_8_
  12.1 0.0 collective-permute-done.5.refs_7_
  12.1 0.3 %collective-permute-done.4.refs_6_ = f32[8,256]{1,0:T(8,128)S(1)} collective-permute-done((f32[8,256]{1,0:T(8,128)S(1)}, f32[8,256]{1,0:T(8,128)S(1)}, u32[]{:S(2)}, u32[]{:S(2)}) %collective-permute-start.4) | collective-permute-done | bytes 8224 | tf_op jit(solution)/shard_map/ppermute | solution.py:627
  12.4 0.0 copy-start
  12.4 0.7 %copy-done = f32[8,256]{1,0:T(8,128)S(1)} copy-done((f32[8,256]{1,0:T(8,128)S(1)}, f32[8,256]{1,0:T(8,128)}, u32[]{:S(2)}) %copy-start) | copy-done | bytes 8216
  13.1 3.9 %pair_map.1 = f32[2,260,520]{2,1,0:T(8,128)S(1)} custom-call(f32[1]{0:T(128)S(6)} %copy.7.refs_0_, f32[8,256]{1,0:T(8,128)S(1)} %copy-done, f32[8,256]{1,0:T(8,128)S(1)} %collective-permute-done.refs_2_, f32[8,256]{1,0:T(8,128)S(1)} %collective-permute-done.1.refs_3_, f32[8,256]{1,0:T(8,128)S(1)} %collective-permute-done.2.refs_4_, ...), custom_call_target="tpu_custom_call" | custom-call | tf_op jit(solution)/shard_map/pair_map/pallas_call | solution.py:637
  17.0 1.7 %copy.6 = f32[2,260,520]{2,0,1:T(2,128)} copy(f32[2,260,520]{2,1,0:T(8,128)S(1)} %pair_map.1) | data formatting | bytes 2163200 | tf_op jit(solution)/shard_map/pair_map/pallas_call | solution.py:637
Async XLA Ops:
  1.3 8.2 %collective-permute-start.2 = (f32[8,256]{1,0:T(8,128)}, f32[8,256]{1,0:T(8,128)S(1)}, u32[]{:S(2)}, u32[]{:S(2)}) collective-permute-start(f32[8,256]{1,0:T(8,128)} %cells.1.refs_1_), channel_id=1, source_target_pairs={{0,4},{4,0},{8,12},{12,8},{16,20},{20,16},{24,28},{28,24},{1,5},{5... | collective-permute-start | bytes 24584 | tf_op jit(solution)/shard_map/ppermute | solution.py:627
  4.4 6.6 %collective-permute-start.1 = (f32[8,256]{1,0:T(8,128)}, f32[8,256]{1,0:T(8,128)S(1)}, u32[]{:S(2)}, u32[]{:S(2)}) collective-permute-start(f32[8,256]{1,0:T(8,128)} %cells.1.refs_1_), channel_id=1, source_target_pairs={{4,8},{8,4},{12,16},{16,12},{20,24},{24,20},{28,0},{0,28},{5,9},{9... | collective-permute-start | bytes 24584 | tf_op jit(solution)/shard_map/ppermute | solution.py:627
  7.9 3.3 %collective-permute-start = (f32[8,256]{1,0:T(8,128)}, f32[8,256]{1,0:T(8,128)S(1)}, u32[]{:S(2)}, u32[]{:S(2)}) collective-permute-start(f32[8,256]{1,0:T(8,128)} %cells.1.refs_1_), channel_id=1, source_target_pairs={{1,2},{2,1},{3,0},{0,3},{5,6},{6,5},{7,4},{4,7},{9,10},{10,9},{11,... | collective-permute-start | bytes 24584 | tf_op jit(solution)/shard_map/ppermute | solution.py:627
  8.3 3.8 %collective-permute-start.3 = (f32[8,256]{1,0:T(8,128)}, f32[8,256]{1,0:T(8,128)S(1)}, u32[]{:S(2)}, u32[]{:S(2)}) collective-permute-start(f32[8,256]{1,0:T(8,128)} %cells.1.refs_1_), channel_id=1, source_target_pairs={{0,1},{1,0},{2,3},{3,2},{4,5},{5,4},{6,7},{7,6},{8,9},{9,8},{10,11... | collective-permute-start | bytes 24584 | tf_op jit(solution)/shard_map/ppermute | solution.py:627
  9.5 2.6 %collective-permute-start.6 = (f32[8,256]{1,0:T(8,128)S(1)}, f32[8,256]{1,0:T(8,128)S(1)}, u32[]{:S(2)}, u32[]{:S(2)}) collective-permute-start(f32[8,256]{1,0:T(8,128)S(1)} %collective-permute-done.2.refs_4_), channel_id=1, source_target_pairs={{0,1},{1,0},{2,3},{3,2},{4,5},{5,4},{6,7},{7,6},{8,9},{9,8},{10,11... | collective-permute-start | bytes 24584 | tf_op jit(solution)/shard_map/ppermute | solution.py:627
  10.9 1.2 %collective-permute-start.5 = (f32[8,256]{1,0:T(8,128)S(1)}, f32[8,256]{1,0:T(8,128)S(1)}, u32[]{:S(2)}, u32[]{:S(2)}) collective-permute-start(f32[8,256]{1,0:T(8,128)S(1)} %collective-permute-done.1.refs_3_), channel_id=1, source_target_pairs={{0,1},{1,0},{2,3},{3,2},{4,5},{5,4},{6,7},{7,6},{8,9},{9,8},{10,11... | collective-permute-start | bytes 24584 | tf_op jit(solution)/shard_map/ppermute | solution.py:627
  11.2 1.2 %collective-permute-start.4 = (f32[8,256]{1,0:T(8,128)S(1)}, f32[8,256]{1,0:T(8,128)S(1)}, u32[]{:S(2)}, u32[]{:S(2)}) collective-permute-start(f32[8,256]{1,0:T(8,128)S(1)} %collective-permute-done.refs_2_), channel_id=1, source_target_pairs={{0,1},{1,0},{2,3},{3,2},{4,5},{5,4},{6,7},{7,6},{8,9},{9,8},{10,11... | collective-permute-start | bytes 24584 | tf_op jit(solution)/shard_map/ppermute | solution.py:627
  12.4 0.7 %copy-start = (f32[8,256]{1,0:T(8,128)S(1)}, f32[8,256]{1,0:T(8,128)}, u32[]{:S(2)}) copy-start(f32[8,256]{1,0:T(8,128)} %cells.1.refs_1_) | copy-start | bytes 24580

commit v6 on v5

--- a/solution.py
+++ b/solution.py
@@ -20,6 +20,10 @@
 
 def lane_take(value, index):
     return jnp.take_along_axis(value, index, axis=1, mode="promise_in_bounds")
+
+
+def sub_take(value, index):
+    return jnp.take_along_axis(value, index, axis=0, mode="promise_in_bounds")
 
 
 def iota(dim):
@@ -494,29 +498,38 @@
 
 def finish(top, local, edge, is_alpha, store):
     lane, sub = iota(1), iota(0)
-    for part, name in enumerate(("re", "im")):
-        full = getattr(top, name)
-        edge_part = getattr(edge, name)
-        for half in range(2):
-            product = getattr(local[half][0], name)
-            on_in = getattr(local[half][1], name)
-            on_out = getattr(local[half][2], name)
-            for row in range(0, LANES, 8):
-                here = lane == sub + row
+    full = [top.re, top.im]
+    for half in range(2):
+        for row in range(0, LANES, 8):
+            here = lane == sub + row
+            at = half * LANES + row
+            both = []
+            for part, name in enumerate(("re", "im")):
+                product, on_in, on_out = [getattr(value, name) for value in local[half]]
                 low = product[row : row + 8, :LANES] + jnp.where(here, on_in, 0.0)
                 high = product[row : row + 8, LANES:] + jnp.where(here, on_out, 0.0)
                 high = lane_roll(high, 4)
-                at = half * LANES + row
-                out = [full[at : at + 8, t * LANES : (t + 1) * LANES] for t in range(5)]
+                out = [full[part][at : at + 8, t * LANES : (t + 1) * LANES] for t in range(5)]
                 out[half] = out[half] + low
                 out[2 + half] = out[2 + half] + jnp.where(lane < 4, 0.0, high)
                 out[3 + half] = out[3 + half] + jnp.where(lane < 4, high, 0.0)
-                store(part, at, 8, [-value for value in out])
-        at = 2 * LANES
-        out = [full[at : at + 8, t * LANES : (t + 1) * LANES] for t in range(5)]
+                both.append([-value for value in out])
+            store(at, 8, both)
+    at = 2 * LANES
+    both = []
+    for part, name in enumerate(("re", "im")):
+        edge_part = getattr(edge, name)
+        out = [full[part][at : at + 8, t * LANES : (t + 1) * LANES] for t in range(5)]
         out[2] = out[2] - jnp.where(is_alpha, edge_part, 0.0)
         out[4] = out[4] - jnp.where(is_alpha, 0.0, lane_roll(edge_part, 4))
-        store(part, at, 4, [-value for value in out])
+        both.append([-value for value in out])
+    store(at, 4, both)
+
+
+def interleaved(first, second, half):
+    sub = iota(0)
+    index = 4 * half + (sub >> 1)
+    return jnp.where((sub & 1) == 0, sub_take(first, index), sub_take(second, index))
 
 
 def cell_data(ref, angular):
@@ -578,12 +591,16 @@
         cycles * depth,
     )
 
-    def store(part, row, count, tiles):
-        for number, tile in enumerate(tiles):
-            width = min(LANES, out.shape[2] - number * LANES)
-            out[part, row : row + count, number * LANES : number * LANES + width] = tile[
-                :count, :width
-            ]
+    def store(row, count, both):
+        for number, (real, imag) in enumerate(zip(*both)):
+            at = number * LANES
+            width = min(LANES, out.shape[2] - at)
+            for half in range(count // 4):
+                tile = interleaved(real, imag, half)
+                first = row + 4 * half
+                out[first : first + 4, :, at : at + width] = tile.reshape(4, 2, LANES)[
+                    :, :, :width
+                ]
 
     finish(top, local, edge, is_alpha, store)
 
@@ -614,6 +631,7 @@
         out_specs=pl.BlockSpec(memory_space=pltpu.VMEM),
         scratch_shapes=[pltpu.VMEM(value.shape, value.dtype) for value in arguments]
         + [pltpu.SemaphoreType.DMA((4,))],
+        compiler_params=pltpu.CompilerParams(vmem_limit_bytes=4 * 1024 * 1024),
         name="cells",
     )(*held)
 
@@ -634,9 +652,9 @@
     own = [cells, swapped(cells, "rad", 1), swapped(cells, "az", 1), swapped(cells, "az", 0)]
     other = [swapped(part, "rad", 0) for part in own]
     outer_nodes = arc + 2 * depth
-    return pl.pallas_call(
+    out = pl.pallas_call(
         lambda *refs: merge_kernel(cycles, depth, *refs),
-        out_shape=jax.ShapeDtypeStruct((2, outer_nodes, 2 * outer_nodes), jnp.float32),
+        out_shape=jax.ShapeDtypeStruct((outer_nodes, 2, 2 * outer_nodes), jnp.float32),
         in_specs=[pl.BlockSpec(memory_space=pltpu.SMEM)]
         + [pl.BlockSpec(memory_space=pltpu.VMEM)] * 8,
         out_specs=pl.BlockSpec(memory_space=pltpu.VMEM),
@@ -647,6 +665,7 @@
         compiler_params=pltpu.CompilerParams(vmem_limit_bytes=48 * 1024 * 1024),
         name="pair_map",
     )(angular_frequency, *own, *other)
+    return jnp.transpose(out, (1, 0, 2))
 
 
 def solution(mesh):

time: 19 us -> 17 us (0.89)
  local copies, waits for them, and re-layouts: 2.45 us -> 0 us
  Pallas kernels: 5.26 us -> 5.92 us
    pallas_call x1 -> x0, local copies, waits for them, and re-layouts: 1.75 us -> none  [per_device(): pl.pallas_call(lambda *refs: merge_kernel(cycles, depth, *refs), out_shap...]
    pallas_call x1, Pallas kernels: 3.92 us -> 5.18 us  [per_device(): pl.pallas_call(lambda *refs: merge_kernel(cycles, depth, *refs), out_shap...]
    unnamed x2 -> x0, local copies, waits for them, and re-layouts: 0.7 us -> none
    pallas_call x1, Pallas kernels: 1.34 us -> 0.74 us  [packed(): pl.pallas_call(pack_kernel, out_shape=jax.ShapeDtypeStruct((8, arguments[...]
where the time goes in v6:
time: 17 us; the launch traced here: 16.8 us
  starting transfers between devices  8.39 us (49%)
  Pallas kernels  5.92 us (35%)
  waiting for transfers between devices  1.81 us (11%)
  between operations  0.69 us (4%)
    ppermute x7, starting transfers between devices, swapped(): return lax.ppermute(cells, axis, route)  8.39 us
    pallas_call x1, Pallas kernels, per_device(): pl.pallas_call(lambda *refs: merge_kernel(cycles, depth, *refs), out_shap...  5.18 us
    ppermute x7, waiting for transfers between devices, swapped(): return lax.ppermute(cells, axis, route)  1.81 us
    pallas_call x1, Pallas kernels, packed(): pl.pallas_call(pack_kernel, out_shape=jax.ShapeDtypeStruct((8, arguments[...  0.74 us
  transfers between devices with their start and end apart: 7, of which 3 were waited for; matrix products, arithmetic and copies ran while one was open for 0% of the time, Pallas kernels for 0%

profile of v6, /device:TPU:0, one launch (start us, length us, event | category | flops | bytes accessed | tf_op | source)
XLA Modules:
  0.0 16.8 jit_solution(10366382731007254805)
XLA Ops:
  0.0 0.7 %cells.1.refs_1_ = f32[8,256]{1,0:T(8,128)S(1)} custom-call(s32[2,256]{1,0:T(2,128)} %refs_0_.2, f32[2,256]{1,0:T(2,128)} %refs_1_.1, f32[8]{0:T(128)} %refs_2_.1, f32[8]{0:T(128)} %refs_3_.1), custom_call_target="tpu_custom_call" | custom-call | tf_op jit(solution)/shard_map/cells/pallas_call | solution.py:627
  0.8 3.0 %collective-permute-start.2 = (f32[8,256]{1,0:T(8,128)S(1)}, f32[8,256]{1,0:T(8,128)S(1)}, u32[]{:S(2)}, u32[]{:S(2)}) collective-permute-start(f32[8,256]{1,0:T(8,128)S(1)} %cells.1.refs_1_), channel_id=1, source_target_pairs={{0,4},{4,0},{8,12},{12,8},{16,20},{20,16},{24,28},{28,24},{1,5},{5... | collective-permute-start | bytes 24584 | tf_op jit(solution)/shard_map/ppermute | solution.py:645
  3.8 3.5 %collective-permute-start.1 = (f32[8,256]{1,0:T(8,128)S(1)}, f32[8,256]{1,0:T(8,128)S(1)}, u32[]{:S(2)}, u32[]{:S(2)}) collective-permute-start(f32[8,256]{1,0:T(8,128)S(1)} %cells.1.refs_1_), channel_id=1, source_target_pairs={{4,8},{8,4},{12,16},{16,12},{20,24},{24,20},{28,0},{0,28},{5,9},{9... | collective-permute-start | bytes 24584 | tf_op jit(solution)/shard_map/ppermute | solution.py:645
  7.3 0.4 %collective-permute-start = (f32[8,256]{1,0:T(8,128)S(1)}, f32[8,256]{1,0:T(8,128)S(1)}, u32[]{:S(2)}, u32[]{:S(2)}) collective-permute-start(f32[8,256]{1,0:T(8,128)S(1)} %cells.1.refs_1_), channel_id=1, source_target_pairs={{1,2},{2,1},{3,0},{0,3},{5,6},{6,5},{7,4},{4,7},{9,10},{10,9},{11,... | collective-permute-start | bytes 24584 | tf_op jit(solution)/shard_map/ppermute | solution.py:645
  7.7 1.2 %collective-permute-start.3 = (f32[8,256]{1,0:T(8,128)S(1)}, f32[8,256]{1,0:T(8,128)S(1)}, u32[]{:S(2)}, u32[]{:S(2)}) collective-permute-start(f32[8,256]{1,0:T(8,128)S(1)} %cells.1.refs_1_), channel_id=1, source_target_pairs={{0,1},{1,0},{2,3},{3,2},{4,5},{5,4},{6,7},{7,6},{8,9},{9,8},{10,11... | collective-permute-start | bytes 24584 | tf_op jit(solution)/shard_map/ppermute | solution.py:645
  8.9 0.0 collective-permute-done.2.refs_4_
  8.9 0.0 collective-permute-start.6
  8.9 1.2 %collective-permute-done.1.refs_3_ = f32[8,256]{1,0:T(8,128)S(1)} collective-permute-done((f32[8,256]{1,0:T(8,128)S(1)}, f32[8,256]{1,0:T(8,128)S(1)}, u32[]{:S(2)}, u32[]{:S(2)}) %collective-permute-start.1) | collective-permute-done | bytes 8224 | tf_op jit(solution)/shard_map/ppermute | solution.py:645
  10.1 0.0 collective-permute-start.5
  10.1 0.3 %collective-permute-done.refs_2_ = f32[8,256]{1,0:T(8,128)S(1)} collective-permute-done((f32[8,256]{1,0:T(8,128)S(1)}, f32[8,256]{1,0:T(8,128)S(1)}, u32[]{:S(2)}, u32[]{:S(2)}) %collective-permute-start) | collective-permute-done | bytes 8224 | tf_op jit(solution)/shard_map/ppermute | solution.py:645
  10.4 0.2 %collective-permute-start.4 = (f32[8,256]{1,0:T(8,128)S(1)}, f32[8,256]{1,0:T(8,128)S(1)}, u32[]{:S(2)}, u32[]{:S(2)}) collective-permute-start(f32[8,256]{1,0:T(8,128)S(1)} %collective-permute-done.refs_2_), channel_id=1, source_target_pairs={{0,1},{1,0},{2,3},{3,2},{4,5},{5,4},{6,7},{7,6},{8,9},{9,8},{10,11... | collective-permute-start | bytes 24584 | tf_op jit(solution)/shard_map/ppermute | solution.py:645
  11.3 0.0 collective-permute-done.3.refs_5_
  11.3 0.0 collective-permute-done.6.refs_8_
  11.3 0.0 collective-permute-done.5.refs_7_
  11.3 0.3 %collective-permute-done.4.refs_6_ = f32[8,256]{1,0:T(8,128)S(1)} collective-permute-done((f32[8,256]{1,0:T(8,128)S(1)}, f32[8,256]{1,0:T(8,128)S(1)}, u32[]{:S(2)}, u32[]{:S(2)}) %collective-permute-start.4) | collective-permute-done | bytes 8224 | tf_op jit(solution)/shard_map/ppermute | solution.py:645
  11.6 5.2 %pair_map.1 = f32[260,2,520]{2,1,0:T(2,128)} custom-call(f32[1]{0:T(128)S(6)} %copy.6.refs_0_, f32[8,256]{1,0:T(8,128)S(1)} %cells.1.refs_1_, f32[8,256]{1,0:T(8,128)S(1)} %collective-permute-done.refs_2_, f32[8,256]{1,0:T(8,128)S(1)} %collective-permute-done.1.refs_3_, f32[8,256]{1,0:T(8,128)S(1)} %collective-permute-done.2.refs_4_, ...), custom_call_target="tpu_custom_call" | custom-call | tf_op jit(solution)/shard_map/pair_map/pallas_call | solution.py:655
Async XLA Ops:
  0.8 8.2 %collective-permute-start.2 = (f32[8,256]{1,0:T(8,128)S(1)}, f32[8,256]{1,0:T(8,128)S(1)}, u32[]{:S(2)}, u32[]{:S(2)}) collective-permute-start(f32[8,256]{1,0:T(8,128)S(1)} %cells.1.refs_1_), channel_id=1, source_target_pairs={{0,4},{4,0},{8,12},{12,8},{16,20},{20,16},{24,28},{28,24},{1,5},{5... | collective-permute-start | bytes 24584 | tf_op jit(solution)/shard_map/ppermute | solution.py:645
  3.8 6.3 %collective-permute-start.1 = (f32[8,256]{1,0:T(8,128)S(1)}, f32[8,256]{1,0:T(8,128)S(1)}, u32[]{:S(2)}, u32[]{:S(2)}) collective-permute-start(f32[8,256]{1,0:T(8,128)S(1)} %cells.1.refs_1_), channel_id=1, source_target_pairs={{4,8},{8,4},{12,16},{16,12},{20,24},{24,20},{28,0},{0,28},{5,9},{9... | collective-permute-start | bytes 24584 | tf_op jit(solution)/shard_map/ppermute | solution.py:645
  7.3 3.1 %collective-permute-start = (f32[8,256]{1,0:T(8,128)S(1)}, f32[8,256]{1,0:T(8,128)S(1)}, u32[]{:S(2)}, u32[]{:S(2)}) collective-permute-start(f32[8,256]{1,0:T(8,128)S(1)} %cells.1.refs_1_), channel_id=1, source_target_pairs={{1,2},{2,1},{3,0},{0,3},{5,6},{6,5},{7,4},{4,7},{9,10},{10,9},{11,... | collective-permute-start | bytes 24584 | tf_op jit(solution)/shard_map/ppermute | solution.py:645
  7.7 3.6 %collective-permute-start.3 = (f32[8,256]{1,0:T(8,128)S(1)}, f32[8,256]{1,0:T(8,128)S(1)}, u32[]{:S(2)}, u32[]{:S(2)}) collective-permute-start(f32[8,256]{1,0:T(8,128)S(1)} %cells.1.refs_1_), channel_id=1, source_target_pairs={{0,1},{1,0},{2,3},{3,2},{4,5},{5,4},{6,7},{7,6},{8,9},{9,8},{10,11... | collective-permute-start | bytes 24584 | tf_op jit(solution)/shard_map/ppermute | solution.py:645
  8.9 2.4 %collective-permute-start.6 = (f32[8,256]{1,0:T(8,128)S(1)}, f32[8,256]{1,0:T(8,128)S(1)}, u32[]{:S(2)}, u32[]{:S(2)}) collective-permute-start(f32[8,256]{1,0:T(8,128)S(1)} %collective-permute-done.2.refs_4_), channel_id=1, source_target_pairs={{0,1},{1,0},{2,3},{3,2},{4,5},{5,4},{6,7},{7,6},{8,9},{9,8},{10,11... | collective-permute-start | bytes 24584 | tf_op jit(solution)/shard_map/ppermute | solution.py:645
  10.1 1.2 %collective-permute-start.5 = (f32[8,256]{1,0:T(8,128)S(1)}, f32[8,256]{1,0:T(8,128)S(1)}, u32[]{:S(2)}, u32[]{:S(2)}) collective-permute-start(f32[8,256]{1,0:T(8,128)S(1)} %collective-permute-done.1.refs_3_), channel_id=1, source_target_pairs={{0,1},{1,0},{2,3},{3,2},{4,5},{5,4},{6,7},{7,6},{8,9},{9,8},{10,11... | collective-permute-start | bytes 24584 | tf_op jit(solution)/shard_map/ppermute | solution.py:645
  10.4 1.2 %collective-permute-start.4 = (f32[8,256]{1,0:T(8,128)S(1)}, f32[8,256]{1,0:T(8,128)S(1)}, u32[]{:S(2)}, u32[]{:S(2)}) collective-permute-start(f32[8,256]{1,0:T(8,128)S(1)} %collective-permute-done.refs_2_), channel_id=1, source_target_pairs={{0,1},{1,0},{2,3},{3,2},{4,5},{5,4},{6,7},{7,6},{8,9},{9,8},{10,11... | collective-permute-start | bytes 24584 | tf_op jit(solution)/shard_map/ppermute | solution.py:645

commit v7 on v6

--- a/solution.py
+++ b/solution.py
@@ -466,8 +466,8 @@
 
     even_d = [inverse_e[0].row(0), inverse_e[0].row(3), inverse_e[3].row(3)]
     even_d = [natural(value, nothing) for value in even_d]
-    local = []
-    for half in range(2):
+
+    def local(half):
         low, high = both(inner, half), both(outer, half)
         own = {key: jnp.where(is_alpha, low[key], high[key]) for key in low}
         every = {key: jnp.concatenate([low[key], high[key]], axis=1) for key in low}
@@ -487,7 +487,8 @@
         on_out = pick(is_alpha, cross, even_d[2][half] * g_out * g_out)
         on_in = pick(solo, on_in, 0.0) - pick(is_alpha, g_in, nothing)
         on_out = pick(solo, on_out, 0.0) - pick(is_alpha, nothing, g_out)
-        local.append((product, on_in, on_out))
+        return product, on_in, on_out
+
     edge = pick((lane == sub) & lower4, pick(is_alpha, gain_corner[0], gain_corner[1]), 0.0)
     return top, local, edge
 
@@ -500,12 +501,13 @@
     lane, sub = iota(1), iota(0)
     full = [top.re, top.im]
     for half in range(2):
+        terms = local(half)
         for row in range(0, LANES, 8):
             here = lane == sub + row
             at = half * LANES + row
             both = []
             for part, name in enumerate(("re", "im")):
-                product, on_in, on_out = [getattr(value, name) for value in local[half]]
+                product, on_in, on_out = [getattr(value, name) for value in terms]
                 low = product[row : row + 8, :LANES] + jnp.where(here, on_in, 0.0)
                 high = product[row : row + 8, LANES:] + jnp.where(here, on_out, 0.0)
                 high = lane_roll(high, 4)
@@ -548,11 +550,11 @@
     return angular * lookups[0] * sheet * sheet, lookups[1]
 
 
-def gather_rows(angular, own, other, is_alpha, is_even, is_first, is_last, main, side):
+def gather_rows(angular, own, other, is_alpha, is_first, is_last, main, side):
     lane = lax.broadcasted_iota(jnp.int32, (2, LANES), 1)
     own, other = [[cell_data(ref, angular) for ref in refs] for refs in (own, other)]
     for field in range(2):
-        (mine, near, long, short), (theirs, far, long_x, short_x) = (
+        (mine, near, after, before), (theirs, far, after_x, before_x) = (
             [data[field] for data in part] for part in (own, other)
         )
         alpha, beta = jnp.where(is_alpha, mine, theirs), jnp.where(is_alpha, theirs, mine)
@@ -562,9 +564,8 @@
         main[field, 5:6, :] = jnp.where(is_last, beta[1:2], jnp.where(is_alpha, far, near)[0:1])
         main[field, 6:8, :] = beta
         ends = []
-        for longs, shorts in ((long, short), (long_x, short_x)):
-            left = jnp.where(is_even, longs, shorts)[:, LANES:]
-            right = jnp.where(is_even, shorts, longs)[:, :LANES]
+        for lefts, rights in ((before, after), (before_x, after_x)):
+            left, right = lefts[:, LANES:], rights[:, :LANES]
             ends.append(jnp.where(lane == LANES - 1, left, jnp.where(lane == 0, right, 1.0)))
         ends_alpha = jnp.where(is_alpha, ends[0], ends[1])
         ends_beta = jnp.where(is_alpha, ends[1], ends[0])
@@ -576,13 +577,12 @@
 
 
 def merge_kernel(cycles, depth, angular, *refs):
-    own, other, (out, main, side) = refs[:4], refs[4:8], refs[8:]
+    own, other, (out, main, side, held, sems) = refs[:4], refs[4:8], refs[8:]
     index = lax.axis_index("rad")
-    is_even = lax.axis_index("az") % 2 == 0
     is_alpha = index % 2 == 0
     is_first = index // 2 == 0
     is_last = index // 2 == cycles // 2 - 1
-    gather_rows(angular[0], own, other, is_alpha, is_even, is_first, is_last, main, side)
+    gather_rows(angular[0], own, other, is_alpha, is_first, is_last, main, side)
     top, local, edge = strip(
         (main[0], main[1]),
         (side[0], side[1]),
@@ -590,6 +590,14 @@
         (index // 2) * (2 * depth),
         cycles * depth,
     )
+    rows = out.shape[0]
+    bounds = [0, 64, 128, 192, rows]
+    copies = [
+        pltpu.make_async_copy(
+            held.at[first : last, :, :], out.at[first : last, :, :], sems.at[number]
+        )
+        for number, (first, last) in enumerate(zip(bounds, bounds[1:]))
+    ]
 
     def store(row, count, both):
         for number, (real, imag) in enumerate(zip(*both)):
@@ -598,11 +606,15 @@
             for half in range(count // 4):
                 tile = interleaved(real, imag, half)
                 first = row + 4 * half
-                out[first : first + 4, :, at : at + width] = tile.reshape(4, 2, LANES)[
+                held[first : first + 4, :, at : at + width] = tile.reshape(4, 2, LANES)[
                     :, :, :width
                 ]
+        if row + count in bounds:
+            copies[bounds.index(row + count) - 1].start()
 
     finish(top, local, edge, is_alpha, store)
+    for copy in copies:
+        copy.wait()
 
 
 def pack_kernel(*refs):
@@ -649,7 +661,10 @@
     depth, arc = thickness.shape
     cells = packed(material_id, thickness, sigma_table, nu_table)
     cycles = lax.axis_size("rad")
-    own = [cells, swapped(cells, "rad", 1), swapped(cells, "az", 1), swapped(cells, "az", 0)]
+    blocks = lax.axis_size("az")
+    before = lax.ppermute(cells, "az", [(i, (i + 1) % blocks) for i in range(blocks)])
+    after = lax.ppermute(cells, "az", [((i + 1) % blocks, i) for i in range(blocks)])
+    own = [cells, swapped(cells, "rad", 1), after, before]
     other = [swapped(part, "rad", 0) for part in own]
     outer_nodes = arc + 2 * depth
     out = pl.pallas_call(
@@ -657,10 +672,12 @@
         out_shape=jax.ShapeDtypeStruct((outer_nodes, 2, 2 * outer_nodes), jnp.float32),
         in_specs=[pl.BlockSpec(memory_space=pltpu.SMEM)]
         + [pl.BlockSpec(memory_space=pltpu.VMEM)] * 8,
-        out_specs=pl.BlockSpec(memory_space=pltpu.VMEM),
+        out_specs=pl.BlockSpec(memory_space=pltpu.HBM),
         scratch_shapes=[
             pltpu.VMEM((2, 8, arc), jnp.float32),
             pltpu.VMEM((2, 8, LANES), jnp.float32),
+            pltpu.VMEM((outer_nodes, 2, 2 * outer_nodes), jnp.float32),
+            pltpu.SemaphoreType.DMA((4,)),
         ],
         compiler_params=pltpu.CompilerParams(vmem_limit_bytes=48 * 1024 * 1024),
         name="pair_map",

time: 17 us -> 16.3 us (0.959)
  waiting for transfers between devices: 1.81 us -> 1.24 us
  Pallas kernels: 5.92 us -> 5.7 us
    ppermute x0 -> x2, starting transfers between devices: none -> 6.12 us  [the longest x1 3.1 us: per_device(): lax.ppermute(cells, 'az', [((i + 1) % blocks, i) for i in range(blocks)])]
    ppermute x7 -> x5, starting transfers between devices: 8.39 us -> 2.33 us  [swapped(): return lax.ppermute(cells, axis, route)]
    ppermute x7 -> x5, waiting for transfers between devices: 1.81 us -> 1.23 us  [swapped(): return lax.ppermute(cells, axis, route)]
    pallas_call x1, Pallas kernels: 5.18 us -> 4.96 us  [per_device(): pl.pallas_call(lambda *refs: merge_kernel(cycles, depth, *refs), out_shap...]
  transfers between devices with their start and end apart: 7 -> 7, of which waited for: 3 -> 2; matrix products, arithmetic and copies ran while one was open for 0% -> 0% of each run, Pallas kernels for 0% -> 0%
where the time goes in v7:
time: 16.3 us; the launch traced here: 16.1 us
  starting transfers between devices  8.45 us (52%)
  Pallas kernels  5.7 us (35%)
  waiting for transfers between devices  1.24 us (8%)
  between operations  0.69 us (4%)
    pallas_call x1, Pallas kernels, per_device(): pl.pallas_call(lambda *refs: merge_kernel(cycles, depth, *refs), out_shap...  4.96 us
    ppermute x1, starting transfers between devices, per_device(): lax.ppermute(cells, 'az', [((i + 1) % blocks, i) for i in range(blocks)])  3.1 us
    ppermute x1, starting transfers between devices, per_device(): lax.ppermute(cells, 'az', [(i, (i + 1) % blocks) for i in range(blocks)])  3.02 us
    ppermute x5, starting transfers between devices, swapped(): return lax.ppermute(cells, axis, route)  2.33 us
    ppermute x5, waiting for transfers between devices, swapped(): return lax.ppermute(cells, axis, route)  1.23 us
    pallas_call x1, Pallas kernels, packed(): pl.pallas_call(pack_kernel, out_shape=jax.ShapeDtypeStruct((8, arguments[...  0.74 us
  transfers between devices with their start and end apart: 7, of which 2 were waited for; matrix products, arithmetic and copies ran while one was open for 0% of the time, Pallas kernels for 0%

profile of v7, /device:TPU:0, one launch (start us, length us, event | category | flops | bytes accessed | tf_op | source)
XLA Modules:
  0.0 16.1 jit_solution(1235486463281430924)
XLA Ops:
  0.0 0.7 %cells.1.refs_1_ = f32[8,256]{1,0:T(8,128)S(1)} custom-call(s32[2,256]{1,0:T(2,128)} %refs_0_.2, f32[2,256]{1,0:T(2,128)} %refs_1_.1, f32[8]{0:T(128)} %refs_2_.1, f32[8]{0:T(128)} %refs_3_.1), custom_call_target="tpu_custom_call" | custom-call | tf_op jit(solution)/shard_map/cells/pallas_call | solution.py:639
  0.8 3.0 %collective-permute-start.2 = (f32[8,256]{1,0:T(8,128)S(1)}, f32[8,256]{1,0:T(8,128)S(1)}, u32[]{:S(2)}, u32[]{:S(2)}) collective-permute-start(f32[8,256]{1,0:T(8,128)S(1)} %cells.1.refs_1_), channel_id=1, source_target_pairs={{0,4},{4,8},{8,12},{12,16},{16,20},{20,24},{24,28},{28,0},{1,5},{5... | collective-permute-start | bytes 24584 | tf_op jit(solution)/shard_map/ppermute | solution.py:665
  3.8 3.1 %collective-permute-start.1 = (f32[8,256]{1,0:T(8,128)S(1)}, f32[8,256]{1,0:T(8,128)S(1)}, u32[]{:S(2)}, u32[]{:S(2)}) collective-permute-start(f32[8,256]{1,0:T(8,128)S(1)} %cells.1.refs_1_), channel_id=1, source_target_pairs={{4,0},{8,4},{12,8},{16,12},{20,16},{24,20},{28,24},{0,28},{5,1},{9... | collective-permute-start | bytes 24584 | tf_op jit(solution)/shard_map/ppermute | solution.py:666
  6.9 0.7 %collective-permute-start = (f32[8,256]{1,0:T(8,128)S(1)}, f32[8,256]{1,0:T(8,128)S(1)}, u32[]{:S(2)}, u32[]{:S(2)}) collective-permute-start(f32[8,256]{1,0:T(8,128)S(1)} %cells.1.refs_1_), channel_id=1, source_target_pairs={{1,2},{2,1},{3,0},{0,3},{5,6},{6,5},{7,4},{4,7},{9,10},{10,9},{11,... | collective-permute-start | bytes 24584 | tf_op jit(solution)/shard_map/ppermute | solution.py:657
  7.5 1.1 %collective-permute-start.3 = (f32[8,256]{1,0:T(8,128)S(1)}, f32[8,256]{1,0:T(8,128)S(1)}, u32[]{:S(2)}, u32[]{:S(2)}) collective-permute-start(f32[8,256]{1,0:T(8,128)S(1)} %cells.1.refs_1_), channel_id=1, source_target_pairs={{0,1},{1,0},{2,3},{3,2},{4,5},{5,4},{6,7},{7,6},{8,9},{9,8},{10,11... | collective-permute-start | bytes 24584 | tf_op jit(solution)/shard_map/ppermute | solution.py:657
  8.6 0.0 collective-permute-done.2.refs_4_
  8.6 0.0 collective-permute-start.6
  8.6 0.0 collective-permute-done.1.refs_3_
  8.6 0.5 %collective-permute-start.5 = (f32[8,256]{1,0:T(8,128)S(1)}, f32[8,256]{1,0:T(8,128)S(1)}, u32[]{:S(2)}, u32[]{:S(2)}) collective-permute-start(f32[8,256]{1,0:T(8,128)S(1)} %collective-permute-done.1.refs_3_), channel_id=1, source_target_pairs={{0,1},{1,0},{2,3},{3,2},{4,5},{5,4},{6,7},{7,6},{8,9},{9,8},{10,11... | collective-permute-start | bytes 24584 | tf_op jit(solution)/shard_map/ppermute | solution.py:657
  9.1 0.9 %collective-permute-done.refs_2_ = f32[8,256]{1,0:T(8,128)S(1)} collective-permute-done((f32[8,256]{1,0:T(8,128)S(1)}, f32[8,256]{1,0:T(8,128)S(1)}, u32[]{:S(2)}, u32[]{:S(2)}) %collective-permute-start) | collective-permute-done | bytes 8224 | tf_op jit(solution)/shard_map/ppermute | solution.py:657
  10.0 0.1 collective-permute-start.4
  10.7 0.0 collective-permute-done.3.refs_5_
  10.7 0.0 collective-permute-done.6.refs_8_
  10.7 0.0 collective-permute-done.5.refs_7_
  10.8 0.4 %collective-permute-done.4.refs_6_ = f32[8,256]{1,0:T(8,128)S(1)} collective-permute-done((f32[8,256]{1,0:T(8,128)S(1)}, f32[8,256]{1,0:T(8,128)S(1)}, u32[]{:S(2)}, u32[]{:S(2)}) %collective-permute-start.4) | collective-permute-done | bytes 8224 | tf_op jit(solution)/shard_map/ppermute | solution.py:657
  11.1 5.0 %pair_map.1 = f32[260,2,520]{2,1,0:T(2,128)} custom-call(f32[1]{0:T(128)S(6)} %copy.6.refs_0_, f32[8,256]{1,0:T(8,128)S(1)} %cells.1.refs_1_, f32[8,256]{1,0:T(8,128)S(1)} %collective-permute-done.refs_2_, f32[8,256]{1,0:T(8,128)S(1)} %collective-permute-done.1.refs_3_, f32[8,256]{1,0:T(8,128)S(1)} %collective-permute-done.2.refs_4_, ...), custom_call_target="tpu_custom_call" | custom-call | tf_op jit(solution)/shard_map/pair_map/pallas_call | solution.py:670
Async XLA Ops:
  0.8 7.8 %collective-permute-start.2 = (f32[8,256]{1,0:T(8,128)S(1)}, f32[8,256]{1,0:T(8,128)S(1)}, u32[]{:S(2)}, u32[]{:S(2)}) collective-permute-start(f32[8,256]{1,0:T(8,128)S(1)} %cells.1.refs_1_), channel_id=1, source_target_pairs={{0,4},{4,8},{8,12},{12,16},{16,20},{20,24},{24,28},{28,0},{1,5},{5... | collective-permute-start | bytes 24584 | tf_op jit(solution)/shard_map/ppermute | solution.py:665
  3.8 4.8 %collective-permute-start.1 = (f32[8,256]{1,0:T(8,128)S(1)}, f32[8,256]{1,0:T(8,128)S(1)}, u32[]{:S(2)}, u32[]{:S(2)}) collective-permute-start(f32[8,256]{1,0:T(8,128)S(1)} %cells.1.refs_1_), channel_id=1, source_target_pairs={{4,0},{8,4},{12,8},{16,12},{20,16},{24,20},{28,24},{0,28},{5,1},{9... | collective-permute-start | bytes 24584 | tf_op jit(solution)/shard_map/ppermute | solution.py:666
  6.9 3.1 %collective-permute-start = (f32[8,256]{1,0:T(8,128)S(1)}, f32[8,256]{1,0:T(8,128)S(1)}, u32[]{:S(2)}, u32[]{:S(2)}) collective-permute-start(f32[8,256]{1,0:T(8,128)S(1)} %cells.1.refs_1_), channel_id=1, source_target_pairs={{1,2},{2,1},{3,0},{0,3},{5,6},{6,5},{7,4},{4,7},{9,10},{10,9},{11,... | collective-permute-start | bytes 24584 | tf_op jit(solution)/shard_map/ppermute | solution.py:657
  7.5 3.2 %collective-permute-start.3 = (f32[8,256]{1,0:T(8,128)S(1)}, f32[8,256]{1,0:T(8,128)S(1)}, u32[]{:S(2)}, u32[]{:S(2)}) collective-permute-start(f32[8,256]{1,0:T(8,128)S(1)} %cells.1.refs_1_), channel_id=1, source_target_pairs={{0,1},{1,0},{2,3},{3,2},{4,5},{5,4},{6,7},{7,6},{8,9},{9,8},{10,11... | collective-permute-start | bytes 24584 | tf_op jit(solution)/shard_map/ppermute | solution.py:657
  8.6 2.1 %collective-permute-start.6 = (f32[8,256]{1,0:T(8,128)S(1)}, f32[8,256]{1,0:T(8,128)S(1)}, u32[]{:S(2)}, u32[]{:S(2)}) collective-permute-start(f32[8,256]{1,0:T(8,128)S(1)} %collective-permute-done.2.refs_4_), channel_id=1, source_target_pairs={{0,1},{1,0},{2,3},{3,2},{4,5},{5,4},{6,7},{7,6},{8,9},{9,8},{10,11... | collective-permute-start | bytes 24584 | tf_op jit(solution)/shard_map/ppermute | solution.py:657
  8.6 2.1 %collective-permute-start.5 = (f32[8,256]{1,0:T(8,128)S(1)}, f32[8,256]{1,0:T(8,128)S(1)}, u32[]{:S(2)}, u32[]{:S(2)}) collective-permute-start(f32[8,256]{1,0:T(8,128)S(1)} %collective-permute-done.1.refs_3_), channel_id=1, source_target_pairs={{0,1},{1,0},{2,3},{3,2},{4,5},{5,4},{6,7},{7,6},{8,9},{9,8},{10,11... | collective-permute-start | bytes 24584 | tf_op jit(solution)/shard_map/ppermute | solution.py:657
  10.0 1.2 %collective-permute-start.4 = (f32[8,256]{1,0:T(8,128)S(1)}, f32[8,256]{1,0:T(8,128)S(1)}, u32[]{:S(2)}, u32[]{:S(2)}) collective-permute-start(f32[8,256]{1,0:T(8,128)S(1)} %collective-permute-done.refs_2_), channel_id=1, source_target_pairs={{0,1},{1,0},{2,3},{3,2},{4,5},{5,4},{6,7},{7,6},{8,9},{9,8},{10,11... | collective-permute-start | bytes 24584 | tf_op jit(solution)/shard_map/ppermute | solution.py:657

commit v8 on v7

--- a/solution.py
+++ b/solution.py
@@ -554,7 +554,7 @@
     lane = lax.broadcasted_iota(jnp.int32, (2, LANES), 1)
     own, other = [[cell_data(ref, angular) for ref in refs] for refs in (own, other)]
     for field in range(2):
-        (mine, near, after, before), (theirs, far, after_x, before_x) = (
+        (mine, after, near, before), (theirs, after_x, far, before_x) = (
             [data[field] for data in part] for part in (own, other)
         )
         alpha, beta = jnp.where(is_alpha, mine, theirs), jnp.where(is_alpha, theirs, mine)
@@ -664,7 +664,7 @@
     blocks = lax.axis_size("az")
     before = lax.ppermute(cells, "az", [(i, (i + 1) % blocks) for i in range(blocks)])
     after = lax.ppermute(cells, "az", [((i + 1) % blocks, i) for i in range(blocks)])
-    own = [cells, swapped(cells, "rad", 1), after, before]
+    own = [cells, after, swapped(cells, "rad", 1), before]
     other = [swapped(part, "rad", 0) for part in own]
     outer_nodes = arc + 2 * depth
     out = pl.pallas_call(

time: 16.3 us -> 15.5 us (0.951)
  starting transfers between devices: 8.45 us -> 8.06 us
  waiting for transfers between devices: 1.24 us -> 0.87 us
    ppermute x5, waiting for transfers between devices: 1.23 us -> 0.5 us  [swapped(): return lax.ppermute(cells, axis, route)]
    ppermute x5, starting transfers between devices: 2.33 us -> 1.65 us  [swapped(): return lax.ppermute(cells, axis, route)]
    ppermute x1, starting transfers between devices: 3.1 us -> 3.4 us  [per_device(): lax.ppermute(cells, 'az', [((i + 1) % blocks, i) for i in range(blocks)])]
    ppermute x1, waiting for transfers between devices: 0.01 us -> 0.23 us  [per_device(): lax.ppermute(cells, 'az', [((i + 1) % blocks, i) for i in range(blocks)])]
  transfers between devices with their start and end apart: 7 -> 7, of which waited for: 2 -> 3; matrix products, arithmetic and copies ran while one was open for 0% -> 0% of each run, Pallas kernels for 0% -> 0%
where the time goes in v8:
time: 15.5 us; the launch traced here: 15.3 us
  starting transfers between devices  8.06 us (52%)
  Pallas kernels  5.7 us (37%)
  waiting for transfers between devices  0.87 us (6%)
  between operations  0.69 us (4%)
    pallas_call x1, Pallas kernels, per_device(): pl.pallas_call(lambda *refs: merge_kernel(cycles, depth, *refs), out_shap...  4.96 us
    ppermute x1, starting transfers between devices, per_device(): lax.ppermute(cells, 'az', [((i + 1) % blocks, i) for i in range(blocks)])  3.4 us
    ppermute x1, starting transfers between devices, per_device(): lax.ppermute(cells, 'az', [(i, (i + 1) % blocks) for i in range(blocks)])  3.02 us
    ppermute x5, starting transfers between devices, swapped(): return lax.ppermute(cells, axis, route)  1.65 us
    pallas_call x1, Pallas kernels, packed(): pl.pallas_call(pack_kernel, out_shape=jax.ShapeDtypeStruct((8, arguments[...  0.74 us
    ppermute x5, waiting for transfers between devices, swapped(): return lax.ppermute(cells, axis, route)  0.5 us
  transfers between devices with their start and end apart: 7, of which 3 were waited for; matrix products, arithmetic and copies ran while one was open for 0% of the time, Pallas kernels for 0%

profile of v8, /device:TPU:0, one launch (start us, length us, event | category | flops | bytes accessed | tf_op | source)
XLA Modules:
  0.0 15.3 jit_solution(16397559854493549728)
XLA Ops:
  0.0 0.7 %cells.1.refs_1_ = f32[8,256]{1,0:T(8,128)S(1)} custom-call(s32[2,256]{1,0:T(2,128)} %refs_0_.2, f32[2,256]{1,0:T(2,128)} %refs_1_.1, f32[8]{0:T(128)} %refs_2_.1, f32[8]{0:T(128)} %refs_3_.1), custom_call_target="tpu_custom_call" | custom-call | tf_op jit(solution)/shard_map/cells/pallas_call | solution.py:639
  0.8 3.0 %collective-permute-start.2 = (f32[8,256]{1,0:T(8,128)S(1)}, f32[8,256]{1,0:T(8,128)S(1)}, u32[]{:S(2)}, u32[]{:S(2)}) collective-permute-start(f32[8,256]{1,0:T(8,128)S(1)} %cells.1.refs_1_), channel_id=1, source_target_pairs={{0,4},{4,8},{8,12},{12,16},{16,20},{20,24},{24,28},{28,0},{1,5},{5... | collective-permute-start | bytes 24584 | tf_op jit(solution)/shard_map/ppermute | solution.py:665
  3.8 0.7 %collective-permute-start.1 = (f32[8,256]{1,0:T(8,128)S(1)}, f32[8,256]{1,0:T(8,128)S(1)}, u32[]{:S(2)}, u32[]{:S(2)}) collective-permute-start(f32[8,256]{1,0:T(8,128)S(1)} %cells.1.refs_1_), channel_id=1, source_target_pairs={{1,2},{2,1},{3,0},{0,3},{5,6},{6,5},{7,4},{4,7},{9,10},{10,9},{11,... | collective-permute-start | bytes 24584 | tf_op jit(solution)/shard_map/ppermute | solution.py:657
  4.4 3.4 %collective-permute-start = (f32[8,256]{1,0:T(8,128)S(1)}, f32[8,256]{1,0:T(8,128)S(1)}, u32[]{:S(2)}, u32[]{:S(2)}) collective-permute-start(f32[8,256]{1,0:T(8,128)S(1)} %cells.1.refs_1_), channel_id=1, source_target_pairs={{4,0},{8,4},{12,8},{16,12},{20,16},{24,20},{28,24},{0,28},{5,1},{9... | collective-permute-start | bytes 24584 | tf_op jit(solution)/shard_map/ppermute | solution.py:666
  7.8 0.5 %collective-permute-start.3 = (f32[8,256]{1,0:T(8,128)S(1)}, f32[8,256]{1,0:T(8,128)S(1)}, u32[]{:S(2)}, u32[]{:S(2)}) collective-permute-start(f32[8,256]{1,0:T(8,128)S(1)} %cells.1.refs_1_), channel_id=1, source_target_pairs={{0,1},{1,0},{2,3},{3,2},{4,5},{5,4},{6,7},{7,6},{8,9},{9,8},{10,11... | collective-permute-start | bytes 24584 | tf_op jit(solution)/shard_map/ppermute | solution.py:657
  8.3 0.1 collective-permute-done.2.refs_4_
  8.4 0.0 collective-permute-start.6
  8.4 0.0 collective-permute-done.1.refs_3_
  8.4 0.5 %collective-permute-start.5 = (f32[8,256]{1,0:T(8,128)S(1)}, f32[8,256]{1,0:T(8,128)S(1)}, u32[]{:S(2)}, u32[]{:S(2)}) collective-permute-start(f32[8,256]{1,0:T(8,128)S(1)} %collective-permute-done.1.refs_3_), channel_id=1, source_target_pairs={{0,1},{1,0},{2,3},{3,2},{4,5},{5,4},{6,7},{7,6},{8,9},{9,8},{10,11... | collective-permute-start | bytes 24584 | tf_op jit(solution)/shard_map/ppermute | solution.py:657
  9.0 0.2 %collective-permute-done.refs_2_ = f32[8,256]{1,0:T(8,128)S(1)} collective-permute-done((f32[8,256]{1,0:T(8,128)S(1)}, f32[8,256]{1,0:T(8,128)S(1)}, u32[]{:S(2)}, u32[]{:S(2)}) %collective-permute-start) | collective-permute-done | bytes 8224 | tf_op jit(solution)/shard_map/ppermute | solution.py:666
  9.2 0.0 collective-permute-start.4
  9.8 0.0 collective-permute-done.3.refs_5_
  9.9 0.0 collective-permute-done.6.refs_8_
  9.9 0.0 collective-permute-done.5.refs_7_
  9.9 0.5 %collective-permute-done.4.refs_6_ = f32[8,256]{1,0:T(8,128)S(1)} collective-permute-done((f32[8,256]{1,0:T(8,128)S(1)}, f32[8,256]{1,0:T(8,128)S(1)}, u32[]{:S(2)}, u32[]{:S(2)}) %collective-permute-start.4) | collective-permute-done | bytes 8224 | tf_op jit(solution)/shard_map/ppermute | solution.py:657
  10.4 5.0 %pair_map.1 = f32[260,2,520]{2,1,0:T(2,128)} custom-call(f32[1]{0:T(128)S(6)} %copy.6.refs_0_, f32[8,256]{1,0:T(8,128)S(1)} %cells.1.refs_1_, f32[8,256]{1,0:T(8,128)S(1)} %collective-permute-done.refs_2_, f32[8,256]{1,0:T(8,128)S(1)} %collective-permute-done.1.refs_3_, f32[8,256]{1,0:T(8,128)S(1)} %collective-permute-done.2.refs_4_, ...), custom_call_target="tpu_custom_call" | custom-call | tf_op jit(solution)/shard_map/pair_map/pallas_call | solution.py:670
Async XLA Ops:
  0.8 7.7 %collective-permute-start.2 = (f32[8,256]{1,0:T(8,128)S(1)}, f32[8,256]{1,0:T(8,128)S(1)}, u32[]{:S(2)}, u32[]{:S(2)}) collective-permute-start(f32[8,256]{1,0:T(8,128)S(1)} %cells.1.refs_1_), channel_id=1, source_target_pairs={{0,4},{4,8},{8,12},{12,16},{16,20},{20,24},{24,28},{28,0},{1,5},{5... | collective-permute-start | bytes 24584 | tf_op jit(solution)/shard_map/ppermute | solution.py:665
  3.8 4.7 %collective-permute-start.1 = (f32[8,256]{1,0:T(8,128)S(1)}, f32[8,256]{1,0:T(8,128)S(1)}, u32[]{:S(2)}, u32[]{:S(2)}) collective-permute-start(f32[8,256]{1,0:T(8,128)S(1)} %cells.1.refs_1_), channel_id=1, source_target_pairs={{1,2},{2,1},{3,0},{0,3},{5,6},{6,5},{7,4},{4,7},{9,10},{10,9},{11,... | collective-permute-start | bytes 24584 | tf_op jit(solution)/shard_map/ppermute | solution.py:657
  4.4 4.8 %collective-permute-start = (f32[8,256]{1,0:T(8,128)S(1)}, f32[8,256]{1,0:T(8,128)S(1)}, u32[]{:S(2)}, u32[]{:S(2)}) collective-permute-start(f32[8,256]{1,0:T(8,128)S(1)} %cells.1.refs_1_), channel_id=1, source_target_pairs={{4,0},{8,4},{12,8},{16,12},{20,16},{24,20},{28,24},{0,28},{5,1},{9... | collective-permute-start | bytes 24584 | tf_op jit(solution)/shard_map/ppermute | solution.py:666
  7.8 2.0 %collective-permute-start.3 = (f32[8,256]{1,0:T(8,128)S(1)}, f32[8,256]{1,0:T(8,128)S(1)}, u32[]{:S(2)}, u32[]{:S(2)}) collective-permute-start(f32[8,256]{1,0:T(8,128)S(1)} %cells.1.refs_1_), channel_id=1, source_target_pairs={{0,1},{1,0},{2,3},{3,2},{4,5},{5,4},{6,7},{7,6},{8,9},{9,8},{10,11... | collective-permute-start | bytes 24584 | tf_op jit(solution)/shard_map/ppermute | solution.py:657
  8.4 1.4 %collective-permute-start.6 = (f32[8,256]{1,0:T(8,128)S(1)}, f32[8,256]{1,0:T(8,128)S(1)}, u32[]{:S(2)}, u32[]{:S(2)}) collective-permute-start(f32[8,256]{1,0:T(8,128)S(1)} %collective-permute-done.2.refs_4_), channel_id=1, source_target_pairs={{0,1},{1,0},{2,3},{3,2},{4,5},{5,4},{6,7},{7,6},{8,9},{9,8},{10,11... | collective-permute-start | bytes 24584 | tf_op jit(solution)/shard_map/ppermute | solution.py:657
  8.4 1.4 %collective-permute-start.5 = (f32[8,256]{1,0:T(8,128)S(1)}, f32[8,256]{1,0:T(8,128)S(1)}, u32[]{:S(2)}, u32[]{:S(2)}) collective-permute-start(f32[8,256]{1,0:T(8,128)S(1)} %collective-permute-done.1.refs_3_), channel_id=1, source_target_pairs={{0,1},{1,0},{2,3},{3,2},{4,5},{5,4},{6,7},{7,6},{8,9},{9,8},{10,11... | collective-permute-start | bytes 24584 | tf_op jit(solution)/shard_map/ppermute | solution.py:657
  9.2 1.2 %collective-permute-start.4 = (f32[8,256]{1,0:T(8,128)S(1)}, f32[8,256]{1,0:T(8,128)S(1)}, u32[]{:S(2)}, u32[]{:S(2)}) collective-permute-start(f32[8,256]{1,0:T(8,128)S(1)} %collective-permute-done.refs_2_), channel_id=1, source_target_pairs={{0,1},{1,0},{2,3},{3,2},{4,5},{5,4},{6,7},{7,6},{8,9},{9,8},{10,11... | collective-permute-start | bytes 24584 | tf_op jit(solution)/shard_map/ppermute | solution.py:657

commit v9 on v8

--- a/solution.py
+++ b/solution.py
@@ -134,6 +134,29 @@
             value = value - lower[c, r] * out[c]
         out[r] = value
     return out
+
+
+def inverse2(first, second, cross):
+    scale = (first * second - cross * cross).inverse()
+    return second * scale, first * scale, -(cross * scale)
+
+
+def solve_blocks(entry, right):
+    cross = [[entry(2 + c, r) for c in range(2)] for r in range(2)]
+    i00, i11, i01 = inverse2(entry(0, 0), entry(1, 1), entry(1, 0))
+    ratio = [
+        [i00 * cross[0][c] + i01 * cross[1][c] for c in range(2)],
+        [i01 * cross[0][c] + i11 * cross[1][c] for c in range(2)],
+    ]
+
+    def rest(r, c):
+        return entry(2 + r, 2 + c) - (cross[0][r] * ratio[0][c] + cross[1][r] * ratio[1][c])
+
+    j00, j11, j01 = inverse2(rest(0, 0), rest(1, 1), rest(1, 0))
+    start = [i00 * right[0] + i01 * right[1], i01 * right[0] + i11 * right[1]]
+    low = [right[2 + r] - (ratio[0][r] * right[0] + ratio[1][r] * right[1]) for r in range(2)]
+    out = [j00 * low[0] + j01 * low[1], j01 * low[0] + j11 * low[1]]
+    return [start[r] - (ratio[r][0] * out[0] + ratio[r][1] * out[1]) for r in range(2)] + out
 
 
 def seeds(lower, pivots):
@@ -197,8 +220,8 @@
 
 def contract(left, right):
     return lax.dot_general(
-        left.astype(jnp.bfloat16),
-        right.astype(jnp.bfloat16),
+        left,
+        right,
         (((0,), (0,)), ((), ())),
         preferred_element_type=jnp.float32,
     )
@@ -209,9 +232,8 @@
     lower4 = sub < 4
     column = sub & 3
 
-    cells = lamination(main[0], main[1])
-    rims = lamination(side[0], side[1])
-    tiles = [cells.map(lambda part: part[:, :LANES]), cells.map(lambda part: part[:, LANES:])]
+    rims = lamination(*side)
+    tiles = [lamination(*cells) for cells in main]
     cycle = (first_cycle + sub - 1).astype(jnp.float32)
     center = 1.0 + (cycle + 0.5) / radial_count
     face = 1.0 + cycle / radial_count
@@ -292,7 +314,7 @@
     for level in range(1, 8):
         step = 1 << (level - 1)
         stay = ((lane + 1) & (2 * step - 1)) == 0
-        reach = solve(*factor(lambda r, c: matrix[r].row(c)), pair)
+        reach = solve_blocks(lambda r, c: matrix[r].row(c), pair)
         next_matrix, next_pair = [], []
         for r in range(4):
             to_left = total(pair[k].row(r) * reach[k] for k in range(4)).lanes(-step)
@@ -338,8 +360,9 @@
         before = [row.lanes(1) for row in odd[group]]
         even[group] = []
         for r in range(4):
-            terms = [reach_e_rows[r][k] * before[k] for k in range(4)]
-            terms += [reach_e_rows[r][4 + k] * odd[group][k] for k in range(4)]
+            terms = [reach_e_rows[r][4 + k] * odd[group][k] for k in range(4)]
+            if r in (0, 3):
+                terms += [reach_e_rows[r][k] * before[k] for k in range(4)]
             even[group].append(total(terms))
 
     def corners(lefts, rights):
@@ -398,86 +421,80 @@
         rows = []
         for group in parts:
             pieces = [getattr(value[which], name) for value in group]
-            rows.append(jnp.concatenate(pieces, axis=1) * sign)
+            row = jnp.concatenate(pieces, axis=1)
+            rows.append(row if sign > 0 else -row)
         return rows
 
-    fill = [jnp.zeros((8, 3 * LANES), jnp.float32)] * 2
-    left = (
-        wide(left_parts, 0, "re")
-        + wide(left_parts, 0, "re")
-        + wide(left_parts, 1, "re")
-        + wide(left_parts, 0, "im")
-        + wide(left_parts, 0, "im")
-        + wide(left_parts, 1, "im")
-        + fill
+    def stacked(parts, order):
+        rows = [row for which, name, sign in order for row in wide(parts, which, name, sign)]
+        rows += [jnp.zeros_like(rows[0])] * (32 - len(rows))
+        return jnp.concatenate(rows, axis=0).astype(jnp.bfloat16)
+
+    hr, hi, lr, li = (0, "re"), (0, "im"), (1, "re"), (1, "im")
+    left = stacked(left_parts, [key + (-1.0,) for key in (hr, hr, lr, hi, hi, li)])
+    signs = (1.0, 1.0, 1.0, -1.0, -1.0, -1.0)
+    right_re = stacked(
+        right_parts, [key + (sign,) for key, sign in zip((hr, lr, hr, hi, li, hi), signs)]
     )
-    fill = [jnp.zeros((8, 5 * LANES), jnp.float32)] * 2
-    right_re = (
-        wide(right_parts, 0, "re")
-        + wide(right_parts, 1, "re")
-        + wide(right_parts, 0, "re")
-        + wide(right_parts, 0, "im", -1.0)
-        + wide(right_parts, 1, "im", -1.0)
-        + wide(right_parts, 0, "im", -1.0)
-        + fill
-    )
-    right_im = (
-        wide(right_parts, 0, "im")
-        + wide(right_parts, 1, "im")
-        + wide(right_parts, 0, "im")
-        + wide(right_parts, 0, "re")
-        + wide(right_parts, 1, "re")
-        + wide(right_parts, 0, "re")
-        + fill
-    )
-    left = jnp.concatenate(left, axis=0)
-    top = Cx(
-        contract(left, jnp.concatenate(right_re, axis=0)),
-        contract(left, jnp.concatenate(right_im, axis=0)),
-    )
-
+    right_im = stacked(right_parts, [key + (1.0,) for key in (hi, li, hi, hr, lr, hr)])
+    top = contract(left, jnp.concatenate([right_re, right_im], axis=1))
+    top = Cx(top[:, : 5 * LANES], top[:, 5 * LANES :])
+
+    wide_lane = lax.broadcasted_iota(jnp.int32, (16, LANES), 1)
+    wide_sub = lax.broadcasted_iota(jnp.int32, (16, LANES), 0)
     masks = []
-    for level in range(1, 7):
-        for tile in range(max((1 << (6 - level)) // 2, 1)):
-            masks.append((level, (lane >> (level + 1)) == 2 * tile + (sub >> 2)))
-
-    def spread(value):
-        out = []
-        for level, mask in masks:
-            out.append(jnp.where(mask, value[level], 0.0))
-        return jnp.concatenate(out, axis=0)
-
-    def both(values, half):
+    for level in range(1, 5):
+        for tile in range(1 << (4 - level)):
+            mask = (wide_lane >> (level + 1)) == 4 * tile + (wide_sub >> 2)
+            masks.append((level, mask))
+    last = ((wide_lane >> 6) == (wide_sub >> 2)) | ((wide_sub >> 2) == 2)
+    masks = [
+        (level, jnp.where(mask, 1.0, 0.0).astype(jnp.bfloat16))
+        for level, mask in masks + [(5, last)]
+    ]
+
+    def spread(values, half):
         levels = {}
         for group in range(1, GROUPS):
-            value = values[group][half]
+            value = values[group]
             if half == 0:
                 value = pick(lane < (2 << level_of(group)), nothing, value)
             turned = value.subs(4)
-            levels[2 * group - 1] = split(pick(lower4, value, turned))
-            levels[2 * group] = split(pick(lower4, turned, value))
-        return {
-            (which, name): spread(
-                {level: getattr(pair[which], name) for level, pair in levels.items()}
-            )
-            for which in range(2)
-            for name in ("re", "im")
-        }
+            levels[2 * group - 1] = pick(lower4, value, turned)
+            levels[2 * group] = pick(lower4, turned, value)
+        out = {}
+        for name in ("re", "im"):
+            parts = {level: getattr(value, name) for level, value in levels.items()}
+            tiles = {level: [parts[level]] * 2 for level in range(1, 5)}
+            tiles[5] = [parts[5], parts[6]]
+            tiles = {level: jnp.concatenate(tile, axis=0) for level, tile in tiles.items()}
+            high = {level: tile.astype(jnp.bfloat16) for level, tile in tiles.items()}
+            low = {
+                level: (tile - high[level].astype(jnp.float32)).astype(jnp.bfloat16)
+                for level, tile in tiles.items()
+            }
+            for which, part in enumerate((high, low)):
+                rows = [part[level] * mask for level, mask in masks]
+                out[which, name] = jnp.concatenate(rows, axis=0)
+        return out
 
     even_d = [inverse_e[0].row(0), inverse_e[0].row(3), inverse_e[3].row(3)]
     even_d = [natural(value, nothing) for value in even_d]
 
     def local(half):
-        low, high = both(inner, half), both(outer, half)
-        own = {key: jnp.where(is_alpha, low[key], high[key]) for key in low}
+        low, high = {}, {}
+        for group in range(1, GROUPS):
+            low[group], high[group] = inner[group][half], outer[group][half]
+        mine = {group: -pick(is_alpha, low[group], high[group]) for group in low}
+        low, high, mine = [spread(values, half) for values in (low, high, mine)]
         every = {key: jnp.concatenate([low[key], high[key]], axis=1) for key in low}
-        hr, hi, lr, li = (0, "re"), (0, "im"), (1, "re"), (1, "im")
-        left = jnp.concatenate([own[key] for key in (hr, hi, hr, hi, lr, li)], axis=0)
+        left = jnp.concatenate([mine[key] for key in (hr, hi, hr, hi, lr, li)], axis=0)
         right_re = jnp.concatenate(
             [every[hr], -every[hi], every[lr], -every[li], every[hr], -every[hi]], axis=0
         )
         right_im = jnp.concatenate([every[key] for key in (hi, hr, li, lr, hi, hr)], axis=0)
-        product = Cx(contract(left, right_re), contract(left, right_im))
+        product = contract(left, jnp.concatenate([right_re, right_im], axis=1))
+        product = Cx(product[:, : 2 * LANES], product[:, 2 * LANES :])
         g_in, g_out = gain_in[half], gain_out[half]
         solo = (lane & 1) == 0
         if half == 0:
@@ -485,8 +502,8 @@
         cross = even_d[1][half] * g_in * g_out
         on_in = pick(is_alpha, even_d[0][half] * g_in * g_in, cross)
         on_out = pick(is_alpha, cross, even_d[2][half] * g_out * g_out)
-        on_in = pick(solo, on_in, 0.0) - pick(is_alpha, g_in, nothing)
-        on_out = pick(solo, on_out, 0.0) - pick(is_alpha, nothing, g_out)
+        on_in = pick(is_alpha, g_in, nothing) - pick(solo, on_in, 0.0)
+        on_out = pick(is_alpha, nothing, g_out) - pick(solo, on_out, 0.0)
         return product, on_in, on_out
 
     edge = pick((lane == sub) & lower4, pick(is_alpha, gain_corner[0], gain_corner[1]), 0.0)
@@ -515,16 +532,16 @@
                 out[half] = out[half] + low
                 out[2 + half] = out[2 + half] + jnp.where(lane < 4, 0.0, high)
                 out[3 + half] = out[3 + half] + jnp.where(lane < 4, high, 0.0)
-                both.append([-value for value in out])
+                both.append(out)
             store(at, 8, both)
     at = 2 * LANES
     both = []
     for part, name in enumerate(("re", "im")):
         edge_part = getattr(edge, name)
         out = [full[part][at : at + 8, t * LANES : (t + 1) * LANES] for t in range(5)]
-        out[2] = out[2] - jnp.where(is_alpha, edge_part, 0.0)
-        out[4] = out[4] - jnp.where(is_alpha, 0.0, lane_roll(edge_part, 4))
-        both.append([-value for value in out])
+        out[2] = out[2] + jnp.where(is_alpha, edge_part, 0.0)
+        out[4] = out[4] + jnp.where(is_alpha, 0.0, lane_roll(edge_part, 4))
+        both.append(out)
     store(at, 4, both)
 
 
@@ -534,28 +551,12 @@
     return jnp.where((sub & 1) == 0, sub_take(first, index), sub_take(second, index))
 
 
-def cell_data(ref, angular):
-    value = ref[...]
-    levels = value[:2].astype(jnp.int32)
-    lookups = []
-    for row in (4, 5):
-        table = jnp.broadcast_to(value[row : row + 1, :LANES], (8, LANES))
-        halves = []
-        for half in range(2):
-            index = levels[:, half * LANES : (half + 1) * LANES]
-            index = jnp.concatenate([index] * 4, axis=0)
-            halves.append(lane_take(table, index)[:2])
-        lookups.append(jnp.concatenate(halves, axis=1))
-    sheet = value[2:4]
-    return angular * lookups[0] * sheet * sheet, lookups[1]
-
-
-def gather_rows(angular, own, other, is_alpha, is_first, is_last, main, side):
+def gather_rows(own, other, is_alpha, is_first, is_last, main, side):
     lane = lax.broadcasted_iota(jnp.int32, (2, LANES), 1)
-    own, other = [[cell_data(ref, angular) for ref in refs] for refs in (own, other)]
     for field in range(2):
+        rows = slice(2 * field, 2 * field + 2)
         (mine, after, near, before), (theirs, after_x, far, before_x) = (
-            [data[field] for data in part] for part in (own, other)
+            [ref[rows, :] for ref in refs] for refs in (own, other)
         )
         alpha, beta = jnp.where(is_alpha, mine, theirs), jnp.where(is_alpha, theirs, mine)
         main[field, 0:1, :] = jnp.where(is_first, alpha[0:1], jnp.where(is_alpha, near, far)[1:2])
@@ -565,8 +566,7 @@
         main[field, 6:8, :] = beta
         ends = []
         for lefts, rights in ((before, after), (before_x, after_x)):
-            left, right = lefts[:, LANES:], rights[:, :LANES]
-            ends.append(jnp.where(lane == LANES - 1, left, jnp.where(lane == 0, right, 1.0)))
+            ends.append(jnp.where(lane == LANES - 1, lefts[:, LANES:], rights[:, :LANES]))
         ends_alpha = jnp.where(is_alpha, ends[0], ends[1])
         ends_beta = jnp.where(is_alpha, ends[1], ends[0])
         side[field, 0:1, :] = ends_alpha[0:1]
@@ -576,16 +576,30 @@
         side[field, 7:8, :] = ends_beta[0:1]
 
 
+def looked_up(tables, angular, material, sheet):
+    index = material.astype(jnp.int32)
+    sigma, base = [lane_take(table, index) for table in tables]
+    return angular * sigma * sheet * sheet, base
+
+
 def merge_kernel(cycles, depth, angular, *refs):
     own, other, (out, main, side, held, sems) = refs[:4], refs[4:8], refs[8:]
     index = lax.axis_index("rad")
     is_alpha = index % 2 == 0
     is_first = index // 2 == 0
     is_last = index // 2 == cycles // 2 - 1
-    gather_rows(angular[0], own, other, is_alpha, is_first, is_last, main, side)
+    gather_rows(own, other, is_alpha, is_first, is_last, main, side)
+    tables = [
+        jnp.broadcast_to(own[0][row : row + 1, :LANES], (8, LANES)) for row in (4, 5)
+    ]
+    parts = [(main, 0), (main, LANES), (side, 0)]
+    parts = [
+        looked_up(tables, angular[0], ref[0, :, at : at + LANES], ref[1, :, at : at + LANES])
+        for ref, at in parts
+    ]
     top, local, edge = strip(
-        (main[0], main[1]),
-        (side[0], side[1]),
+        parts[:2],
+        parts[2],
         is_alpha,
         (index // 2) * (2 * depth),
         cycles * depth,

time: 15.5 us -> 15.5 us (level)
  no operation moved by 1% of the time
where the time goes in v9:
time: 15.5 us; the launch traced here: 15.3 us
  starting transfers between devices  8.06 us (52%)
  Pallas kernels  5.67 us (37%)
  waiting for transfers between devices  0.87 us (6%)
  between operations  0.69 us (4%)
    pallas_call x1, Pallas kernels, per_device(): pl.pallas_call(lambda *refs: merge_kernel(cycles, depth, *refs), out_shap...  4.93 us
    ppermute x1, starting transfers between devices, per_device(): lax.ppermute(cells, 'az', [((i + 1) % blocks, i) for i in range(blocks)])  3.4 us
    ppermute x1, starting transfers between devices, per_device(): lax.ppermute(cells, 'az', [(i, (i + 1) % blocks) for i in range(blocks)])  3.02 us
    ppermute x5, starting transfers between devices, swapped(): return lax.ppermute(cells, axis, route)  1.65 us
    pallas_call x1, Pallas kernels, packed(): pl.pallas_call(pack_kernel, out_shape=jax.ShapeDtypeStruct((8, arguments[...  0.74 us
    ppermute x5, waiting for transfers between devices, swapped(): return lax.ppermute(cells, axis, route)  0.5 us
  transfers between devices with their start and end apart: 7, of which 3 were waited for; matrix products, arithmetic and copies ran while one was open for 0% of the time, Pallas kernels for 0%

profile of v9, /device:TPU:0, one launch (start us, length us, event | category | flops | bytes accessed | tf_op | source)
XLA Modules:
  0.0 15.3 jit_solution(12694160372070251717)
XLA Ops:
  0.0 0.7 %cells.1.refs_1_ = f32[8,256]{1,0:T(8,128)S(1)} custom-call(s32[2,256]{1,0:T(2,128)} %refs_0_.2, f32[2,256]{1,0:T(2,128)} %refs_1_.1, f32[8]{0:T(128)} %refs_2_.1, f32[8]{0:T(128)} %refs_3_.1), custom_call_target="tpu_custom_call" | custom-call | tf_op jit(solution)/shard_map/cells/pallas_call | solution.py:653
  0.8 3.0 %collective-permute-start.2 = (f32[8,256]{1,0:T(8,128)S(1)}, f32[8,256]{1,0:T(8,128)S(1)}, u32[]{:S(2)}, u32[]{:S(2)}) collective-permute-start(f32[8,256]{1,0:T(8,128)S(1)} %cells.1.refs_1_), channel_id=1, source_target_pairs={{0,4},{4,8},{8,12},{12,16},{16,20},{20,24},{24,28},{28,0},{1,5},{5... | collective-permute-start | bytes 24584 | tf_op jit(solution)/shard_map/ppermute | solution.py:679
  3.8 0.7 %collective-permute-start.1 = (f32[8,256]{1,0:T(8,128)S(1)}, f32[8,256]{1,0:T(8,128)S(1)}, u32[]{:S(2)}, u32[]{:S(2)}) collective-permute-start(f32[8,256]{1,0:T(8,128)S(1)} %cells.1.refs_1_), channel_id=1, source_target_pairs={{1,2},{2,1},{3,0},{0,3},{5,6},{6,5},{7,4},{4,7},{9,10},{10,9},{11,... | collective-permute-start | bytes 24584 | tf_op jit(solution)/shard_map/ppermute | solution.py:671
  4.4 3.4 %collective-permute-start = (f32[8,256]{1,0:T(8,128)S(1)}, f32[8,256]{1,0:T(8,128)S(1)}, u32[]{:S(2)}, u32[]{:S(2)}) collective-permute-start(f32[8,256]{1,0:T(8,128)S(1)} %cells.1.refs_1_), channel_id=1, source_target_pairs={{4,0},{8,4},{12,8},{16,12},{20,16},{24,20},{28,24},{0,28},{5,1},{9... | collective-permute-start | bytes 24584 | tf_op jit(solution)/shard_map/ppermute | solution.py:680
  7.8 0.5 %collective-permute-start.3 = (f32[8,256]{1,0:T(8,128)S(1)}, f32[8,256]{1,0:T(8,128)S(1)}, u32[]{:S(2)}, u32[]{:S(2)}) collective-permute-start(f32[8,256]{1,0:T(8,128)S(1)} %cells.1.refs_1_), channel_id=1, source_target_pairs={{0,1},{1,0},{2,3},{3,2},{4,5},{5,4},{6,7},{7,6},{8,9},{9,8},{10,11... | collective-permute-start | bytes 24584 | tf_op jit(solution)/shard_map/ppermute | solution.py:671
  8.3 0.1 collective-permute-done.2.refs_4_
  8.4 0.0 collective-permute-start.6
  8.4 0.0 collective-permute-done.1.refs_3_
  8.4 0.5 %collective-permute-start.5 = (f32[8,256]{1,0:T(8,128)S(1)}, f32[8,256]{1,0:T(8,128)S(1)}, u32[]{:S(2)}, u32[]{:S(2)}) collective-permute-start(f32[8,256]{1,0:T(8,128)S(1)} %collective-permute-done.1.refs_3_), channel_id=1, source_target_pairs={{0,1},{1,0},{2,3},{3,2},{4,5},{5,4},{6,7},{7,6},{8,9},{9,8},{10,11... | collective-permute-start | bytes 24584 | tf_op jit(solution)/shard_map/ppermute | solution.py:671
  9.0 0.2 %collective-permute-done.refs_2_ = f32[8,256]{1,0:T(8,128)S(1)} collective-permute-done((f32[8,256]{1,0:T(8,128)S(1)}, f32[8,256]{1,0:T(8,128)S(1)}, u32[]{:S(2)}, u32[]{:S(2)}) %collective-permute-start) | collective-permute-done | bytes 8224 | tf_op jit(solution)/shard_map/ppermute | solution.py:680
  9.2 0.0 collective-permute-start.4
  9.8 0.0 collective-permute-done.3.refs_5_
  9.9 0.0 collective-permute-done.6.refs_8_
  9.9 0.0 collective-permute-done.5.refs_7_
  9.9 0.5 %collective-permute-done.4.refs_6_ = f32[8,256]{1,0:T(8,128)S(1)} collective-permute-done((f32[8,256]{1,0:T(8,128)S(1)}, f32[8,256]{1,0:T(8,128)S(1)}, u32[]{:S(2)}, u32[]{:S(2)}) %collective-permute-start.4) | collective-permute-done | bytes 8224 | tf_op jit(solution)/shard_map/ppermute | solution.py:671
  10.4 4.9 %pair_map.1 = f32[260,2,520]{2,1,0:T(2,128)} custom-call(f32[1]{0:T(128)S(6)} %copy.6.refs_0_, f32[8,256]{1,0:T(8,128)S(1)} %cells.1.refs_1_, f32[8,256]{1,0:T(8,128)S(1)} %collective-permute-done.refs_2_, f32[8,256]{1,0:T(8,128)S(1)} %collective-permute-done.1.refs_3_, f32[8,256]{1,0:T(8,128)S(1)} %collective-permute-done.2.refs_4_, ...), custom_call_target="tpu_custom_call" | custom-call | tf_op jit(solution)/shard_map/pair_map/pallas_call | solution.py:684
Async XLA Ops:
  0.8 7.7 %collective-permute-start.2 = (f32[8,256]{1,0:T(8,128)S(1)}, f32[8,256]{1,0:T(8,128)S(1)}, u32[]{:S(2)}, u32[]{:S(2)}) collective-permute-start(f32[8,256]{1,0:T(8,128)S(1)} %cells.1.refs_1_), channel_id=1, source_target_pairs={{0,4},{4,8},{8,12},{12,16},{16,20},{20,24},{24,28},{28,0},{1,5},{5... | collective-permute-start | bytes 24584 | tf_op jit(solution)/shard_map/ppermute | solution.py:679
  3.8 4.7 %collective-permute-start.1 = (f32[8,256]{1,0:T(8,128)S(1)}, f32[8,256]{1,0:T(8,128)S(1)}, u32[]{:S(2)}, u32[]{:S(2)}) collective-permute-start(f32[8,256]{1,0:T(8,128)S(1)} %cells.1.refs_1_), channel_id=1, source_target_pairs={{1,2},{2,1},{3,0},{0,3},{5,6},{6,5},{7,4},{4,7},{9,10},{10,9},{11,... | collective-permute-start | bytes 24584 | tf_op jit(solution)/shard_map/ppermute | solution.py:671
  4.4 4.8 %collective-permute-start = (f32[8,256]{1,0:T(8,128)S(1)}, f32[8,256]{1,0:T(8,128)S(1)}, u32[]{:S(2)}, u32[]{:S(2)}) collective-permute-start(f32[8,256]{1,0:T(8,128)S(1)} %cells.1.refs_1_), channel_id=1, source_target_pairs={{4,0},{8,4},{12,8},{16,12},{20,16},{24,20},{28,24},{0,28},{5,1},{9... | collective-permute-start | bytes 24584 | tf_op jit(solution)/shard_map/ppermute | solution.py:680
  7.8 2.0 %collective-permute-start.3 = (f32[8,256]{1,0:T(8,128)S(1)}, f32[8,256]{1,0:T(8,128)S(1)}, u32[]{:S(2)}, u32[]{:S(2)}) collective-permute-start(f32[8,256]{1,0:T(8,128)S(1)} %cells.1.refs_1_), channel_id=1, source_target_pairs={{0,1},{1,0},{2,3},{3,2},{4,5},{5,4},{6,7},{7,6},{8,9},{9,8},{10,11... | collective-permute-start | bytes 24584 | tf_op jit(solution)/shard_map/ppermute | solution.py:671
  8.4 1.4 %collective-permute-start.6 = (f32[8,256]{1,0:T(8,128)S(1)}, f32[8,256]{1,0:T(8,128)S(1)}, u32[]{:S(2)}, u32[]{:S(2)}) collective-permute-start(f32[8,256]{1,0:T(8,128)S(1)} %collective-permute-done.2.refs_4_), channel_id=1, source_target_pairs={{0,1},{1,0},{2,3},{3,2},{4,5},{5,4},{6,7},{7,6},{8,9},{9,8},{10,11... | collective-permute-start | bytes 24584 | tf_op jit(solution)/shard_map/ppermute | solution.py:671
  8.4 1.4 %collective-permute-start.5 = (f32[8,256]{1,0:T(8,128)S(1)}, f32[8,256]{1,0:T(8,128)S(1)}, u32[]{:S(2)}, u32[]{:S(2)}) collective-permute-start(f32[8,256]{1,0:T(8,128)S(1)} %collective-permute-done.1.refs_3_), channel_id=1, source_target_pairs={{0,1},{1,0},{2,3},{3,2},{4,5},{5,4},{6,7},{7,6},{8,9},{9,8},{10,11... | collective-permute-start | bytes 24584 | tf_op jit(solution)/shard_map/ppermute | solution.py:671
  9.2 1.2 %collective-permute-start.4 = (f32[8,256]{1,0:T(8,128)S(1)}, f32[8,256]{1,0:T(8,128)S(1)}, u32[]{:S(2)}, u32[]{:S(2)}) collective-permute-start(f32[8,256]{1,0:T(8,128)S(1)} %collective-permute-done.refs_2_), channel_id=1, source_target_pairs={{0,1},{1,0},{2,3},{3,2},{4,5},{5,4},{6,7},{7,6},{8,9},{9,8},{10,11... | collective-permute-start | bytes 24584 | tf_op jit(solution)/shard_map/ppermute | solution.py:671

commit v10 on v9

--- a/solution.py
+++ b/solution.py
@@ -583,7 +583,7 @@
 
 
 def merge_kernel(cycles, depth, angular, *refs):
-    own, other, (out, main, side, held, sems) = refs[:4], refs[4:8], refs[8:]
+    own, other, (out, main, side, held, rest, sems) = refs[:4], refs[4:8], refs[8:]
     index = lax.axis_index("rad")
     is_alpha = index % 2 == 0
     is_first = index // 2 == 0
@@ -604,31 +604,40 @@
         (index // 2) * (2 * depth),
         cycles * depth,
     )
-    rows = out.shape[0]
+    rows, columns = out.shape[0], out.shape[2]
     bounds = [0, 64, 128, 192, rows]
-    copies = [
-        pltpu.make_async_copy(
-            held.at[first : last, :, :], out.at[first : last, :, :], sems.at[number]
-        )
-        for number, (first, last) in enumerate(zip(bounds, bounds[1:]))
-    ]
+    whole = held.shape[0]
+    copies = []
+    for number, (first, last) in enumerate(zip(bounds, bounds[1:])):
+        part = []
+        for tile in range(whole + 1):
+            if tile < whole:
+                source = held.at[tile].reshape(rows, 2, LANES)
+            else:
+                source = rest
+            at = tile * LANES
+            target = out.at[first:last, :, at : min(at + LANES, columns)]
+            part.append(
+                pltpu.make_async_copy(source.at[first:last, :, :], target, sems.at[number, tile])
+            )
+        copies.append(part)
 
     def store(row, count, both):
-        for number, (real, imag) in enumerate(zip(*both)):
-            at = number * LANES
-            width = min(LANES, out.shape[2] - at)
-            for half in range(count // 4):
-                tile = interleaved(real, imag, half)
-                first = row + 4 * half
-                held[first : first + 4, :, at : at + width] = tile.reshape(4, 2, LANES)[
-                    :, :, :width
-                ]
+        for part, tiles in enumerate(both):
+            for number, tile in enumerate(tiles[:whole]):
+                held[number, pl.ds(2 * row + part, count, stride=2), :] = tile[:count]
+        for half in range(count // 4):
+            tile = interleaved(both[0][whole], both[1][whole], half).reshape(4, 2, LANES)
+            first = row + 4 * half
+            rest[first : first + 4, :, :] = tile[:, :, : rest.shape[2]]
         if row + count in bounds:
-            copies[bounds.index(row + count) - 1].start()
+            for copy in copies[bounds.index(row + count) - 1]:
+                copy.start()
 
     finish(top, local, edge, is_alpha, store)
-    for copy in copies:
-        copy.wait()
+    for part in copies:
+        for copy in part:
+            copy.wait()
 
 
 def pack_kernel(*refs):
@@ -681,6 +690,7 @@
     own = [cells, after, swapped(cells, "rad", 1), before]
     other = [swapped(part, "rad", 0) for part in own]
     outer_nodes = arc + 2 * depth
+    whole, rest = divmod(2 * outer_nodes, LANES)
     out = pl.pallas_call(
         lambda *refs: merge_kernel(cycles, depth, *refs),
         out_shape=jax.ShapeDtypeStruct((outer_nodes, 2, 2 * outer_nodes), jnp.float32),
@@ -690,8 +700,9 @@
         scratch_shapes=[
             pltpu.VMEM((2, 8, arc), jnp.float32),
             pltpu.VMEM((2, 8, LANES), jnp.float32),
-            pltpu.VMEM((outer_nodes, 2, 2 * outer_nodes), jnp.float32),
-            pltpu.SemaphoreType.DMA((4,)),
+            pltpu.VMEM((whole, 2 * outer_nodes, LANES), jnp.float32),
+            pltpu.VMEM((outer_nodes, 2, rest), jnp.float32),
+            pltpu.SemaphoreType.DMA((4, whole + 1)),
         ],
         compiler_params=pltpu.CompilerParams(vmem_limit_bytes=48 * 1024 * 1024),
         name="pair_map",

time: 15.5 us -> 15.5 us (level)
  no operation moved by 1% of the time
where the time goes in v10:
time: 15.5 us; the launch traced here: 15.3 us
  starting transfers between devices  8.06 us (52%)
  Pallas kernels  5.66 us (37%)
  waiting for transfers between devices  0.87 us (6%)
  between operations  0.69 us (4%)
    pallas_call x1, Pallas kernels, per_device(): pl.pallas_call(lambda *refs: merge_kernel(cycles, depth, *refs), out_shap...  4.92 us
    ppermute x1, starting transfers between devices, per_device(): lax.ppermute(cells, 'az', [((i + 1) % blocks, i) for i in range(blocks)])  3.4 us
    ppermute x1, starting transfers between devices, per_device(): lax.ppermute(cells, 'az', [(i, (i + 1) % blocks) for i in range(blocks)])  3.02 us
    ppermute x5, starting transfers between devices, swapped(): return lax.ppermute(cells, axis, route)  1.65 us
    pallas_call x1, Pallas kernels, packed(): pl.pallas_call(pack_kernel, out_shape=jax.ShapeDtypeStruct((8, arguments[...  0.74 us
    ppermute x5, waiting for transfers between devices, swapped(): return lax.ppermute(cells, axis, route)  0.5 us
  transfers between devices with their start and end apart: 7, of which 3 were waited for; matrix products, arithmetic and copies ran while one was open for 0% of the time, Pallas kernels for 0%

profile of v10, /device:TPU:0, one launch (start us, length us, event | category | flops | bytes accessed | tf_op | source)
XLA Modules:
  0.0 15.3 jit_solution(7674395757998752093)
XLA Ops:
  0.0 0.7 %cells.1.refs_1_ = f32[8,256]{1,0:T(8,128)S(1)} custom-call(s32[2,256]{1,0:T(2,128)} %refs_0_.2, f32[2,256]{1,0:T(2,128)} %refs_1_.1, f32[8]{0:T(128)} %refs_2_.1, f32[8]{0:T(128)} %refs_3_.1), custom_call_target="tpu_custom_call" | custom-call | tf_op jit(solution)/shard_map/cells/pallas_call | solution.py:662
  0.8 3.0 %collective-permute-start.2 = (f32[8,256]{1,0:T(8,128)S(1)}, f32[8,256]{1,0:T(8,128)S(1)}, u32[]{:S(2)}, u32[]{:S(2)}) collective-permute-start(f32[8,256]{1,0:T(8,128)S(1)} %cells.1.refs_1_), channel_id=1, source_target_pairs={{0,4},{4,8},{8,12},{12,16},{16,20},{20,24},{24,28},{28,0},{1,5},{5... | collective-permute-start | bytes 24584 | tf_op jit(solution)/shard_map/ppermute | solution.py:688
  3.8 0.7 %collective-permute-start.1 = (f32[8,256]{1,0:T(8,128)S(1)}, f32[8,256]{1,0:T(8,128)S(1)}, u32[]{:S(2)}, u32[]{:S(2)}) collective-permute-start(f32[8,256]{1,0:T(8,128)S(1)} %cells.1.refs_1_), channel_id=1, source_target_pairs={{1,2},{2,1},{3,0},{0,3},{5,6},{6,5},{7,4},{4,7},{9,10},{10,9},{11,... | collective-permute-start | bytes 24584 | tf_op jit(solution)/shard_map/ppermute | solution.py:680
  4.4 3.4 %collective-permute-start = (f32[8,256]{1,0:T(8,128)S(1)}, f32[8,256]{1,0:T(8,128)S(1)}, u32[]{:S(2)}, u32[]{:S(2)}) collective-permute-start(f32[8,256]{1,0:T(8,128)S(1)} %cells.1.refs_1_), channel_id=1, source_target_pairs={{4,0},{8,4},{12,8},{16,12},{20,16},{24,20},{28,24},{0,28},{5,1},{9... | collective-permute-start | bytes 24584 | tf_op jit(solution)/shard_map/ppermute | solution.py:689
  7.8 0.5 %collective-permute-start.3 = (f32[8,256]{1,0:T(8,128)S(1)}, f32[8,256]{1,0:T(8,128)S(1)}, u32[]{:S(2)}, u32[]{:S(2)}) collective-permute-start(f32[8,256]{1,0:T(8,128)S(1)} %cells.1.refs_1_), channel_id=1, source_target_pairs={{0,1},{1,0},{2,3},{3,2},{4,5},{5,4},{6,7},{7,6},{8,9},{9,8},{10,11... | collective-permute-start | bytes 24584 | tf_op jit(solution)/shard_map/ppermute | solution.py:680
  8.3 0.1 collective-permute-done.2.refs_4_
  8.4 0.0 collective-permute-start.6
  8.4 0.0 collective-permute-done.1.refs_3_
  8.4 0.5 %collective-permute-start.5 = (f32[8,256]{1,0:T(8,128)S(1)}, f32[8,256]{1,0:T(8,128)S(1)}, u32[]{:S(2)}, u32[]{:S(2)}) collective-permute-start(f32[8,256]{1,0:T(8,128)S(1)} %collective-permute-done.1.refs_3_), channel_id=1, source_target_pairs={{0,1},{1,0},{2,3},{3,2},{4,5},{5,4},{6,7},{7,6},{8,9},{9,8},{10,11... | collective-permute-start | bytes 24584 | tf_op jit(solution)/shard_map/ppermute | solution.py:680
  9.0 0.2 %collective-permute-done.refs_2_ = f32[8,256]{1,0:T(8,128)S(1)} collective-permute-done((f32[8,256]{1,0:T(8,128)S(1)}, f32[8,256]{1,0:T(8,128)S(1)}, u32[]{:S(2)}, u32[]{:S(2)}) %collective-permute-start) | collective-permute-done | bytes 8224 | tf_op jit(solution)/shard_map/ppermute | solution.py:689
  9.2 0.0 collective-permute-start.4
  9.8 0.0 collective-permute-done.3.refs_5_
  9.9 0.0 collective-permute-done.6.refs_8_
  9.9 0.0 collective-permute-done.5.refs_7_
  9.9 0.5 %collective-permute-done.4.refs_6_ = f32[8,256]{1,0:T(8,128)S(1)} collective-permute-done((f32[8,256]{1,0:T(8,128)S(1)}, f32[8,256]{1,0:T(8,128)S(1)}, u32[]{:S(2)}, u32[]{:S(2)}) %collective-permute-start.4) | collective-permute-done | bytes 8224 | tf_op jit(solution)/shard_map/ppermute | solution.py:680
  10.4 4.9 %pair_map.1 = f32[260,2,520]{2,1,0:T(2,128)} custom-call(f32[1]{0:T(128)S(6)} %copy.6.refs_0_, f32[8,256]{1,0:T(8,128)S(1)} %cells.1.refs_1_, f32[8,256]{1,0:T(8,128)S(1)} %collective-permute-done.refs_2_, f32[8,256]{1,0:T(8,128)S(1)} %collective-permute-done.1.refs_3_, f32[8,256]{1,0:T(8,128)S(1)} %collective-permute-done.2.refs_4_, ...), custom_call_target="tpu_custom_call" | custom-call | tf_op jit(solution)/shard_map/pair_map/pallas_call | solution.py:694
Async XLA Ops:
  0.8 7.7 %collective-permute-start.2 = (f32[8,256]{1,0:T(8,128)S(1)}, f32[8,256]{1,0:T(8,128)S(1)}, u32[]{:S(2)}, u32[]{:S(2)}) collective-permute-start(f32[8,256]{1,0:T(8,128)S(1)} %cells.1.refs_1_), channel_id=1, source_target_pairs={{0,4},{4,8},{8,12},{12,16},{16,20},{20,24},{24,28},{28,0},{1,5},{5... | collective-permute-start | bytes 24584 | tf_op jit(solution)/shard_map/ppermute | solution.py:688
  3.8 4.7 %collective-permute-start.1 = (f32[8,256]{1,0:T(8,128)S(1)}, f32[8,256]{1,0:T(8,128)S(1)}, u32[]{:S(2)}, u32[]{:S(2)}) collective-permute-start(f32[8,256]{1,0:T(8,128)S(1)} %cells.1.refs_1_), channel_id=1, source_target_pairs={{1,2},{2,1},{3,0},{0,3},{5,6},{6,5},{7,4},{4,7},{9,10},{10,9},{11,... | collective-permute-start | bytes 24584 | tf_op jit(solution)/shard_map/ppermute | solution.py:680
  4.4 4.8 %collective-permute-start = (f32[8,256]{1,0:T(8,128)S(1)}, f32[8,256]{1,0:T(8,128)S(1)}, u32[]{:S(2)}, u32[]{:S(2)}) collective-permute-start(f32[8,256]{1,0:T(8,128)S(1)} %cells.1.refs_1_), channel_id=1, source_target_pairs={{4,0},{8,4},{12,8},{16,12},{20,16},{24,20},{28,24},{0,28},{5,1},{9... | collective-permute-start | bytes 24584 | tf_op jit(solution)/shard_map/ppermute | solution.py:689
  7.8 2.0 %collective-permute-start.3 = (f32[8,256]{1,0:T(8,128)S(1)}, f32[8,256]{1,0:T(8,128)S(1)}, u32[]{:S(2)}, u32[]{:S(2)}) collective-permute-start(f32[8,256]{1,0:T(8,128)S(1)} %cells.1.refs_1_), channel_id=1, source_target_pairs={{0,1},{1,0},{2,3},{3,2},{4,5},{5,4},{6,7},{7,6},{8,9},{9,8},{10,11... | collective-permute-start | bytes 24584 | tf_op jit(solution)/shard_map/ppermute | solution.py:680
  8.4 1.4 %collective-permute-start.6 = (f32[8,256]{1,0:T(8,128)S(1)}, f32[8,256]{1,0:T(8,128)S(1)}, u32[]{:S(2)}, u32[]{:S(2)}) collective-permute-start(f32[8,256]{1,0:T(8,128)S(1)} %collective-permute-done.2.refs_4_), channel_id=1, source_target_pairs={{0,1},{1,0},{2,3},{3,2},{4,5},{5,4},{6,7},{7,6},{8,9},{9,8},{10,11... | collective-permute-start | bytes 24584 | tf_op jit(solution)/shard_map/ppermute | solution.py:680
  8.4 1.4 %collective-permute-start.5 = (f32[8,256]{1,0:T(8,128)S(1)}, f32[8,256]{1,0:T(8,128)S(1)}, u32[]{:S(2)}, u32[]{:S(2)}) collective-permute-start(f32[8,256]{1,0:T(8,128)S(1)} %collective-permute-done.1.refs_3_), channel_id=1, source_target_pairs={{0,1},{1,0},{2,3},{3,2},{4,5},{5,4},{6,7},{7,6},{8,9},{9,8},{10,11... | collective-permute-start | bytes 24584 | tf_op jit(solution)/shard_map/ppermute | solution.py:680
  9.2 1.2 %collective-permute-start.4 = (f32[8,256]{1,0:T(8,128)S(1)}, f32[8,256]{1,0:T(8,128)S(1)}, u32[]{:S(2)}, u32[]{:S(2)}) collective-permute-start(f32[8,256]{1,0:T(8,128)S(1)} %collective-permute-done.refs_2_), channel_id=1, source_target_pairs={{0,1},{1,0},{2,3},{3,2},{4,5},{5,4},{6,7},{7,6},{8,9},{9,8},{10,11... | collective-permute-start | bytes 24584 | tf_op jit(solution)/shard_map/ppermute | solution.py:680

commit v11 on v10

--- a/solution.py
+++ b/solution.py
@@ -70,6 +70,18 @@
 
     def subs(self, shift):
         return self.map(lambda part: sub_roll(part, shift))
+
+
+def roll_by(value, shift):
+    return pltpu.roll(value, shift, 1)
+
+
+def flat(values):
+    return tuple(part for value in values for part in (value.re, value.im))
+
+
+def packs(parts):
+    return [Cx(*parts[i : i + 2]) for i in range(0, len(parts), 2)]
 
 
 def pick(mask, first, second):
@@ -311,19 +323,25 @@
             base = pick(column == r - 1, -up_o.row(r), base)
         matrix.append(base - change - change.subs(4))
 
-    for level in range(1, 8):
-        step = 1 << (level - 1)
+    def halve(level, state):
+        matrix, pair = packs(state[:8]), packs(state[8:])
+        step = jnp.left_shift(1, level)
         stay = ((lane + 1) & (2 * step - 1)) == 0
         reach = solve_blocks(lambda r, c: matrix[r].row(c), pair)
         next_matrix, next_pair = [], []
         for r in range(4):
-            to_left = total(pair[k].row(r) * reach[k] for k in range(4)).lanes(-step)
-            to_right = total(pair[k].row(4 + r) * reach[k] for k in range(4)).lanes(step)
+            to_left = total(pair[k].row(r) * reach[k] for k in range(4))
+            to_left = to_left.map(lambda part: roll_by(part, LANES - step))
+            to_right = total(pair[k].row(4 + r) * reach[k] for k in range(4))
+            to_right = to_right.map(lambda part: roll_by(part, step))
             change = pick(lower4, to_left, to_right)
             change = change + change.subs(4)
             next_matrix.append(pick(stay, matrix[r] - change, matrix[r]))
             next_pair.append(pick(stay, pick(lower4, to_right, to_left), pair[r]))
-        matrix, pair = next_matrix, next_pair
+        return flat(next_matrix) + flat(next_pair)
+
+    state = lax.fori_loop(0, 7, halve, flat(matrix) + flat(pair))
+    matrix, pair = packs(state[:8]), packs(state[8:])
 
     lower, pivots = factor(lambda r, c: matrix[r].row(c))
     reach = solve(lower, pivots, pair)

time: 15.5 us -> 15.6 us (level)
  no operation moved by 1% of the time
where the time goes in v11:
time: 15.6 us; the launch traced here: 15.4 us
  starting transfers between devices  8.06 us (52%)
  Pallas kernels  5.8 us (37%)
  waiting for transfers between devices  0.87 us (6%)
  between operations  0.69 us (4%)
    pallas_call x1, Pallas kernels, per_device(): pl.pallas_call(lambda *refs: merge_kernel(cycles, depth, *refs), out_shap...  5.05 us
    ppermute x1, starting transfers between devices, per_device(): lax.ppermute(cells, 'az', [((i + 1) % blocks, i) for i in range(blocks)])  3.4 us
    ppermute x1, starting transfers between devices, per_device(): lax.ppermute(cells, 'az', [(i, (i + 1) % blocks) for i in range(blocks)])  3.02 us
    ppermute x5, starting transfers between devices, swapped(): return lax.ppermute(cells, axis, route)  1.65 us
    pallas_call x1, Pallas kernels, packed(): pl.pallas_call(pack_kernel, out_shape=jax.ShapeDtypeStruct((8, arguments[...  0.74 us
    ppermute x5, waiting for transfers between devices, swapped(): return lax.ppermute(cells, axis, route)  0.5 us
  transfers between devices with their start and end apart: 7, of which 3 were waited for; matrix products, arithmetic and copies ran while one was open for 0% of the time, Pallas kernels for 0%

profile of v11, /device:TPU:0, one launch (start us, length us, event | category | flops | bytes accessed | tf_op | source)
XLA Modules:
  0.0 15.4 jit_solution(7277656267657439444)
XLA Ops:
  0.0 0.7 %cells.1.refs_1_ = f32[8,256]{1,0:T(8,128)S(1)} custom-call(s32[2,256]{1,0:T(2,128)} %refs_0_.2, f32[2,256]{1,0:T(2,128)} %refs_1_.1, f32[8]{0:T(128)} %refs_2_.1, f32[8]{0:T(128)} %refs_3_.1), custom_call_target="tpu_custom_call" | custom-call | tf_op jit(solution)/shard_map/cells/pallas_call | solution.py:680
  0.8 3.0 %collective-permute-start.2 = (f32[8,256]{1,0:T(8,128)S(1)}, f32[8,256]{1,0:T(8,128)S(1)}, u32[]{:S(2)}, u32[]{:S(2)}) collective-permute-start(f32[8,256]{1,0:T(8,128)S(1)} %cells.1.refs_1_), channel_id=1, source_target_pairs={{0,4},{4,8},{8,12},{12,16},{16,20},{20,24},{24,28},{28,0},{1,5},{5... | collective-permute-start | bytes 24584 | tf_op jit(solution)/shard_map/ppermute | solution.py:706
  3.8 0.7 %collective-permute-start.1 = (f32[8,256]{1,0:T(8,128)S(1)}, f32[8,256]{1,0:T(8,128)S(1)}, u32[]{:S(2)}, u32[]{:S(2)}) collective-permute-start(f32[8,256]{1,0:T(8,128)S(1)} %cells.1.refs_1_), channel_id=1, source_target_pairs={{1,2},{2,1},{3,0},{0,3},{5,6},{6,5},{7,4},{4,7},{9,10},{10,9},{11,... | collective-permute-start | bytes 24584 | tf_op jit(solution)/shard_map/ppermute | solution.py:698
  4.4 3.4 %collective-permute-start = (f32[8,256]{1,0:T(8,128)S(1)}, f32[8,256]{1,0:T(8,128)S(1)}, u32[]{:S(2)}, u32[]{:S(2)}) collective-permute-start(f32[8,256]{1,0:T(8,128)S(1)} %cells.1.refs_1_), channel_id=1, source_target_pairs={{4,0},{8,4},{12,8},{16,12},{20,16},{24,20},{28,24},{0,28},{5,1},{9... | collective-permute-start | bytes 24584 | tf_op jit(solution)/shard_map/ppermute | solution.py:707
  7.8 0.5 %collective-permute-start.3 = (f32[8,256]{1,0:T(8,128)S(1)}, f32[8,256]{1,0:T(8,128)S(1)}, u32[]{:S(2)}, u32[]{:S(2)}) collective-permute-start(f32[8,256]{1,0:T(8,128)S(1)} %cells.1.refs_1_), channel_id=1, source_target_pairs={{0,1},{1,0},{2,3},{3,2},{4,5},{5,4},{6,7},{7,6},{8,9},{9,8},{10,11... | collective-permute-start | bytes 24584 | tf_op jit(solution)/shard_map/ppermute | solution.py:698
  8.3 0.1 collective-permute-done.2.refs_4_
  8.4 0.0 collective-permute-start.6
  8.4 0.0 collective-permute-done.1.refs_3_
  8.4 0.5 %collective-permute-start.5 = (f32[8,256]{1,0:T(8,128)S(1)}, f32[8,256]{1,0:T(8,128)S(1)}, u32[]{:S(2)}, u32[]{:S(2)}) collective-permute-start(f32[8,256]{1,0:T(8,128)S(1)} %collective-permute-done.1.refs_3_), channel_id=1, source_target_pairs={{0,1},{1,0},{2,3},{3,2},{4,5},{5,4},{6,7},{7,6},{8,9},{9,8},{10,11... | collective-permute-start | bytes 24584 | tf_op jit(solution)/shard_map/ppermute | solution.py:698
  9.0 0.2 %collective-permute-done.refs_2_ = f32[8,256]{1,0:T(8,128)S(1)} collective-permute-done((f32[8,256]{1,0:T(8,128)S(1)}, f32[8,256]{1,0:T(8,128)S(1)}, u32[]{:S(2)}, u32[]{:S(2)}) %collective-permute-start) | collective-permute-done | bytes 8224 | tf_op jit(solution)/shard_map/ppermute | solution.py:707
  9.2 0.0 collective-permute-start.4
  9.8 0.0 collective-permute-done.3.refs_5_
  9.9 0.0 collective-permute-done.6.refs_8_
  9.9 0.0 collective-permute-done.5.refs_7_
  9.9 0.5 %collective-permute-done.4.refs_6_ = f32[8,256]{1,0:T(8,128)S(1)} collective-permute-done((f32[8,256]{1,0:T(8,128)S(1)}, f32[8,256]{1,0:T(8,128)S(1)}, u32[]{:S(2)}, u32[]{:S(2)}) %collective-permute-start.4) | collective-permute-done | bytes 8224 | tf_op jit(solution)/shard_map/ppermute | solution.py:698
  10.4 5.1 %pair_map.1 = f32[260,2,520]{2,1,0:T(2,128)} custom-call(f32[1]{0:T(128)S(6)} %copy.6.refs_0_, f32[8,256]{1,0:T(8,128)S(1)} %cells.1.refs_1_, f32[8,256]{1,0:T(8,128)S(1)} %collective-permute-done.refs_2_, f32[8,256]{1,0:T(8,128)S(1)} %collective-permute-done.1.refs_3_, f32[8,256]{1,0:T(8,128)S(1)} %collective-permute-done.2.refs_4_, ...), custom_call_target="tpu_custom_call" | custom-call | tf_op jit(solution)/shard_map/pair_map/pallas_call | solution.py:712
Async XLA Ops:
  0.8 7.7 %collective-permute-start.2 = (f32[8,256]{1,0:T(8,128)S(1)}, f32[8,256]{1,0:T(8,128)S(1)}, u32[]{:S(2)}, u32[]{:S(2)}) collective-permute-start(f32[8,256]{1,0:T(8,128)S(1)} %cells.1.refs_1_), channel_id=1, source_target_pairs={{0,4},{4,8},{8,12},{12,16},{16,20},{20,24},{24,28},{28,0},{1,5},{5... | collective-permute-start | bytes 24584 | tf_op jit(solution)/shard_map/ppermute | solution.py:706
  3.8 4.7 %collective-permute-start.1 = (f32[8,256]{1,0:T(8,128)S(1)}, f32[8,256]{1,0:T(8,128)S(1)}, u32[]{:S(2)}, u32[]{:S(2)}) collective-permute-start(f32[8,256]{1,0:T(8,128)S(1)} %cells.1.refs_1_), channel_id=1, source_target_pairs={{1,2},{2,1},{3,0},{0,3},{5,6},{6,5},{7,4},{4,7},{9,10},{10,9},{11,... | collective-permute-start | bytes 24584 | tf_op jit(solution)/shard_map/ppermute | solution.py:698
  4.4 4.8 %collective-permute-start = (f32[8,256]{1,0:T(8,128)S(1)}, f32[8,256]{1,0:T(8,128)S(1)}, u32[]{:S(2)}, u32[]{:S(2)}) collective-permute-start(f32[8,256]{1,0:T(8,128)S(1)} %cells.1.refs_1_), channel_id=1, source_target_pairs={{4,0},{8,4},{12,8},{16,12},{20,16},{24,20},{28,24},{0,28},{5,1},{9... | collective-permute-start | bytes 24584 | tf_op jit(solution)/shard_map/ppermute | solution.py:707
  7.8 2.0 %collective-permute-start.3 = (f32[8,256]{1,0:T(8,128)S(1)}, f32[8,256]{1,0:T(8,128)S(1)}, u32[]{:S(2)}, u32[]{:S(2)}) collective-permute-start(f32[8,256]{1,0:T(8,128)S(1)} %cells.1.refs_1_), channel_id=1, source_target_pairs={{0,1},{1,0},{2,3},{3,2},{4,5},{5,4},{6,7},{7,6},{8,9},{9,8},{10,11... | collective-permute-start | bytes 24584 | tf_op jit(solution)/shard_map/ppermute | solution.py:698
  8.4 1.4 %collective-permute-start.6 = (f32[8,256]{1,0:T(8,128)S(1)}, f32[8,256]{1,0:T(8,128)S(1)}, u32[]{:S(2)}, u32[]{:S(2)}) collective-permute-start(f32[8,256]{1,0:T(8,128)S(1)} %collective-permute-done.2.refs_4_), channel_id=1, source_target_pairs={{0,1},{1,0},{2,3},{3,2},{4,5},{5,4},{6,7},{7,6},{8,9},{9,8},{10,11... | collective-permute-start | bytes 24584 | tf_op jit(solution)/shard_map/ppermute | solution.py:698
  8.4 1.4 %collective-permute-start.5 = (f32[8,256]{1,0:T(8,128)S(1)}, f32[8,256]{1,0:T(8,128)S(1)}, u32[]{:S(2)}, u32[]{:S(2)}) collective-permute-start(f32[8,256]{1,0:T(8,128)S(1)} %collective-permute-done.1.refs_3_), channel_id=1, source_target_pairs={{0,1},{1,0},{2,3},{3,2},{4,5},{5,4},{6,7},{7,6},{8,9},{9,8},{10,11... | collective-permute-start | bytes 24584 | tf_op jit(solution)/shard_map/ppermute | solution.py:698
  9.2 1.2 %collective-permute-start.4 = (f32[8,256]{1,0:T(8,128)S(1)}, f32[8,256]{1,0:T(8,128)S(1)}, u32[]{:S(2)}, u32[]{:S(2)}) collective-permute-start(f32[8,256]{1,0:T(8,128)S(1)} %collective-permute-done.refs_2_), channel_id=1, source_target_pairs={{0,1},{1,0},{2,3},{3,2},{4,5},{5,4},{6,7},{7,6},{8,9},{9,8},{10,11... | collective-permute-start | bytes 24584 | tf_op jit(solution)/shard_map/ppermute | solution.py:698

commit v12 on v10

--- a/solution.py
+++ b/solution.py
@@ -399,6 +399,9 @@
     for group in range(GROUPS + 1):
         if group in (0, GROUPS):
             low, high = inner[group], outer[group]
+            if group == 0:
+                low = [low[0], pick(lower4, nothing, inner[3][1])]
+                high = [high[0], pick(lower4, nothing, outer[3][1])]
         else:
             near = lane < (2 << level_of(group))
             low = [pick(near, inner[group][0], 0.0), nothing]
@@ -443,30 +446,28 @@
     wide_lane = lax.broadcasted_iota(jnp.int32, (16, LANES), 1)
     wide_sub = lax.broadcasted_iota(jnp.int32, (16, LANES), 0)
     masks = []
-    for level in range(1, 5):
-        for tile in range(1 << (4 - level)):
-            mask = (wide_lane >> (level + 1)) == 4 * tile + (wide_sub >> 2)
-            masks.append((level, mask))
-    last = ((wide_lane >> 6) == (wide_sub >> 2)) | ((wide_sub >> 2) == 2)
+    within = wide_lane & 63
+    for level in range(1, 4):
+        for tile in range(1 << (3 - level)):
+            masks.append((level, (within >> (level + 1)) == 4 * tile + (wide_sub >> 2)))
+    last = ((within >> 5) == (wide_sub >> 2)) | ((wide_sub >> 2) == 2)
     masks = [
         (level, jnp.where(mask, 1.0, 0.0).astype(jnp.bfloat16))
-        for level, mask in masks + [(5, last)]
+        for level, mask in masks + [(4, last)]
     ]
 
-    def spread(values, half):
+    def spread(values):
         levels = {}
         for group in range(1, GROUPS):
             value = values[group]
-            if half == 0:
-                value = pick(lane < (2 << level_of(group)), nothing, value)
             turned = value.subs(4)
             levels[2 * group - 1] = pick(lower4, value, turned)
             levels[2 * group] = pick(lower4, turned, value)
         out = {}
         for name in ("re", "im"):
             parts = {level: getattr(value, name) for level, value in levels.items()}
-            tiles = {level: [parts[level]] * 2 for level in range(1, 5)}
-            tiles[5] = [parts[5], parts[6]]
+            tiles = {level: [parts[level]] * 2 for level in range(1, 4)}
+            tiles[4] = [parts[4], parts[5]]
             tiles = {level: jnp.concatenate(tile, axis=0) for level, tile in tiles.items()}
             high = {level: tile.astype(jnp.bfloat16) for level, tile in tiles.items()}
             low = {
@@ -481,20 +482,27 @@
     even_d = [inverse_e[0].row(0), inverse_e[0].row(3), inverse_e[3].row(3)]
     even_d = [natural(value, nothing) for value in even_d]
 
-    def local(half):
-        low, high = {}, {}
+    def local(half, quarter):
+        packed, mine = {}, {}
         for group in range(1, GROUPS):
-            low[group], high[group] = inner[group][half], outer[group][half]
-        mine = {group: -pick(is_alpha, low[group], high[group]) for group in low}
-        low, high, mine = [spread(values, half) for values in (low, high, mine)]
-        every = {key: jnp.concatenate([low[key], high[key]], axis=1) for key in low}
+            low, high = inner[group][half], outer[group][half]
+            if half == 0:
+                near = lane < (2 << level_of(group))
+                low, high = pick(near, nothing, low), pick(near, nothing, high)
+            packed[group] = pick((lane >> 6) == quarter, low, high.lanes(64))
+            turned = packed[group].lanes(64)
+            pair = (packed[group], turned) if quarter == 0 else (turned, packed[group])
+            mine[group] = -pick(is_alpha, *pair)
+        every, mine = spread(packed), spread(mine)
         left = jnp.concatenate([mine[key] for key in (hr, hi, hr, hi, lr, li)], axis=0)
         right_re = jnp.concatenate(
             [every[hr], -every[hi], every[lr], -every[li], every[hr], -every[hi]], axis=0
         )
         right_im = jnp.concatenate([every[key] for key in (hi, hr, li, lr, hi, hr)], axis=0)
-        product = contract(left, jnp.concatenate([right_re, right_im], axis=1))
-        product = Cx(product[:, : 2 * LANES], product[:, 2 * LANES :])
+        product = contract(left[:, :64], jnp.concatenate([right_re, right_im], axis=1))
+        return Cx(product[:, :LANES], product[:, LANES:])
+
+    def diagonals(half):
         g_in, g_out = gain_in[half], gain_out[half]
         solo = (lane & 1) == 0
         if half == 0:
@@ -504,10 +512,10 @@
         on_out = pick(is_alpha, cross, even_d[2][half] * g_out * g_out)
         on_in = pick(is_alpha, g_in, nothing) - pick(solo, on_in, 0.0)
         on_out = pick(is_alpha, nothing, g_out) - pick(solo, on_out, 0.0)
-        return product, on_in, on_out
+        return on_in, on_out.lanes(4)
 
     edge = pick((lane == sub) & lower4, pick(is_alpha, gain_corner[0], gain_corner[1]), 0.0)
-    return top, local, edge
+    return top, (local, diagonals), edge
 
 
 def lower_lanes(lane, count):
@@ -517,21 +525,30 @@
 def finish(top, local, edge, is_alpha, store):
     lane, sub = iota(1), iota(0)
     full = [top.re, top.im]
-    for half in range(2):
-        terms = local(half)
-        for row in range(0, LANES, 8):
-            here = lane == sub + row
-            at = half * LANES + row
+    local, diagonals = local
+    for half, quarter in ((0, 0), (0, 1), (1, 0), (1, 1)):
+        if quarter == 0:
+            on_in, on_out = diagonals(half)
+        product = local(half, quarter)
+        inside = (lane >> 6) == quarter
+        for row in range(0, 64, 8):
+            here = lane == sub + (64 * quarter + row)
+            moved = ((lane - 4) & (LANES - 1)) == sub + (64 * quarter + row)
+            at = half * LANES + quarter * 64 + row
             both = []
             for part, name in enumerate(("re", "im")):
-                product, on_in, on_out = [getattr(value, name) for value in terms]
-                low = product[row : row + 8, :LANES] + jnp.where(here, on_in, 0.0)
-                high = product[row : row + 8, LANES:] + jnp.where(here, on_out, 0.0)
-                high = lane_roll(high, 4)
+                value = getattr(product, name)[row : row + 8]
+                low = jnp.where(inside, value, 0.0)
+                low = low + jnp.where(here, getattr(on_in, name), 0.0)
+                high = lane_roll(jnp.where(inside, 0.0, value), 68)
+                high = high + jnp.where(moved, getattr(on_out, name), 0.0)
                 out = [full[part][at : at + 8, t * LANES : (t + 1) * LANES] for t in range(5)]
                 out[half] = out[half] + low
-                out[2 + half] = out[2 + half] + jnp.where(lane < 4, 0.0, high)
-                out[3 + half] = out[3 + half] + jnp.where(lane < 4, high, 0.0)
+                if quarter == 0:
+                    out[2 + half] = out[2 + half] + high
+                else:
+                    out[2 + half] = out[2 + half] + jnp.where(lane < 4, 0.0, high)
+                    out[3 + half] = out[3 + half] + jnp.where(lane < 4, high, 0.0)
                 both.append(out)
             store(at, 8, both)
     at = 2 * LANES

time: 15.5 us -> 15.5 us (level)
  no operation moved by 1% of the time
where the time goes in v12:
time: 15.5 us; the launch traced here: 15.3 us
  starting transfers between devices  8.06 us (52%)
  Pallas kernels  5.66 us (37%)
  waiting for transfers between devices  0.87 us (6%)
  between operations  0.69 us (4%)
    pallas_call x1, Pallas kernels, per_device(): pl.pallas_call(lambda *refs: merge_kernel(cycles, depth, *refs), out_shap...  4.92 us
    ppermute x1, starting transfers between devices, per_device(): lax.ppermute(cells, 'az', [((i + 1) % blocks, i) for i in range(blocks)])  3.4 us
    ppermute x1, starting transfers between devices, per_device(): lax.ppermute(cells, 'az', [(i, (i + 1) % blocks) for i in range(blocks)])  3.02 us
    ppermute x5, starting transfers between devices, swapped(): return lax.ppermute(cells, axis, route)  1.65 us
    pallas_call x1, Pallas kernels, packed(): pl.pallas_call(pack_kernel, out_shape=jax.ShapeDtypeStruct((8, arguments[...  0.74 us
    ppermute x5, waiting for transfers between devices, swapped(): return lax.ppermute(cells, axis, route)  0.5 us
  transfers between devices with their start and end apart: 7, of which 3 were waited for; matrix products, arithmetic and copies ran while one was open for 0% of the time, Pallas kernels for 0%

profile of v12, /device:TPU:0, one launch (start us, length us, event | category | flops | bytes accessed | tf_op | source)
XLA Modules:
  0.0 15.3 jit_solution(9873862720531809698)
XLA Ops:
  0.0 0.7 %cells.1.refs_1_ = f32[8,256]{1,0:T(8,128)S(1)} custom-call(s32[2,256]{1,0:T(2,128)} %refs_0_.2, f32[2,256]{1,0:T(2,128)} %refs_1_.1, f32[8]{0:T(128)} %refs_2_.1, f32[8]{0:T(128)} %refs_3_.1), custom_call_target="tpu_custom_call" | custom-call | tf_op jit(solution)/shard_map/cells/pallas_call | solution.py:679
  0.8 3.0 %collective-permute-start.2 = (f32[8,256]{1,0:T(8,128)S(1)}, f32[8,256]{1,0:T(8,128)S(1)}, u32[]{:S(2)}, u32[]{:S(2)}) collective-permute-start(f32[8,256]{1,0:T(8,128)S(1)} %cells.1.refs_1_), channel_id=1, source_target_pairs={{0,4},{4,8},{8,12},{12,16},{16,20},{20,24},{24,28},{28,0},{1,5},{5... | collective-permute-start | bytes 24584 | tf_op jit(solution)/shard_map/ppermute | solution.py:705
  3.8 0.7 %collective-permute-start.1 = (f32[8,256]{1,0:T(8,128)S(1)}, f32[8,256]{1,0:T(8,128)S(1)}, u32[]{:S(2)}, u32[]{:S(2)}) collective-permute-start(f32[8,256]{1,0:T(8,128)S(1)} %cells.1.refs_1_), channel_id=1, source_target_pairs={{1,2},{2,1},{3,0},{0,3},{5,6},{6,5},{7,4},{4,7},{9,10},{10,9},{11,... | collective-permute-start | bytes 24584 | tf_op jit(solution)/shard_map/ppermute | solution.py:697
  4.4 3.4 %collective-permute-start = (f32[8,256]{1,0:T(8,128)S(1)}, f32[8,256]{1,0:T(8,128)S(1)}, u32[]{:S(2)}, u32[]{:S(2)}) collective-permute-start(f32[8,256]{1,0:T(8,128)S(1)} %cells.1.refs_1_), channel_id=1, source_target_pairs={{4,0},{8,4},{12,8},{16,12},{20,16},{24,20},{28,24},{0,28},{5,1},{9... | collective-permute-start | bytes 24584 | tf_op jit(solution)/shard_map/ppermute | solution.py:706
  7.8 0.5 %collective-permute-start.3 = (f32[8,256]{1,0:T(8,128)S(1)}, f32[8,256]{1,0:T(8,128)S(1)}, u32[]{:S(2)}, u32[]{:S(2)}) collective-permute-start(f32[8,256]{1,0:T(8,128)S(1)} %cells.1.refs_1_), channel_id=1, source_target_pairs={{0,1},{1,0},{2,3},{3,2},{4,5},{5,4},{6,7},{7,6},{8,9},{9,8},{10,11... | collective-permute-start | bytes 24584 | tf_op jit(solution)/shard_map/ppermute | solution.py:697
  8.3 0.1 collective-permute-done.2.refs_4_
  8.4 0.0 collective-permute-start.6
  8.4 0.0 collective-permute-done.1.refs_3_
  8.4 0.5 %collective-permute-start.5 = (f32[8,256]{1,0:T(8,128)S(1)}, f32[8,256]{1,0:T(8,128)S(1)}, u32[]{:S(2)}, u32[]{:S(2)}) collective-permute-start(f32[8,256]{1,0:T(8,128)S(1)} %collective-permute-done.1.refs_3_), channel_id=1, source_target_pairs={{0,1},{1,0},{2,3},{3,2},{4,5},{5,4},{6,7},{7,6},{8,9},{9,8},{10,11... | collective-permute-start | bytes 24584 | tf_op jit(solution)/shard_map/ppermute | solution.py:697
  9.0 0.2 %collective-permute-done.refs_2_ = f32[8,256]{1,0:T(8,128)S(1)} collective-permute-done((f32[8,256]{1,0:T(8,128)S(1)}, f32[8,256]{1,0:T(8,128)S(1)}, u32[]{:S(2)}, u32[]{:S(2)}) %collective-permute-start) | collective-permute-done | bytes 8224 | tf_op jit(solution)/shard_map/ppermute | solution.py:706
  9.2 0.0 collective-permute-start.4
  9.8 0.0 collective-permute-done.3.refs_5_
  9.9 0.0 collective-permute-done.6.refs_8_
  9.9 0.0 collective-permute-done.5.refs_7_
  9.9 0.5 %collective-permute-done.4.refs_6_ = f32[8,256]{1,0:T(8,128)S(1)} collective-permute-done((f32[8,256]{1,0:T(8,128)S(1)}, f32[8,256]{1,0:T(8,128)S(1)}, u32[]{:S(2)}, u32[]{:S(2)}) %collective-permute-start.4) | collective-permute-done | bytes 8224 | tf_op jit(solution)/shard_map/ppermute | solution.py:697
  10.4 4.9 %pair_map.1 = f32[260,2,520]{2,1,0:T(2,128)} custom-call(f32[1]{0:T(128)S(6)} %copy.6.refs_0_, f32[8,256]{1,0:T(8,128)S(1)} %cells.1.refs_1_, f32[8,256]{1,0:T(8,128)S(1)} %collective-permute-done.refs_2_, f32[8,256]{1,0:T(8,128)S(1)} %collective-permute-done.1.refs_3_, f32[8,256]{1,0:T(8,128)S(1)} %collective-permute-done.2.refs_4_, ...), custom_call_target="tpu_custom_call" | custom-call | tf_op jit(solution)/shard_map/pair_map/pallas_call | solution.py:711
Async XLA Ops:
  0.8 7.7 %collective-permute-start.2 = (f32[8,256]{1,0:T(8,128)S(1)}, f32[8,256]{1,0:T(8,128)S(1)}, u32[]{:S(2)}, u32[]{:S(2)}) collective-permute-start(f32[8,256]{1,0:T(8,128)S(1)} %cells.1.refs_1_), channel_id=1, source_target_pairs={{0,4},{4,8},{8,12},{12,16},{16,20},{20,24},{24,28},{28,0},{1,5},{5... | collective-permute-start | bytes 24584 | tf_op jit(solution)/shard_map/ppermute | solution.py:705
  3.8 4.7 %collective-permute-start.1 = (f32[8,256]{1,0:T(8,128)S(1)}, f32[8,256]{1,0:T(8,128)S(1)}, u32[]{:S(2)}, u32[]{:S(2)}) collective-permute-start(f32[8,256]{1,0:T(8,128)S(1)} %cells.1.refs_1_), channel_id=1, source_target_pairs={{1,2},{2,1},{3,0},{0,3},{5,6},{6,5},{7,4},{4,7},{9,10},{10,9},{11,... | collective-permute-start | bytes 24584 | tf_op jit(solution)/shard_map/ppermute | solution.py:697
  4.4 4.8 %collective-permute-start = (f32[8,256]{1,0:T(8,128)S(1)}, f32[8,256]{1,0:T(8,128)S(1)}, u32[]{:S(2)}, u32[]{:S(2)}) collective-permute-start(f32[8,256]{1,0:T(8,128)S(1)} %cells.1.refs_1_), channel_id=1, source_target_pairs={{4,0},{8,4},{12,8},{16,12},{20,16},{24,20},{28,24},{0,28},{5,1},{9... | collective-permute-start | bytes 24584 | tf_op jit(solution)/shard_map/ppermute | solution.py:706
  7.8 2.0 %collective-permute-start.3 = (f32[8,256]{1,0:T(8,128)S(1)}, f32[8,256]{1,0:T(8,128)S(1)}, u32[]{:S(2)}, u32[]{:S(2)}) collective-permute-start(f32[8,256]{1,0:T(8,128)S(1)} %cells.1.refs_1_), channel_id=1, source_target_pairs={{0,1},{1,0},{2,3},{3,2},{4,5},{5,4},{6,7},{7,6},{8,9},{9,8},{10,11... | collective-permute-start | bytes 24584 | tf_op jit(solution)/shard_map/ppermute | solution.py:697
  8.4 1.4 %collective-permute-start.6 = (f32[8,256]{1,0:T(8,128)S(1)}, f32[8,256]{1,0:T(8,128)S(1)}, u32[]{:S(2)}, u32[]{:S(2)}) collective-permute-start(f32[8,256]{1,0:T(8,128)S(1)} %collective-permute-done.2.refs_4_), channel_id=1, source_target_pairs={{0,1},{1,0},{2,3},{3,2},{4,5},{5,4},{6,7},{7,6},{8,9},{9,8},{10,11... | collective-permute-start | bytes 24584 | tf_op jit(solution)/shard_map/ppermute | solution.py:697
  8.4 1.4 %collective-permute-start.5 = (f32[8,256]{1,0:T(8,128)S(1)}, f32[8,256]{1,0:T(8,128)S(1)}, u32[]{:S(2)}, u32[]{:S(2)}) collective-permute-start(f32[8,256]{1,0:T(8,128)S(1)} %collective-permute-done.1.refs_3_), channel_id=1, source_target_pairs={{0,1},{1,0},{2,3},{3,2},{4,5},{5,4},{6,7},{7,6},{8,9},{9,8},{10,11... | collective-permute-start | bytes 24584 | tf_op jit(solution)/shard_map/ppermute | solution.py:697
  9.2 1.2 %collective-permute-start.4 = (f32[8,256]{1,0:T(8,128)S(1)}, f32[8,256]{1,0:T(8,128)S(1)}, u32[]{:S(2)}, u32[]{:S(2)}) collective-permute-start(f32[8,256]{1,0:T(8,128)S(1)} %collective-permute-done.refs_2_), channel_id=1, source_target_pairs={{0,1},{1,0},{2,3},{3,2},{4,5},{5,4},{6,7},{7,6},{8,9},{9,8},{10,11... | collective-permute-start | bytes 24584 | tf_op jit(solution)/shard_map/ppermute | solution.py:697

commit v13 on v12

--- a/solution.py
+++ b/solution.py
@@ -648,8 +648,8 @@
             first = row + 4 * half
             rest[first : first + 4, :, :] = tile[:, :, : rest.shape[2]]
         if row + count in bounds:
-            for copy in copies[bounds.index(row + count) - 1]:
-                copy.start()
+            for number, copy in enumerate(copies[bounds.index(row + count) - 1]):
+                copy.start(priority=number % 2)
 
     finish(top, local, edge, is_alpha, store)
     for part in copies:

time: 15.5 us -> 15.5 us (level)
  no operation moved by 1% of the time
where the time goes in v13:
time: 15.5 us; the launch traced here: 15.3 us
  starting transfers between devices  8.06 us (52%)
  Pallas kernels  5.66 us (37%)
  waiting for transfers between devices  0.87 us (6%)
  between operations  0.69 us (4%)
    pallas_call x1, Pallas kernels, per_device(): pl.pallas_call(lambda *refs: merge_kernel(cycles, depth, *refs), out_shap...  4.92 us
    ppermute x1, starting transfers between devices, per_device(): lax.ppermute(cells, 'az', [((i + 1) % blocks, i) for i in range(blocks)])  3.4 us
    ppermute x1, starting transfers between devices, per_device(): lax.ppermute(cells, 'az', [(i, (i + 1) % blocks) for i in range(blocks)])  3.02 us
    ppermute x5, starting transfers between devices, swapped(): return lax.ppermute(cells, axis, route)  1.65 us
    pallas_call x1, Pallas kernels, packed(): pl.pallas_call(pack_kernel, out_shape=jax.ShapeDtypeStruct((8, arguments[...  0.74 us
    ppermute x5, waiting for transfers between devices, swapped(): return lax.ppermute(cells, axis, route)  0.5 us
  transfers between devices with their start and end apart: 7, of which 3 were waited for; matrix products, arithmetic and copies ran while one was open for 0% of the time, Pallas kernels for 0%

profile of v13, /device:TPU:0, one launch (start us, length us, event | category | flops | bytes accessed | tf_op | source)
XLA Modules:
  0.0 15.3 jit_solution(7325170230093729067)
XLA Ops:
  0.0 0.7 %cells.1.refs_1_ = f32[8,256]{1,0:T(8,128)S(1)} custom-call(s32[2,256]{1,0:T(2,128)} %refs_0_.2, f32[2,256]{1,0:T(2,128)} %refs_1_.1, f32[8]{0:T(128)} %refs_2_.1, f32[8]{0:T(128)} %refs_3_.1), custom_call_target="tpu_custom_call" | custom-call | tf_op jit(solution)/shard_map/cells/pallas_call | solution.py:679
  0.8 3.0 %collective-permute-start.2 = (f32[8,256]{1,0:T(8,128)S(1)}, f32[8,256]{1,0:T(8,128)S(1)}, u32[]{:S(2)}, u32[]{:S(2)}) collective-permute-start(f32[8,256]{1,0:T(8,128)S(1)} %cells.1.refs_1_), channel_id=1, source_target_pairs={{0,4},{4,8},{8,12},{12,16},{16,20},{20,24},{24,28},{28,0},{1,5},{5... | collective-permute-start | bytes 24584 | tf_op jit(solution)/shard_map/ppermute | solution.py:705
  3.8 0.7 %collective-permute-start.1 = (f32[8,256]{1,0:T(8,128)S(1)}, f32[8,256]{1,0:T(8,128)S(1)}, u32[]{:S(2)}, u32[]{:S(2)}) collective-permute-start(f32[8,256]{1,0:T(8,128)S(1)} %cells.1.refs_1_), channel_id=1, source_target_pairs={{1,2},{2,1},{3,0},{0,3},{5,6},{6,5},{7,4},{4,7},{9,10},{10,9},{11,... | collective-permute-start | bytes 24584 | tf_op jit(solution)/shard_map/ppermute | solution.py:697
  4.4 3.4 %collective-permute-start = (f32[8,256]{1,0:T(8,128)S(1)}, f32[8,256]{1,0:T(8,128)S(1)}, u32[]{:S(2)}, u32[]{:S(2)}) collective-permute-start(f32[8,256]{1,0:T(8,128)S(1)} %cells.1.refs_1_), channel_id=1, source_target_pairs={{4,0},{8,4},{12,8},{16,12},{20,16},{24,20},{28,24},{0,28},{5,1},{9... | collective-permute-start | bytes 24584 | tf_op jit(solution)/shard_map/ppermute | solution.py:706
  7.8 0.5 %collective-permute-start.3 = (f32[8,256]{1,0:T(8,128)S(1)}, f32[8,256]{1,0:T(8,128)S(1)}, u32[]{:S(2)}, u32[]{:S(2)}) collective-permute-start(f32[8,256]{1,0:T(8,128)S(1)} %cells.1.refs_1_), channel_id=1, source_target_pairs={{0,1},{1,0},{2,3},{3,2},{4,5},{5,4},{6,7},{7,6},{8,9},{9,8},{10,11... | collective-permute-start | bytes 24584 | tf_op jit(solution)/shard_map/ppermute | solution.py:697
  8.3 0.1 collective-permute-done.2.refs_4_
  8.4 0.0 collective-permute-start.6
  8.4 0.0 collective-permute-done.1.refs_3_
  8.4 0.5 %collective-permute-start.5 = (f32[8,256]{1,0:T(8,128)S(1)}, f32[8,256]{1,0:T(8,128)S(1)}, u32[]{:S(2)}, u32[]{:S(2)}) collective-permute-start(f32[8,256]{1,0:T(8,128)S(1)} %collective-permute-done.1.refs_3_), channel_id=1, source_target_pairs={{0,1},{1,0},{2,3},{3,2},{4,5},{5,4},{6,7},{7,6},{8,9},{9,8},{10,11... | collective-permute-start | bytes 24584 | tf_op jit(solution)/shard_map/ppermute | solution.py:697
  9.0 0.2 %collective-permute-done.refs_2_ = f32[8,256]{1,0:T(8,128)S(1)} collective-permute-done((f32[8,256]{1,0:T(8,128)S(1)}, f32[8,256]{1,0:T(8,128)S(1)}, u32[]{:S(2)}, u32[]{:S(2)}) %collective-permute-start) | collective-permute-done | bytes 8224 | tf_op jit(solution)/shard_map/ppermute | solution.py:706
  9.2 0.0 collective-permute-start.4
  9.8 0.0 collective-permute-done.3.refs_5_
  9.9 0.0 collective-permute-done.6.refs_8_
  9.9 0.0 collective-permute-done.5.refs_7_
  9.9 0.5 %collective-permute-done.4.refs_6_ = f32[8,256]{1,0:T(8,128)S(1)} collective-permute-done((f32[8,256]{1,0:T(8,128)S(1)}, f32[8,256]{1,0:T(8,128)S(1)}, u32[]{:S(2)}, u32[]{:S(2)}) %collective-permute-start.4) | collective-permute-done | bytes 8224 | tf_op jit(solution)/shard_map/ppermute | solution.py:697
  10.4 4.9 %pair_map.1 = f32[260,2,520]{2,1,0:T(2,128)} custom-call(f32[1]{0:T(128)S(6)} %copy.6.refs_0_, f32[8,256]{1,0:T(8,128)S(1)} %cells.1.refs_1_, f32[8,256]{1,0:T(8,128)S(1)} %collective-permute-done.refs_2_, f32[8,256]{1,0:T(8,128)S(1)} %collective-permute-done.1.refs_3_, f32[8,256]{1,0:T(8,128)S(1)} %collective-permute-done.2.refs_4_, ...), custom_call_target="tpu_custom_call" | custom-call | tf_op jit(solution)/shard_map/pair_map/pallas_call | solution.py:711
Async XLA Ops:
  0.8 7.7 %collective-permute-start.2 = (f32[8,256]{1,0:T(8,128)S(1)}, f32[8,256]{1,0:T(8,128)S(1)}, u32[]{:S(2)}, u32[]{:S(2)}) collective-permute-start(f32[8,256]{1,0:T(8,128)S(1)} %cells.1.refs_1_), channel_id=1, source_target_pairs={{0,4},{4,8},{8,12},{12,16},{16,20},{20,24},{24,28},{28,0},{1,5},{5... | collective-permute-start | bytes 24584 | tf_op jit(solution)/shard_map/ppermute | solution.py:705
  3.8 4.7 %collective-permute-start.1 = (f32[8,256]{1,0:T(8,128)S(1)}, f32[8,256]{1,0:T(8,128)S(1)}, u32[]{:S(2)}, u32[]{:S(2)}) collective-permute-start(f32[8,256]{1,0:T(8,128)S(1)} %cells.1.refs_1_), channel_id=1, source_target_pairs={{1,2},{2,1},{3,0},{0,3},{5,6},{6,5},{7,4},{4,7},{9,10},{10,9},{11,... | collective-permute-start | bytes 24584 | tf_op jit(solution)/shard_map/ppermute | solution.py:697
  4.4 4.8 %collective-permute-start = (f32[8,256]{1,0:T(8,128)S(1)}, f32[8,256]{1,0:T(8,128)S(1)}, u32[]{:S(2)}, u32[]{:S(2)}) collective-permute-start(f32[8,256]{1,0:T(8,128)S(1)} %cells.1.refs_1_), channel_id=1, source_target_pairs={{4,0},{8,4},{12,8},{16,12},{20,16},{24,20},{28,24},{0,28},{5,1},{9... | collective-permute-start | bytes 24584 | tf_op jit(solution)/shard_map/ppermute | solution.py:706
  7.8 2.0 %collective-permute-start.3 = (f32[8,256]{1,0:T(8,128)S(1)}, f32[8,256]{1,0:T(8,128)S(1)}, u32[]{:S(2)}, u32[]{:S(2)}) collective-permute-start(f32[8,256]{1,0:T(8,128)S(1)} %cells.1.refs_1_), channel_id=1, source_target_pairs={{0,1},{1,0},{2,3},{3,2},{4,5},{5,4},{6,7},{7,6},{8,9},{9,8},{10,11... | collective-permute-start | bytes 24584 | tf_op jit(solution)/shard_map/ppermute | solution.py:697
  8.4 1.4 %collective-permute-start.6 = (f32[8,256]{1,0:T(8,128)S(1)}, f32[8,256]{1,0:T(8,128)S(1)}, u32[]{:S(2)}, u32[]{:S(2)}) collective-permute-start(f32[8,256]{1,0:T(8,128)S(1)} %collective-permute-done.2.refs_4_), channel_id=1, source_target_pairs={{0,1},{1,0},{2,3},{3,2},{4,5},{5,4},{6,7},{7,6},{8,9},{9,8},{10,11... | collective-permute-start | bytes 24584 | tf_op jit(solution)/shard_map/ppermute | solution.py:697
  8.4 1.4 %collective-permute-start.5 = (f32[8,256]{1,0:T(8,128)S(1)}, f32[8,256]{1,0:T(8,128)S(1)}, u32[]{:S(2)}, u32[]{:S(2)}) collective-permute-start(f32[8,256]{1,0:T(8,128)S(1)} %collective-permute-done.1.refs_3_), channel_id=1, source_target_pairs={{0,1},{1,0},{2,3},{3,2},{4,5},{5,4},{6,7},{7,6},{8,9},{9,8},{10,11... | collective-permute-start | bytes 24584 | tf_op jit(solution)/shard_map/ppermute | solution.py:697
  9.2 1.2 %collective-permute-start.4 = (f32[8,256]{1,0:T(8,128)S(1)}, f32[8,256]{1,0:T(8,128)S(1)}, u32[]{:S(2)}, u32[]{:S(2)}) collective-permute-start(f32[8,256]{1,0:T(8,128)S(1)} %collective-permute-done.refs_2_), channel_id=1, source_target_pairs={{0,1},{1,0},{2,3},{3,2},{4,5},{5,4},{6,7},{7,6},{8,9},{9,8},{10,11... | collective-permute-start | bytes 24584 | tf_op jit(solution)/shard_map/ppermute | solution.py:697

commit v14 on v8

--- a/solution.py
+++ b/solution.py
@@ -500,6 +500,15 @@
 def finish(top, local, edge, is_alpha, store):
     lane, sub = iota(1), iota(0)
     full = [top.re, top.im]
+    at = 2 * LANES
+    both = []
+    for part, name in enumerate(("re", "im")):
+        edge_part = getattr(edge, name)
+        out = [full[part][at : at + 8, t * LANES : (t + 1) * LANES] for t in range(5)]
+        out[2] = out[2] - jnp.where(is_alpha, edge_part, 0.0)
+        out[4] = out[4] - jnp.where(is_alpha, 0.0, lane_roll(edge_part, 4))
+        both.append([-value for value in out])
+    store(at, 4, both)
     for half in range(2):
         terms = local(half)
         for row in range(0, LANES, 8):
@@ -517,15 +526,6 @@
                 out[3 + half] = out[3 + half] + jnp.where(lane < 4, high, 0.0)
                 both.append([-value for value in out])
             store(at, 8, both)
-    at = 2 * LANES
-    both = []
-    for part, name in enumerate(("re", "im")):
-        edge_part = getattr(edge, name)
-        out = [full[part][at : at + 8, t * LANES : (t + 1) * LANES] for t in range(5)]
-        out[2] = out[2] - jnp.where(is_alpha, edge_part, 0.0)
-        out[4] = out[4] - jnp.where(is_alpha, 0.0, lane_roll(edge_part, 4))
-        both.append([-value for value in out])
-    store(at, 4, both)
 
 
 def interleaved(first, second, half):
@@ -591,7 +591,7 @@
         cycles * depth,
     )
     rows = out.shape[0]
-    bounds = [0, 64, 128, 192, rows]
+    bounds = [*range(0, rows - 2 * depth + 1, 32), rows]
     copies = [
         pltpu.make_async_copy(
             held.at[first : last, :, :], out.at[first : last, :, :], sems.at[number]
@@ -677,7 +677,7 @@
             pltpu.VMEM((2, 8, arc), jnp.float32),
             pltpu.VMEM((2, 8, LANES), jnp.float32),
             pltpu.VMEM((outer_nodes, 2, 2 * outer_nodes), jnp.float32),
-            pltpu.SemaphoreType.DMA((4,)),
+            pltpu.SemaphoreType.DMA((arc // 32 + 1,)),
         ],
         compiler_params=pltpu.CompilerParams(vmem_limit_bytes=48 * 1024 * 1024),
         name="pair_map",

time: 15.5 us -> 15.5 us (level)
  no operation moved by 1% of the time
where the time goes in v14:
time: 15.5 us; the launch traced here: 15.3 us
  starting transfers between devices  8.06 us (52%)
  Pallas kernels  5.72 us (37%)
  waiting for transfers between devices  0.87 us (6%)
  between operations  0.69 us (4%)
    pallas_call x1, Pallas kernels, per_device(): pl.pallas_call(lambda *refs: merge_kernel(cycles, depth, *refs), out_shap...  4.98 us
    ppermute x1, starting transfers between devices, per_device(): lax.ppermute(cells, 'az', [((i + 1) % blocks, i) for i in range(blocks)])  3.4 us
    ppermute x1, starting transfers between devices, per_device(): lax.ppermute(cells, 'az', [(i, (i + 1) % blocks) for i in range(blocks)])  3.02 us
    ppermute x5, starting transfers between devices, swapped(): return lax.ppermute(cells, axis, route)  1.65 us
    pallas_call x1, Pallas kernels, packed(): pl.pallas_call(pack_kernel, out_shape=jax.ShapeDtypeStruct((8, arguments[...  0.74 us
    ppermute x5, waiting for transfers between devices, swapped(): return lax.ppermute(cells, axis, route)  0.5 us
  transfers between devices with their start and end apart: 7, of which 3 were waited for; matrix products, arithmetic and copies ran while one was open for 0% of the time, Pallas kernels for 0%

profile of v14, /device:TPU:0, one launch (start us, length us, event | category | flops | bytes accessed | tf_op | source)
XLA Modules:
  0.0 15.3 jit_solution(97317590994531809)
XLA Ops:
  0.0 0.7 %cells.1.refs_1_ = f32[8,256]{1,0:T(8,128)S(1)} custom-call(s32[2,256]{1,0:T(2,128)} %refs_0_.2, f32[2,256]{1,0:T(2,128)} %refs_1_.1, f32[8]{0:T(128)} %refs_2_.1, f32[8]{0:T(128)} %refs_3_.1), custom_call_target="tpu_custom_call" | custom-call | tf_op jit(solution)/shard_map/cells/pallas_call | solution.py:639
  0.8 3.0 %collective-permute-start.2 = (f32[8,256]{1,0:T(8,128)S(1)}, f32[8,256]{1,0:T(8,128)S(1)}, u32[]{:S(2)}, u32[]{:S(2)}) collective-permute-start(f32[8,256]{1,0:T(8,128)S(1)} %cells.1.refs_1_), channel_id=1, source_target_pairs={{0,4},{4,8},{8,12},{12,16},{16,20},{20,24},{24,28},{28,0},{1,5},{5... | collective-permute-start | bytes 24584 | tf_op jit(solution)/shard_map/ppermute | solution.py:665
  3.8 0.7 %collective-permute-start.1 = (f32[8,256]{1,0:T(8,128)S(1)}, f32[8,256]{1,0:T(8,128)S(1)}, u32[]{:S(2)}, u32[]{:S(2)}) collective-permute-start(f32[8,256]{1,0:T(8,128)S(1)} %cells.1.refs_1_), channel_id=1, source_target_pairs={{1,2},{2,1},{3,0},{0,3},{5,6},{6,5},{7,4},{4,7},{9,10},{10,9},{11,... | collective-permute-start | bytes 24584 | tf_op jit(solution)/shard_map/ppermute | solution.py:657
  4.4 3.4 %collective-permute-start = (f32[8,256]{1,0:T(8,128)S(1)}, f32[8,256]{1,0:T(8,128)S(1)}, u32[]{:S(2)}, u32[]{:S(2)}) collective-permute-start(f32[8,256]{1,0:T(8,128)S(1)} %cells.1.refs_1_), channel_id=1, source_target_pairs={{4,0},{8,4},{12,8},{16,12},{20,16},{24,20},{28,24},{0,28},{5,1},{9... | collective-permute-start | bytes 24584 | tf_op jit(solution)/shard_map/ppermute | solution.py:666
  7.8 0.5 %collective-permute-start.3 = (f32[8,256]{1,0:T(8,128)S(1)}, f32[8,256]{1,0:T(8,128)S(1)}, u32[]{:S(2)}, u32[]{:S(2)}) collective-permute-start(f32[8,256]{1,0:T(8,128)S(1)} %cells.1.refs_1_), channel_id=1, source_target_pairs={{0,1},{1,0},{2,3},{3,2},{4,5},{5,4},{6,7},{7,6},{8,9},{9,8},{10,11... | collective-permute-start | bytes 24584 | tf_op jit(solution)/shard_map/ppermute | solution.py:657
  8.3 0.1 collective-permute-done.2.refs_4_
  8.4 0.0 collective-permute-start.6
  8.4 0.0 collective-permute-done.1.refs_3_
  8.4 0.5 %collective-permute-start.5 = (f32[8,256]{1,0:T(8,128)S(1)}, f32[8,256]{1,0:T(8,128)S(1)}, u32[]{:S(2)}, u32[]{:S(2)}) collective-permute-start(f32[8,256]{1,0:T(8,128)S(1)} %collective-permute-done.1.refs_3_), channel_id=1, source_target_pairs={{0,1},{1,0},{2,3},{3,2},{4,5},{5,4},{6,7},{7,6},{8,9},{9,8},{10,11... | collective-permute-start | bytes 24584 | tf_op jit(solution)/shard_map/ppermute | solution.py:657
  9.0 0.2 %collective-permute-done.refs_2_ = f32[8,256]{1,0:T(8,128)S(1)} collective-permute-done((f32[8,256]{1,0:T(8,128)S(1)}, f32[8,256]{1,0:T(8,128)S(1)}, u32[]{:S(2)}, u32[]{:S(2)}) %collective-permute-start) | collective-permute-done | bytes 8224 | tf_op jit(solution)/shard_map/ppermute | solution.py:666
  9.2 0.0 collective-permute-start.4
  9.8 0.0 collective-permute-done.3.refs_5_
  9.9 0.0 collective-permute-done.6.refs_8_
  9.9 0.0 collective-permute-done.5.refs_7_
  9.9 0.5 %collective-permute-done.4.refs_6_ = f32[8,256]{1,0:T(8,128)S(1)} collective-permute-done((f32[8,256]{1,0:T(8,128)S(1)}, f32[8,256]{1,0:T(8,128)S(1)}, u32[]{:S(2)}, u32[]{:S(2)}) %collective-permute-start.4) | collective-permute-done | bytes 8224 | tf_op jit(solution)/shard_map/ppermute | solution.py:657
  10.4 5.0 %pair_map.1 = f32[260,2,520]{2,1,0:T(2,128)} custom-call(f32[1]{0:T(128)S(6)} %copy.6.refs_0_, f32[8,256]{1,0:T(8,128)S(1)} %cells.1.refs_1_, f32[8,256]{1,0:T(8,128)S(1)} %collective-permute-done.refs_2_, f32[8,256]{1,0:T(8,128)S(1)} %collective-permute-done.1.refs_3_, f32[8,256]{1,0:T(8,128)S(1)} %collective-permute-done.2.refs_4_, ...), custom_call_target="tpu_custom_call" | custom-call | tf_op jit(solution)/shard_map/pair_map/pallas_call | solution.py:670
Async XLA Ops:
  0.8 7.7 %collective-permute-start.2 = (f32[8,256]{1,0:T(8,128)S(1)}, f32[8,256]{1,0:T(8,128)S(1)}, u32[]{:S(2)}, u32[]{:S(2)}) collective-permute-start(f32[8,256]{1,0:T(8,128)S(1)} %cells.1.refs_1_), channel_id=1, source_target_pairs={{0,4},{4,8},{8,12},{12,16},{16,20},{20,24},{24,28},{28,0},{1,5},{5... | collective-permute-start | bytes 24584 | tf_op jit(solution)/shard_map/ppermute | solution.py:665
  3.8 4.7 %collective-permute-start.1 = (f32[8,256]{1,0:T(8,128)S(1)}, f32[8,256]{1,0:T(8,128)S(1)}, u32[]{:S(2)}, u32[]{:S(2)}) collective-permute-start(f32[8,256]{1,0:T(8,128)S(1)} %cells.1.refs_1_), channel_id=1, source_target_pairs={{1,2},{2,1},{3,0},{0,3},{5,6},{6,5},{7,4},{4,7},{9,10},{10,9},{11,... | collective-permute-start | bytes 24584 | tf_op jit(solution)/shard_map/ppermute | solution.py:657
  4.4 4.8 %collective-permute-start = (f32[8,256]{1,0:T(8,128)S(1)}, f32[8,256]{1,0:T(8,128)S(1)}, u32[]{:S(2)}, u32[]{:S(2)}) collective-permute-start(f32[8,256]{1,0:T(8,128)S(1)} %cells.1.refs_1_), channel_id=1, source_target_pairs={{4,0},{8,4},{12,8},{16,12},{20,16},{24,20},{28,24},{0,28},{5,1},{9... | collective-permute-start | bytes 24584 | tf_op jit(solution)/shard_map/ppermute | solution.py:666
  7.8 2.0 %collective-permute-start.3 = (f32[8,256]{1,0:T(8,128)S(1)}, f32[8,256]{1,0:T(8,128)S(1)}, u32[]{:S(2)}, u32[]{:S(2)}) collective-permute-start(f32[8,256]{1,0:T(8,128)S(1)} %cells.1.refs_1_), channel_id=1, source_target_pairs={{0,1},{1,0},{2,3},{3,2},{4,5},{5,4},{6,7},{7,6},{8,9},{9,8},{10,11... | collective-permute-start | bytes 24584 | tf_op jit(solution)/shard_map/ppermute | solution.py:657
  8.4 1.4 %collective-permute-start.6 = (f32[8,256]{1,0:T(8,128)S(1)}, f32[8,256]{1,0:T(8,128)S(1)}, u32[]{:S(2)}, u32[]{:S(2)}) collective-permute-start(f32[8,256]{1,0:T(8,128)S(1)} %collective-permute-done.2.refs_4_), channel_id=1, source_target_pairs={{0,1},{1,0},{2,3},{3,2},{4,5},{5,4},{6,7},{7,6},{8,9},{9,8},{10,11... | collective-permute-start | bytes 24584 | tf_op jit(solution)/shard_map/ppermute | solution.py:657
  8.4 1.4 %collective-permute-start.5 = (f32[8,256]{1,0:T(8,128)S(1)}, f32[8,256]{1,0:T(8,128)S(1)}, u32[]{:S(2)}, u32[]{:S(2)}) collective-permute-start(f32[8,256]{1,0:T(8,128)S(1)} %collective-permute-done.1.refs_3_), channel_id=1, source_target_pairs={{0,1},{1,0},{2,3},{3,2},{4,5},{5,4},{6,7},{7,6},{8,9},{9,8},{10,11... | collective-permute-start | bytes 24584 | tf_op jit(solution)/shard_map/ppermute | solution.py:657
  9.2 1.2 %collective-permute-start.4 = (f32[8,256]{1,0:T(8,128)S(1)}, f32[8,256]{1,0:T(8,128)S(1)}, u32[]{:S(2)}, u32[]{:S(2)}) collective-permute-start(f32[8,256]{1,0:T(8,128)S(1)} %collective-permute-done.refs_2_), channel_id=1, source_target_pairs={{0,1},{1,0},{2,3},{3,2},{4,5},{5,4},{6,7},{7,6},{8,9},{9,8},{10,11... | collective-permute-start | bytes 24584 | tf_op jit(solution)/shard_map/ppermute | solution.py:657

commit v15 on v12

--- a/solution.py
+++ b/solution.py
@@ -51,7 +51,10 @@
         )
 
     def inverse(self):
-        scale = 1.0 / (self.re * self.re + self.im * self.im)
+        size = self.re * self.re + self.im * self.im
+        scale = pl.reciprocal(size, approx=True)
+        for _ in range(2):
+            scale = scale * (2.0 - size * scale)
         return Cx(self.re * scale, -self.im * scale)
 
     def root(self):

time: 15.5 us -> 15.6 us (level)
  no operation moved by 1% of the time
where the time goes in v15:
time: 15.6 us; the launch traced here: 15.4 us
  starting transfers between devices  8.06 us (52%)
  Pallas kernels  5.8 us (37%)
  waiting for transfers between devices  0.87 us (6%)
  between operations  0.69 us (4%)
    pallas_call x1, Pallas kernels, per_device(): pl.pallas_call(lambda *refs: merge_kernel(cycles, depth, *refs), out_shap...  5.05 us
    ppermute x1, starting transfers between devices, per_device(): lax.ppermute(cells, 'az', [((i + 1) % blocks, i) for i in range(blocks)])  3.4 us
    ppermute x1, starting transfers between devices, per_device(): lax.ppermute(cells, 'az', [(i, (i + 1) % blocks) for i in range(blocks)])  3.02 us
    ppermute x5, starting transfers between devices, swapped(): return lax.ppermute(cells, axis, route)  1.65 us
    pallas_call x1, Pallas kernels, packed(): pl.pallas_call(pack_kernel, out_shape=jax.ShapeDtypeStruct((8, arguments[...  0.74 us
    ppermute x5, waiting for transfers between devices, swapped(): return lax.ppermute(cells, axis, route)  0.5 us
  transfers between devices with their start and end apart: 7, of which 3 were waited for; matrix products, arithmetic and copies ran while one was open for 0% of the time, Pallas kernels for 0%

profile of v15, /device:TPU:0, one launch (start us, length us, event | category | flops | bytes accessed | tf_op | source)
XLA Modules:
  0.0 15.4 jit_solution(5162549722353489063)
XLA Ops:
  0.0 0.7 %cells.1.refs_1_ = f32[8,256]{1,0:T(8,128)S(1)} custom-call(s32[2,256]{1,0:T(2,128)} %refs_0_.2, f32[2,256]{1,0:T(2,128)} %refs_1_.1, f32[8]{0:T(128)} %refs_2_.1, f32[8]{0:T(128)} %refs_3_.1), custom_call_target="tpu_custom_call" | custom-call | tf_op jit(solution)/shard_map/cells/pallas_call | solution.py:682
  0.8 3.0 %collective-permute-start.2 = (f32[8,256]{1,0:T(8,128)S(1)}, f32[8,256]{1,0:T(8,128)S(1)}, u32[]{:S(2)}, u32[]{:S(2)}) collective-permute-start(f32[8,256]{1,0:T(8,128)S(1)} %cells.1.refs_1_), channel_id=1, source_target_pairs={{0,4},{4,8},{8,12},{12,16},{16,20},{20,24},{24,28},{28,0},{1,5},{5... | collective-permute-start | bytes 24584 | tf_op jit(solution)/shard_map/ppermute | solution.py:708
  3.8 0.7 %collective-permute-start.1 = (f32[8,256]{1,0:T(8,128)S(1)}, f32[8,256]{1,0:T(8,128)S(1)}, u32[]{:S(2)}, u32[]{:S(2)}) collective-permute-start(f32[8,256]{1,0:T(8,128)S(1)} %cells.1.refs_1_), channel_id=1, source_target_pairs={{1,2},{2,1},{3,0},{0,3},{5,6},{6,5},{7,4},{4,7},{9,10},{10,9},{11,... | collective-permute-start | bytes 24584 | tf_op jit(solution)/shard_map/ppermute | solution.py:700
  4.4 3.4 %collective-permute-start = (f32[8,256]{1,0:T(8,128)S(1)}, f32[8,256]{1,0:T(8,128)S(1)}, u32[]{:S(2)}, u32[]{:S(2)}) collective-permute-start(f32[8,256]{1,0:T(8,128)S(1)} %cells.1.refs_1_), channel_id=1, source_target_pairs={{4,0},{8,4},{12,8},{16,12},{20,16},{24,20},{28,24},{0,28},{5,1},{9... | collective-permute-start | bytes 24584 | tf_op jit(solution)/shard_map/ppermute | solution.py:709
  7.8 0.5 %collective-permute-start.3 = (f32[8,256]{1,0:T(8,128)S(1)}, f32[8,256]{1,0:T(8,128)S(1)}, u32[]{:S(2)}, u32[]{:S(2)}) collective-permute-start(f32[8,256]{1,0:T(8,128)S(1)} %cells.1.refs_1_), channel_id=1, source_target_pairs={{0,1},{1,0},{2,3},{3,2},{4,5},{5,4},{6,7},{7,6},{8,9},{9,8},{10,11... | collective-permute-start | bytes 24584 | tf_op jit(solution)/shard_map/ppermute | solution.py:700
  8.3 0.1 collective-permute-done.2.refs_4_
  8.4 0.0 collective-permute-start.6
  8.4 0.0 collective-permute-done.1.refs_3_
  8.4 0.5 %collective-permute-start.5 = (f32[8,256]{1,0:T(8,128)S(1)}, f32[8,256]{1,0:T(8,128)S(1)}, u32[]{:S(2)}, u32[]{:S(2)}) collective-permute-start(f32[8,256]{1,0:T(8,128)S(1)} %collective-permute-done.1.refs_3_), channel_id=1, source_target_pairs={{0,1},{1,0},{2,3},{3,2},{4,5},{5,4},{6,7},{7,6},{8,9},{9,8},{10,11... | collective-permute-start | bytes 24584 | tf_op jit(solution)/shard_map/ppermute | solution.py:700
  9.0 0.2 %collective-permute-done.refs_2_ = f32[8,256]{1,0:T(8,128)S(1)} collective-permute-done((f32[8,256]{1,0:T(8,128)S(1)}, f32[8,256]{1,0:T(8,128)S(1)}, u32[]{:S(2)}, u32[]{:S(2)}) %collective-permute-start) | collective-permute-done | bytes 8224 | tf_op jit(solution)/shard_map/ppermute | solution.py:709
  9.2 0.0 collective-permute-start.4
  9.8 0.0 collective-permute-done.3.refs_5_
  9.9 0.0 collective-permute-done.6.refs_8_
  9.9 0.0 collective-permute-done.5.refs_7_
  9.9 0.5 %collective-permute-done.4.refs_6_ = f32[8,256]{1,0:T(8,128)S(1)} collective-permute-done((f32[8,256]{1,0:T(8,128)S(1)}, f32[8,256]{1,0:T(8,128)S(1)}, u32[]{:S(2)}, u32[]{:S(2)}) %collective-permute-start.4) | collective-permute-done | bytes 8224 | tf_op jit(solution)/shard_map/ppermute | solution.py:700
  10.4 5.1 %pair_map.1 = f32[260,2,520]{2,1,0:T(2,128)} custom-call(f32[1]{0:T(128)S(6)} %copy.6.refs_0_, f32[8,256]{1,0:T(8,128)S(1)} %cells.1.refs_1_, f32[8,256]{1,0:T(8,128)S(1)} %collective-permute-done.refs_2_, f32[8,256]{1,0:T(8,128)S(1)} %collective-permute-done.1.refs_3_, f32[8,256]{1,0:T(8,128)S(1)} %collective-permute-done.2.refs_4_, ...), custom_call_target="tpu_custom_call" | custom-call | tf_op jit(solution)/shard_map/pair_map/pallas_call | solution.py:714
Async XLA Ops:
  0.8 7.7 %collective-permute-start.2 = (f32[8,256]{1,0:T(8,128)S(1)}, f32[8,256]{1,0:T(8,128)S(1)}, u32[]{:S(2)}, u32[]{:S(2)}) collective-permute-start(f32[8,256]{1,0:T(8,128)S(1)} %cells.1.refs_1_), channel_id=1, source_target_pairs={{0,4},{4,8},{8,12},{12,16},{16,20},{20,24},{24,28},{28,0},{1,5},{5... | collective-permute-start | bytes 24584 | tf_op jit(solution)/shard_map/ppermute | solution.py:708
  3.8 4.7 %collective-permute-start.1 = (f32[8,256]{1,0:T(8,128)S(1)}, f32[8,256]{1,0:T(8,128)S(1)}, u32[]{:S(2)}, u32[]{:S(2)}) collective-permute-start(f32[8,256]{1,0:T(8,128)S(1)} %cells.1.refs_1_), channel_id=1, source_target_pairs={{1,2},{2,1},{3,0},{0,3},{5,6},{6,5},{7,4},{4,7},{9,10},{10,9},{11,... | collective-permute-start | bytes 24584 | tf_op jit(solution)/shard_map/ppermute | solution.py:700
  4.4 4.8 %collective-permute-start = (f32[8,256]{1,0:T(8,128)S(1)}, f32[8,256]{1,0:T(8,128)S(1)}, u32[]{:S(2)}, u32[]{:S(2)}) collective-permute-start(f32[8,256]{1,0:T(8,128)S(1)} %cells.1.refs_1_), channel_id=1, source_target_pairs={{4,0},{8,4},{12,8},{16,12},{20,16},{24,20},{28,24},{0,28},{5,1},{9... | collective-permute-start | bytes 24584 | tf_op jit(solution)/shard_map/ppermute | solution.py:709
  7.8 2.0 %collective-permute-start.3 = (f32[8,256]{1,0:T(8,128)S(1)}, f32[8,256]{1,0:T(8,128)S(1)}, u32[]{:S(2)}, u32[]{:S(2)}) collective-permute-start(f32[8,256]{1,0:T(8,128)S(1)} %cells.1.refs_1_), channel_id=1, source_target_pairs={{0,1},{1,0},{2,3},{3,2},{4,5},{5,4},{6,7},{7,6},{8,9},{9,8},{10,11... | collective-permute-start | bytes 24584 | tf_op jit(solution)/shard_map/ppermute | solution.py:700
  8.4 1.4 %collective-permute-start.6 = (f32[8,256]{1,0:T(8,128)S(1)}, f32[8,256]{1,0:T(8,128)S(1)}, u32[]{:S(2)}, u32[]{:S(2)}) collective-permute-start(f32[8,256]{1,0:T(8,128)S(1)} %collective-permute-done.2.refs_4_), channel_id=1, source_target_pairs={{0,1},{1,0},{2,3},{3,2},{4,5},{5,4},{6,7},{7,6},{8,9},{9,8},{10,11... | collective-permute-start | bytes 24584 | tf_op jit(solution)/shard_map/ppermute | solution.py:700
  8.4 1.4 %collective-permute-start.5 = (f32[8,256]{1,0:T(8,128)S(1)}, f32[8,256]{1,0:T(8,128)S(1)}, u32[]{:S(2)}, u32[]{:S(2)}) collective-permute-start(f32[8,256]{1,0:T(8,128)S(1)} %collective-permute-done.1.refs_3_), channel_id=1, source_target_pairs={{0,1},{1,0},{2,3},{3,2},{4,5},{5,4},{6,7},{7,6},{8,9},{9,8},{10,11... | collective-permute-start | bytes 24584 | tf_op jit(solution)/shard_map/ppermute | solution.py:700
  9.2 1.2 %collective-permute-start.4 = (f32[8,256]{1,0:T(8,128)S(1)}, f32[8,256]{1,0:T(8,128)S(1)}, u32[]{:S(2)}, u32[]{:S(2)}) collective-permute-start(f32[8,256]{1,0:T(8,128)S(1)} %collective-permute-done.refs_2_), channel_id=1, source_target_pairs={{0,1},{1,0},{2,3},{3,2},{4,5},{5,4},{6,7},{7,6},{8,9},{9,8},{10,11... | collective-permute-start | bytes 24584 | tf_op jit(solution)/shard_map/ppermute | solution.py:700
